TPU v7x, 512 devices: a whole 4x8x8 slice. The times are simulated.
512 devices in a mesh: dp: 16 (over y, core), worker: 32 (over x, z).
Axes of the slice: x: 4, y: 8, z: 8, core: 2. Of those that a mesh axis runs over, the one named last changes fastest.
Arguments:
- grad: bfloat16 [48, 32, 512, 512], P('dp', 'worker')
- prev_stats: float32 [32, 2, 512, 512], P('worker', None, 'dp')
- warm_roots: float32 [32, 2, 512, 512], P('worker', None, 'dp')
- owner_items: int32 [32, 2], replicated, may hold values from 0 to 63, as said below
- counts: int32 [64], replicated, may hold values from 1 to 2, as said below
- read_shard: int32 [32], replicated, may hold values from 0 to 31, each once
Outputs:
- roots: float32 [32, 2, 512, 512], P('worker', None, 'dp')
Inputs may be any that keep to these rules, and one draw needn't show every extreme that they name: `owner_items`: each of the 64 statistics stands in exactly one slot; the counts of an owner's two statistics sum to at most 3, and some owner's sum to 3. `counts`: every owner holds one statistic of count 1 and one of count 1 or 2. `read_shard`: each shard reads exactly one block.
All inputs are finite; a program needn't handle non-finite values.
Results may differ from a plain program's by a relative error of at most 0.0003.
Values sent between devices are 32-bit elements; how exact they have to be, the bound alone decides.
No kernel may reach another device: no remote copies, remote signals or barrier semaphores. Data moves between devices by JAX's collectives and lax.ppermute only.
A program may use at most 64 MiB of HBM per device.

v0:
```python
import jax
import jax.numpy as jnp
from jax import lax
from jax.sharding import PartitionSpec as P

HISTORY = 0.5
DAMPING = 0.001
PRECISE = lax.Precision.HIGHEST


def precise_dot(first, second):
    return jnp.dot(first, second, precision=PRECISE, preferred_element_type=jnp.float32)


def refine(statistic, warm_start, iterations):
    block_width = statistic.shape[0]
    frobenius = jnp.sqrt(jnp.sum(statistic * statistic) + 1e-06)
    identity = jnp.eye(block_width, dtype=jnp.float32)
    scaled = statistic / frobenius + DAMPING * identity
    squared = precise_dot(warm_start, warm_start)
    coupled = precise_dot(precise_dot(squared, squared), scaled)
    step_factor = (5.0 * identity - coupled) * 0.25
    estimate = precise_dot(warm_start, step_factor)

    def second_step():
        factor_sq = precise_dot(step_factor, step_factor)
        coupled_next = precise_dot(factor_sq, precise_dot(factor_sq, coupled))
        factor_next = (5.0 * identity - coupled_next) * 0.25
        return precise_dot(estimate, factor_next)

    return lax.cond(iterations >= 2, second_step, lambda: estimate)


def local(grad, prev_stats, warm_roots, owner_items, counts, read_shard):
    gradients = grad[:, 0]
    block_width = gradients.shape[-1]
    dp_count = lax.axis_size("dp")
    share_rows = block_width // dp_count
    dp_pos = lax.axis_index("dp")
    worker_pos = lax.axis_index("worker")
    weight = (1.0 - HISTORY) / (dp_count * gradients.shape[0])
    left_part = jnp.einsum("mik,mjk->ij", gradients, gradients, preferred_element_type=jnp.float32)
    right_part = jnp.einsum("mki,mkj->ij", gradients, gradients, preferred_element_type=jnp.float32)
    summed_all = lax.psum(jnp.concatenate([left_part, right_part], axis=1), "dp")
    own_share = lax.dynamic_slice_in_dim(summed_all, dp_pos * share_rows, share_rows, 0)
    shares = jnp.stack([own_share[:, :block_width], own_share[:, block_width:]])
    stat_rows = HISTORY * prev_stats[0] + weight * shares
    own_items = lax.dynamic_index_in_dim(owner_items, worker_pos, 0, keepdims=False)
    item_block = own_items // 2
    item_kind = own_items % 2
    current = jnp.zeros_like(stat_rows)
    pieces = lax.all_gather(stat_rows[None], "worker", axis=0, tiled=True)
    piece_count = pieces.shape[0]
    picked = []
    for pick_which_slot in range(2):
        offset = item_block[pick_which_slot]
        inside = (offset >= 0) & (offset < piece_count)
        chosen = lax.dynamic_index_in_dim(
            pieces, jnp.clip(offset, 0, piece_count - 1), 0, keepdims=False
        )
        chosen = lax.dynamic_index_in_dim(chosen, item_kind[pick_which_slot], 0, keepdims=False)
        picked.append(jnp.where(inside, chosen, current[pick_which_slot]))
    collected = jnp.stack(picked)
    full_stats, full_warm = (
        lax.all_gather(collected, "dp", axis=1, tiled=True),
        lax.all_gather(warm_roots[0], "dp", axis=1, tiled=True),
    )
    root_list = []
    for which_slot in range(2):
        whole_root = refine(
            full_stats[which_slot], full_warm[which_slot], counts[own_items[which_slot]]
        )
        root_list.append(lax.dynamic_slice_in_dim(whole_root, dp_pos * share_rows, share_rows, 0))
    root_rows = jnp.stack(root_list)
    block_count = read_shard.shape[0]
    reader_block = jnp.sum(
        jnp.where(read_shard == worker_pos, jnp.arange(block_count, dtype=jnp.int32), 0)
    )
    owner_rows = jnp.arange(block_count, dtype=jnp.int32)[:, None]
    slot_columns = jnp.arange(2, dtype=jnp.int32)[None, :]
    owner_of = []
    slot_of = []
    for which_kind in range(2):
        matches = owner_items == 2 * reader_block + which_kind
        owner_of.append(jnp.sum(jnp.where(matches, owner_rows, 0)))
        slot_of.append(jnp.sum(jnp.where(matches, slot_columns, 0)))
    current = jnp.zeros_like(root_rows)
    pieces = lax.all_gather(root_rows[None], "worker", axis=0, tiled=True)
    piece_count = pieces.shape[0]
    placed = []
    for which_kind in range(2):
        offset = owner_of[which_kind]
        inside = (offset >= 0) & (offset < piece_count)
        chosen = lax.dynamic_index_in_dim(
            pieces, jnp.clip(offset, 0, piece_count - 1), 0, keepdims=False
        )
        chosen = lax.dynamic_index_in_dim(chosen, slot_of[which_kind], 0, keepdims=False)
        placed.append(jnp.where(inside, chosen, current[which_kind]))
    result = jnp.stack(placed)
    return result[None]


def solution(mesh):
    return jax.shard_map(
        local,
        mesh=mesh,
        in_specs=(
            P("dp", "worker", None, None),
            P("worker", None, "dp", None),
            P("worker", None, "dp", None),
            P(),
            P(),
            P(),
        ),
        out_specs=P("worker", None, "dp", None),
        check_vma=False,
    )
```

profile of v0, /device:TPU:1, one launch (start us, length us, event | category | flops | bytes accessed | tf_op | source)
XLA Modules:
  0.0 456.9 jit_solution(16120161892422897226)
XLA Ops:
  6.5 0.0 copy-start
  6.5 0.0 all-reduce.2.cloned.1.call-start
  6.5 1.4 copy-done
  7.9 1.0 fusion.6
  9.0 1.0 fusion.9
  10.0 1.5 pad_maximum_fusion
  11.5 0.0 all-reduce.2.cloned.1.call-update
  11.5 0.0 copy-start.9
  11.5 0.0 all-gather.7.cloned.1.call-start
  11.6 125.3 %all-reduce.2.cloned.1.call-done = f32[512,1024]{0,1:T(8,128)} async-done(((f32[512,1024]{0,1:T(8,128)}), f32[512,1024]{0,1:T(8,128)}) %all-reduce.2.cloned.1.call-update) | async-done | bytes 2097168 | tf_op jit(solution)/shard_map/psum | solution.py:44
  136.9 1.2 dynamic-slice_bitcast_fusion.1
  138.1 0.1 copy.19
  138.2 0.1 copy.20
  138.3 0.0 copy-done.7
  138.3 0.7 fusion.31
  139.0 0.0 all-gather.7.cloned.1.call-update
  139.0 0.0 all-gather.11.cloned.1.call-start
  139.1 0.7 all-gather.11.cloned.1.call-update
  139.8 0.0 all-gather.9.cloned.1.call-start
  139.8 0.0 copy-done.8
  139.8 0.2 fusion.39
  140.0 0.7 fusion.43
  148.1 78.0 %all-gather.7.cloned.1.call-done = f32[32,2,32,512]{3,2,1,0:T(8,128)} async-done(((f32[1,2,32,512]{3,2,1,0:T(8,128)}), f32[32,2,32,512]{3,2,1,0:T(8,128)}) %all-gather.7.cloned.1.call-update) | async-done | bytes 4194320 | tf_op jit(solution)/shard_map/all_gather | solution.py:52
  226.1 0.9 select_bitcast_fusion.3
  227.0 0.8 copy.21
  227.8 0.0 all-gather.9.cloned.1.call-update
  227.8 0.4 all-gather.13.cloned.1.call-start
  228.2 0.5 fusion.41
  232.3 0.6 fusion.42
  234.1 0.1 fusion.20
  234.3 36.0 %all-gather.11.cloned.1.call-done = f32[1,2,512,512]{3,2,1,0:T(8,128)} async-done(((f32[1,2,32,512]{3,2,1,0:T(8,128)}), f32[1,2,512,512]{3,2,1,0:T(8,128)}) %all-gather.11.cloned.1.call-update) | async-done | bytes 2097168 | tf_op jit(solution)/shard_map/all_gather | solution.py:66
  270.3 3.5 fusion.21
  273.8 1.8 fusion.22
  275.7 2.9 fusion.49
  278.5 2.8 fusion.50
  281.3 31.8 %all-gather.9.cloned.1.call-done = f32[2,512,512]{2,0,1:T(2,128)} async-done(((f32[2,32,512]{2,0,1:T(2,128)}), f32[2,512,512]{2,0,1:T(2,128)}) %all-gather.9.cloned.1.call-update) | async-done | bytes 2097168 | tf_op jit(solution)/shard_map/all_gather | solution.py:65
  313.1 5.0 %fusion.40 = (f32[1,512,512]{2,0,1:T(1,128)S(1)}, f32[1,512,512]{2,0,1:T(1,128)}) fusion(f32[2,512,512]{2,0,1:T(2,128)} %all-gather.9.cloned.1.call-done), kind=kLoop, calls=%fused_computation.75 | loop fusion | bytes 4194304 | tf_op jit(solution)/shard_map/slice | solution.py:71
  318.1 1.0 copy-done.6
  319.1 0.9 multiply_reduce_fusion.1
  320.7 4.6 %fusion.12 = (f32[512,512]{1,0:T(8,128)}, f32[512,512]{1,0:T(8,128)S(1)}) fusion(f32[512,512]{1,0:T(8,128)} %fusion.49, f32[1,512,512]{2,0,1:T(1,128)} %copy-done.6, f32[]{:T(128)S(6)} %sqrt.6), kind=kOutput, calls=%fused_computation.19 | convolution fusion | flops 1612709888 | bytes 4194308 | tf_op jit(solution)/shard_map/dot_general | solution.py:12
  325.2 14.6 %convolution_bitcast_fusion.3 = f32[512,512]{0,1:T(8,128)} fusion(f32[1,2,512,512]{3,2,1,0:T(8,128)S(1)} %copy-done.2, f32[512,512]{1,0:T(8,128)S(1)} %get-tuple-element.80), kind=kOutput, calls=%fused_computation.16 | convolution fusion | flops 1611661312 | bytes 3145728 | tf_op jit(solution)/shard_map/dot_general | solution.py:12
  339.9 1.1 constant_dynamic-slice_fusion.1
  341.0 0.1 copy.24
  341.1 2.1 multiply_reduce_fusion
  343.9 4.6 %fusion.13 = (f32[512,512]{1,0:T(8,128)}, f32[512,512]{1,0:T(8,128)S(1)}) fusion(f32[512,512]{1,0:T(8,128)} %fusion.50, f32[1,512,512]{2,0,1:T(1,128)} %get-tuple-element.64, f32[]{:T(128)S(6)} %sqrt.7), kind=kOutput, calls=%fused_computation.20 | convolution fusion | flops 1612709888 | bytes 4194308 | tf_op jit(solution)/shard_map/dot_general | solution.py:12
  348.4 0.0 copy-done.3
  348.4 4.5 convolution_bitcast_fusion.2
  352.9 10.1 %conditional.3 = (f32[512,512]{0,1:T(8,128)}) conditional(s32[]{:T(128)} %bitcast.22, f32[512,512]{0,1:T(8,128)} %convolution_bitcast_fusion.2, (f32[512,512]{1,0:T(8,128)S(1)}, f32[512,512]{1,0:T(8,128)}, f32[512,512]{1,0:T(8,128)S(1)}, f32[512,512]{0,1:T(8,128)}) %tuple.18), branch_computations={%region_7.8_spmd, %region_8.9_spmd} | conditional | flops 6443237376 | bytes 18874404 | solution.py:31
  352.9 3.4 fusion.47
  356.3 1.8 fusion.48
  358.2 0.0 copy-start.4
  358.2 1.9 fusion.1
  360.1 0.1 copy.55
  360.1 2.9 convolution_bitcast_fusion.1
  363.0 1.1 constant_dynamic-slice_fusion
  364.1 0.1 copy.27
  364.2 0.7 pad_maximum_fusion.2
  364.8 0.0 all-gather.13.cloned.1.call-update
  364.9 0.0 copy-done.10
  364.9 0.6 fusion.32
  366.1 0.7 select_reduce_fusion.2
  374.4 74.2 %all-gather.13.cloned.1.call-done = f32[64,32,512]{2,1,0:T(8,128)} async-done(((f32[2,32,512]{2,1,0:T(8,128)}), f32[64,32,512]{2,1,0:T(8,128)}) %all-gather.13.cloned.1.call-update) | async-done | bytes 4194320 | tf_op jit(solution)/shard_map/all_gather | solution.py:88
  448.6 0.9 select_bitcast_fusion.1
  449.5 0.7 maximum_bitcast_fusion
  (14 shorter events, 0.0 us)
Async XLA Ops:
  6.5 1.4 copy-start
  6.5 130.3 %all-reduce.2.cloned.1.call-start = ((), (), s32[]{:S(2)}) async-start(), calls=%async_computation | async-start | bytes 4194304 | tf_op jit(solution)/shard_map/psum | solution.py:44
  11.5 126.9 %copy-start.7 = (f32[1,2,32,512]{3,2,1,0:T(8,128)S(1)}, f32[1,2,32,512]{3,2,1,0:T(8,128)}, u32[]{:S(2)}) copy-start(f32[1,2,32,512]{3,2,1,0:T(8,128)} %param.11) | copy-start | bytes 393220
  11.5 128.4 %copy-start.8 = (s32[32,2]{0,1:T(2,128)S(1)}, s32[32,2]{0,1:T(2,128)}, u32[]{:S(2)}) copy-start(s32[32,2]{0,1:T(2,128)} %param.13) | copy-start | bytes 772
  11.5 220.8 %copy-start.9 = (s32[64]{0:T(128)S(1)}, s32[64]{0:T(128)}, u32[]{:S(2)}) copy-start(s32[64]{0:T(128)} %param.14) | copy-start | bytes 772
  11.5 214.6 %all-gather.7.cloned.1.call-start = ((), (), s32[]{:S(2)}) async-start(), calls=%async_computation.1 | async-start | bytes 4325376 | tf_op jit(solution)/shard_map/all_gather | solution.py:52
  139.0 131.2 %all-gather.11.cloned.1.call-start = ((), (), s32[]{:S(2)}) async-start(), calls=%async_computation.3 | async-start | bytes 2228224 | tf_op jit(solution)/shard_map/all_gather | solution.py:66
  139.8 173.3 %all-gather.9.cloned.1.call-start = ((), (), s32[]{:S(2)}) async-start(), calls=%async_computation.2 | async-start | bytes 2228224 | tf_op jit(solution)/shard_map/all_gather | solution.py:65
  227.8 220.8 %all-gather.13.cloned.1.call-start = ((), (), s32[]{:S(2)}) async-start(), calls=%async_computation.4 | async-start | bytes 4325376 | tf_op jit(solution)/shard_map/all_gather | solution.py:88
  270.3 3.5 copy-start.1
  318.1 1.0 copy-start.6
  320.7 4.6 %copy-start.2 = (f32[1,2,512,512]{3,2,1,0:T(8,128)S(1)}, f32[1,2,512,512]{3,2,1,0:T(8,128)}, u32[]{:S(2)}) copy-start(f32[1,2,512,512]{3,2,1,0:T(8,128)} %all-gather.11.cloned.1.call-done) | copy-start | bytes 6291460
  343.9 4.6 %copy-start.3 = (f32[1,2,512,512]{3,2,1,0:T(8,128)S(1)}, f32[1,2,512,512]{3,2,1,0:T(8,128)}, u32[]{:S(2)}) copy-start(f32[1,2,512,512]{3,2,1,0:T(8,128)} %all-gather.11.cloned.1.call-done) | copy-start | bytes 6291460
  352.9 11.9 %copy-start.10 = (s32[32]{0:T(128)S(1)}, s32[32]{0:T(128)}, u32[]{:S(2)}) copy-start(s32[32]{0:T(128)} %param.15) | copy-start | bytes 388
  358.2 1.9 copy-start.4
Sparse Core Ops, SparseCore 0:
  11.6 125.2 all-reduce.1
  140.1 86.0 all-gather.6
  228.3 41.9 all-gather.10
  272.2 40.7 all-gather.8
  365.0 83.5 all-gather.12
where the time goes:
time: 463 us; the launch traced here: 457 us
  waiting for transfers between devices  346 us (75%)
  matrix products  51.3 us (11%)
  between operations  35.2 us (8%)
  local copies, waits for them, and re-layouts  14.1 us (3%)
  other arithmetic  9.75 us (2%)
    psum x1, waiting for transfers between devices, local(): lax.psum(jnp.concatenate([left_part, right_part], axis=1), 'dp')  125 us
    all_gather x1, waiting for transfers between devices, local(): pieces = lax.all_gather(stat_rows[None], 'worker', axis=0, tiled=True)  78 us
    all_gather x1, waiting for transfers between devices, local(): pieces = lax.all_gather(root_rows[None], 'worker', axis=0, tiled=True)  74.2 us
    dot_general x12, matrix products, precise_dot(): jnp.dot(first, second, precision=PRECISE, preferred_element_type=jnp.floa...  49.2 us
    all_gather x1, waiting for transfers between devices, local(): lax.all_gather(warm_roots[0], 'dp', axis=1, tiled=True)  36 us
    all_gather x1, waiting for transfers between devices, local(): lax.all_gather(collected, 'dp', axis=1, tiled=True)  31.8 us
  transfers between devices with their start and end apart: 5, of which 5 were waited for; matrix products, arithmetic and copies ran while one was open for 4% of the time, Pallas kernels for 0%

commit v1 on v0

v1 whole, which is shorter than its diff:
```python
import jax
import jax.numpy as jnp
from jax import lax
from jax.experimental import pallas as pl
from jax.experimental.pallas import tpu as pltpu
from jax.sharding import Mesh, PartitionSpec as P

HISTORY = 0.5
DAMPING = 0.001
WORKER = ("x", "z")
SWAP = [(0, 1), (1, 0)]


def dot(first, second):
    return jnp.dot(
        first, second, precision=lax.Precision.HIGHEST, preferred_element_type=jnp.float32
    )


def to_tiles(rows):
    height, width = rows.shape
    tiles = rows.reshape(height // 8, 8, width // 128, 128).transpose(0, 2, 1, 3)
    return tiles.reshape(-1, 8, 128)


def from_tiles(tiles, height, width):
    split = tiles.reshape(height // 8, width // 128, 8, 128).transpose(0, 2, 1, 3)
    return split.reshape(height, width)


def pick_kernel(block_ref, owner_ref, mine_ref, stat_ref, own_ref, sibling_ref, out_ref):
    for reader in range(out_ref.shape[0]):
        owner = owner_ref[reader]
        out_ref[reader, 0] = stat_ref[block_ref[reader]]
        out_ref[reader, 1] = jnp.where(mine_ref[reader] != 0, own_ref[owner], sibling_ref[owner])


def pick(blocks, owners, mine, stat, own_slot, sibling_slot):
    smem = pl.BlockSpec(memory_space=pltpu.SMEM)
    vmem = pl.BlockSpec(memory_space=pltpu.VMEM)
    return pl.pallas_call(
        pick_kernel,
        out_shape=jax.ShapeDtypeStruct((stat.shape[0], 2) + stat.shape[1:], stat.dtype),
        in_specs=[smem, smem, smem, vmem, vmem, vmem],
        out_specs=vmem,
    )(blocks, owners, mine, stat, own_slot, sibling_slot)


def local(grad, prev_stats, warm_roots, owner_items, counts, read_shard):
    gradients = grad[:, 0]
    width = gradients.shape[-1]
    y_count = lax.axis_size("y")
    y = lax.axis_index("y")
    core = lax.axis_index("core")
    workers = lax.axis_size(WORKER)
    worker = lax.axis_index(WORKER)
    even = core == 0
    share = width // y_count
    half = share // 2
    weight = (1.0 - HISTORY) / (y_count * 2 * gradients.shape[0])

    warm = warm_roots[0]
    warm_sent = jnp.where(even, warm[1], warm[0])
    warm_kept = jnp.where(even, warm[0], warm[1])
    warm_got = lax.ppermute(warm_sent, "core", SWAP)
    own_warm = jnp.where(
        even,
        jnp.concatenate([warm_kept, warm_got], 0),
        jnp.concatenate([warm_got, warm_kept], 0),
    )

    left = jnp.einsum("mik,mjk->ij", gradients, gradients, preferred_element_type=jnp.float32)
    right = jnp.einsum("mki,mkj->ij", gradients, gradients, preferred_element_type=jnp.float32)
    row = (y * 2 + core) * half
    partial_sent = weight * jnp.where(even, right, left)
    partial_kept = weight * jnp.where(even, left, right)
    prev_sent = HISTORY * jnp.where(even, prev_stats[0, 1], prev_stats[0, 0])
    prev_kept = HISTORY * jnp.where(even, prev_stats[0, 0], prev_stats[0, 1])
    partial_got = lax.ppermute(partial_sent, "core", SWAP)
    prev_got = lax.ppermute(prev_sent, "core", SWAP)
    chip_sum = partial_kept + partial_got
    chunks = lax.all_to_all(chip_sum.reshape(y_count, share, width), "y", 0, 0, tiled=True)
    prev_rows = jnp.where(
        even,
        jnp.concatenate([prev_kept, prev_got], 0),
        jnp.concatenate([prev_got, prev_kept], 0),
    )
    stat_rows = prev_rows + jnp.sum(chunks, axis=0)

    ids = jnp.arange(workers, dtype=jnp.int32)
    blocks = jnp.sum(jnp.where(read_shard[None, :] == ids[:, None], ids[None, :], 0), 1)
    items = 2 * blocks + core
    matches = owner_items[None] == items[:, None, None]
    owners = jnp.sum(jnp.where(matches, ids[None, :, None], 0), (1, 2))
    slots = jnp.sum(jnp.where(matches, jnp.arange(2, dtype=jnp.int32), 0), (1, 2))
    mine = (slots == core).astype(jnp.int32)

    spread = jnp.stack([to_tiles(stat_rows), to_tiles(own_warm)], 1)
    spread = lax.all_to_all(spread, WORKER, 0, 0, tiled=True)
    own_slot = spread[:, 1]
    sibling_slot = lax.ppermute(own_slot, "core", SWAP)
    ordered = pick(blocks, owners, mine, spread[:, 0], own_slot, sibling_slot)
    arrived = lax.all_to_all(ordered, WORKER, 0, 0, tiled=True)
    stat_rows = from_tiles(arrived[:, 0], share, width)
    warm_rows = from_tiles(arrived[:, 1], share, width)
    warm_start = lax.all_gather(warm_rows, "y", axis=0, tiled=True)
    statistic = lax.all_gather(stat_rows, "y", axis=0, tiled=True)

    squared = dot(warm_start, warm_start)
    fourth = dot(squared, squared)
    frobenius = jnp.sqrt(jnp.sum(statistic * statistic) + 1e-06)
    identity = jnp.eye(width, dtype=jnp.float32)
    scaled = statistic / frobenius + DAMPING * identity
    coupled = dot(fourth, scaled)
    factor = (5.0 * identity - coupled) * 0.25
    estimate = dot(warm_rows, factor)
    iterations = counts[2 * blocks[worker] + core]

    def second_step():
        factor_sq = dot(factor, factor)
        coupled_next = dot(factor_sq, dot(factor_sq, coupled))
        factor_next = (5.0 * identity - coupled_next) * 0.25
        return dot(estimate, factor_next)

    root_rows = lax.cond(iterations >= 2, second_step, lambda: estimate)
    root_sent = jnp.where(even, root_rows[half:], root_rows[:half])
    root_kept = jnp.where(even, root_rows[:half], root_rows[half:])
    root_got = lax.ppermute(root_sent, "core", SWAP)
    result = jnp.where(
        even, jnp.stack([root_kept, root_got]), jnp.stack([root_got, root_kept])
    )
    return result[None]


def solution(mesh):
    cores = 2
    x_count = 4
    dp_count, worker_count = mesh.devices.shape
    chips = Mesh(
        mesh.devices.reshape(dp_count // cores, cores, x_count, worker_count // x_count),
        ("y", "core", "x", "z"),
    )
    dp = ("y", "core")
    return jax.shard_map(
        local,
        mesh=chips,
        in_specs=(
            P(dp, WORKER, None, None),
            P(WORKER, None, dp, None),
            P(WORKER, None, dp, None),
            P(),
            P(),
            P(),
        ),
        out_specs=P(WORKER, None, dp, None),
        check_vma=False,
    )
```

time: 463 us -> 203 us (0.44); the launches traced: 457 us -> 202 us
  waiting for transfers between devices: 346 us -> 99.4 us
  starting transfers between devices: 0.54 us -> 47.1 us
  matrix products: 51.3 us -> 11.3 us
  between operations: 35.2 us -> 15.6 us
  blocking collectives: 0 us -> 13.9 us
  local copies, waits for them, and re-layouts: 14.1 us -> 5.37 us
    all_gather x4 -> x2, waiting for transfers between devices: 220 us -> 61.6 us  [the longest x1 36.7 us: local(): statistic = lax.all_gather(stat_rows, 'y', axis=0, tiled=True)]
    psum x1 -> x0, waiting for transfers between devices: 125 us -> none  [local(): lax.psum(jnp.concatenate([left_part, right_part], axis=1), 'dp')]
    dot_general x12 -> x4, matrix products: 49.2 us -> 9.28 us  [dot(): jnp.dot(first, second, precision=lax.Precision.HIGHEST, preferred_element...]
    all_to_all x0 -> x2, waiting for transfers between devices: none -> 33.5 us  [the longest x1 24.7 us: local(): lax.all_to_all(chip_sum.reshape(y_count, share, width), 'y', 0, 0, tiled=...]
    ppermute x0 -> x5, starting transfers between devices: none -> 32.3 us  [the longest x1 13.7 us: local(): root_got = lax.ppermute(root_sent, 'core', SWAP)]
    all_to_all x0 -> x2, starting transfers between devices: none -> 14.6 us  [the longest x1 10.9 us: local(): spread = lax.all_to_all(spread, WORKER, 0, 0, tiled=True)]
    all_to_all x0 -> x1, blocking collectives: none -> 13.9 us  [local(): arrived = lax.all_to_all(ordered, WORKER, 0, 0, tiled=True)]
    slice x3 -> x1, local copies, waits for them, and re-layouts: 6.2 us -> 0.7 us  [local(): stat_rows = from_tiles(arrived[:, 0], share, width)]
  transfers between devices with their start and end apart: 5 -> 9, of which waited for: 5 -> 7; matrix products, arithmetic and copies ran while one was open for 4% -> 5% of each run, Pallas kernels for 0% -> 0%
where the time goes in v1:
time: 203 us; the launch traced here: 202 us
  waiting for transfers between devices  99.4 us (49%)
  starting transfers between devices  47.1 us (23%)
  between operations  15.6 us (8%)
  blocking collectives  13.9 us (7%)
  matrix products  11.3 us (6%)
  other arithmetic  7.47 us (4%)
  local copies, waits for them, and re-layouts  5.37 us (3%)
    all_gather x1, waiting for transfers between devices, local(): statistic = lax.all_gather(stat_rows, 'y', axis=0, tiled=True)  36.7 us
    all_gather x1, waiting for transfers between devices, local(): warm_start = lax.all_gather(warm_rows, 'y', axis=0, tiled=True)  24.9 us
    all_to_all x1, waiting for transfers between devices, local(): lax.all_to_all(chip_sum.reshape(y_count, share, width), 'y', 0, 0, tiled=...  24.7 us
    all_to_all x1, blocking collectives, local(): arrived = lax.all_to_all(ordered, WORKER, 0, 0, tiled=True)  13.9 us
    ppermute x1, starting transfers between devices, local(): root_got = lax.ppermute(root_sent, 'core', SWAP)  13.7 us
    all_to_all x1, starting transfers between devices, local(): spread = lax.all_to_all(spread, WORKER, 0, 0, tiled=True)  10.9 us
    dot_general x4, matrix products, dot(): jnp.dot(first, second, precision=lax.Precision.HIGHEST, preferred_element...  9.28 us
    all_to_all x1, waiting for transfers between devices, local(): spread = lax.all_to_all(spread, WORKER, 0, 0, tiled=True)  8.79 us
  transfers between devices with their start and end apart: 9, of which 7 were waited for; matrix products, arithmetic and copies ran while one was open for 5% of the time, Pallas kernels for 0%

profile of v1, /device:TPU:1, one launch (start us, length us, event | category | flops | bytes accessed | tf_op | source)
XLA Modules:
  0.0 202.1 jit_solution(8367828539770960486)
XLA Ops:
  6.5 0.0 copy-start
  6.5 1.4 copy-done
  7.9 1.0 fusion.5
  9.0 1.0 select_multiply_fusion
  10.0 8.8 %collective-permute-start.1 = (f32[512,512]{1,0:T(8,128)S(1)}, f32[512,512]{1,0:T(8,128)S(1)}, u32[]{:S(2)}, u32[]{:S(2)}) collective-permute-start(f32[512,512]{1,0:T(8,128)S(1)} %get-tuple-element.48), channel_id=1, source_target_pairs={{0,32},{32,0},{1,33},{33,1},{2,34},{34,2},{3,35},{35,3},{4,36},{36... | collective-permute-start | bytes 3145736 | tf_op jit(solution)/shard_map/ppermute | solution.py:79
  18.8 2.3 %collective-permute-done.1 = f32[512,512]{1,0:T(8,128)S(1)} collective-permute-done((f32[512,512]{1,0:T(8,128)S(1)}, f32[512,512]{1,0:T(8,128)S(1)}, u32[]{:S(2)}, u32[]{:S(2)}) %collective-permute-start.1) | collective-permute-done | bytes 1048608 | tf_op jit(solution)/shard_map/ppermute | solution.py:79
  21.0 1.4 multiply_add_fusion
  22.4 0.0 copy-start.4
  22.4 0.0 copy-start.5
  22.4 3.7 %all-to-all-start = ((f32[8,64,512]{2,1,0:T(8,128)}), f32[8,64,512]{2,1,0:T(8,128)S(1)}, u32[]{:S(2)}, u32[]{:S(2)}) async-start(f32[8,64,512]{2,1,0:T(8,128)} %bitcast.8), calls=%async_computation | async-start | bytes 2097152 | tf_op jit(solution)/shard_map/all_to_all | solution.py:82
  26.1 0.0 copy-done.4
  26.1 0.0 copy-start.9
  26.1 0.0 copy-start.7
  26.1 2.3 %collective-permute-start.2 = (f32[32,512]{1,0:T(8,128)S(1)}, f32[32,512]{1,0:T(8,128)S(1)}, u32[]{:S(2)}, u32[]{:S(2)}) collective-permute-start(f32[32,512]{1,0:T(8,128)S(1)} %get-tuple-element.47), channel_id=1, source_target_pairs={{0,32},{32,0},{1,33},{33,1},{2,34},{34,2},{3,35},{35,3},{4,36},{36... | collective-permute-start | bytes 196616 | tf_op jit(solution)/shard_map/ppermute | solution.py:65
  28.4 0.0 copy-done.5
  28.5 2.0 %collective-permute-start = (f32[32,512]{1,0:T(8,128)S(1)}, f32[32,512]{1,0:T(8,128)S(1)}, u32[]{:S(2)}, u32[]{:S(2)}) collective-permute-start(f32[32,512]{1,0:T(8,128)S(1)} %get-tuple-element.45), channel_id=1, source_target_pairs={{0,32},{32,0},{1,33},{33,1},{2,34},{34,2},{3,35},{35,3},{4,36},{36... | collective-permute-start | bytes 196616 | tf_op jit(solution)/shard_map/ppermute | solution.py:80
  30.5 0.0 collective-permute-done.2
  30.6 24.7 %all-to-all-done = f32[8,64,512]{2,1,0:T(8,128)S(1)} async-done(((f32[8,64,512]{2,1,0:T(8,128)}), f32[8,64,512]{2,1,0:T(8,128)S(1)}, u32[]{:S(2)}, u32[]{:S(2)}) %all-to-all-start) | async-done | bytes 1048608 | tf_op jit(solution)/shard_map/all_to_all | solution.py:82
  55.3 0.1 reduce_sum.48
  55.4 0.0 collective-permute-done
  55.4 0.7 pad_maximum_fusion
  56.1 0.0 copy-start.10
  56.1 10.9 %all-to-all-start.1 = ((f32[32,2,8,128]{3,2,1,0:T(8,128)}), f32[32,2,8,128]{3,2,1,0:T(8,128)S(1)}, u32[]{:S(2)}, u32[]{:S(2)}) async-start(f32[32,2,8,128]{3,2,1,0:T(8,128)} %pad_maximum_fusion), calls=%async_computation.1 | async-start | bytes 524288 | tf_op jit(solution)/shard_map/all_to_all | solution.py:99
  67.1 0.0 all-gather.3.cloned.1.call-start
  67.1 0.0 copy-done.9
  67.1 0.1 select_reduce_fusion.block_ref
  67.3 0.0 copy-start.8
  67.3 0.0 copy-done.7
  67.3 0.7 fusion.21
  68.0 8.8 %all-to-all-done.1 = f32[32,2,8,128]{3,2,1,0:T(8,128)S(1)} async-done(((f32[32,2,8,128]{3,2,1,0:T(8,128)}), f32[32,2,8,128]{3,2,1,0:T(8,128)S(1)}, u32[]{:S(2)}, u32[]{:S(2)}) %all-to-all-start.1) | async-done | bytes 262176 | tf_op jit(solution)/shard_map/all_to_all | solution.py:99
  76.8 0.7 slice_bitcast_fusion
  77.4 0.0 copy-start.3
  77.4 5.5 %collective-permute-start.3 = (f32[32,8,128]{2,1,0:T(8,128)S(1)}, f32[32,8,128]{2,1,0:T(8,128)S(1)}, u32[]{:S(2)}, u32[]{:S(2)}) collective-permute-start(f32[32,8,128]{2,1,0:T(8,128)S(1)} %get-tuple-element.40.own_ref), channel_id=1, source_target_pairs={{0,32},{32,0},{1,33},{33,1},{2,34},{34,2},{3,35},{35,3},{4,36},{36... | collective-permute-start | bytes 393224 | tf_op jit(solution)/shard_map/ppermute | solution.py:101
  83.0 0.6 compare_convert_fusion.mine_ref
  83.6 0.4 collective-permute-done.3.sibling_ref
  83.9 0.0 copy-start.6
  84.0 0.0 copy-done.8
  84.0 0.0 copy-done.3
  84.0 0.6 copy-done.6
  84.6 1.8 shard_map.64
  86.4 13.9 %all_to_all.15 = f32[32,2,8,128]{3,2,1,0:T(8,128)S(1)} all-to-all(f32[32,2,8,128]{3,2,1,0:T(8,128)} %shard_map.64), channel_id=1, replica_groups=mesh['y'=8,'core'=2,'x'=4,'z'=8] {'x','z'}, dimensions={0} | all-to-all | bytes 524288 | tf_op jit(solution)/shard_map/all_to_all | solution.py:103
  100.3 0.7 fusion.25
  101.0 0.0 all-gather.3.cloned.1.call-update
  101.0 0.0 all-gather.5.cloned.1.call-start
  101.1 0.7 all-gather.5.cloned.1.call-update
  101.8 1.3 dynamic_slice.6
  103.7 0.0 copy-done.10
  103.7 0.7 dynamic_slice.7
  105.0 1.1 fusion.15
  106.1 24.9 %all-gather.3.cloned.1.call-done = f32[512,512]{1,0:T(8,128)} async-done(((f32[64,512]{1,0:T(8,128)}), f32[512,512]{1,0:T(8,128)}) %all-gather.3.cloned.1.call-update) | async-done | bytes 1048592 | tf_op jit(solution)/shard_map/all_gather | solution.py:106
  131.0 3.4 %fusion.28 = f32[512,512]{1,0:T(8,128)S(1)} fusion(f32[512,512]{1,0:T(8,128)} %all-gather.3.cloned.1.call-done), kind=kOutput, calls=%fused_computation.49 | convolution fusion | flops 1610612736 | bytes 2097152 | tf_op jit(solution)/shard_map/dot_general | solution.py:15
  134.4 1.8 fusion.29
  136.2 36.7 %all-gather.5.cloned.1.call-done = f32[512,512]{1,0:T(8,128)} async-done(((f32[64,512]{1,0:T(8,128)}), f32[512,512]{1,0:T(8,128)}) %all-gather.5.cloned.1.call-update) | async-done | bytes 1048592 | tf_op jit(solution)/shard_map/all_gather | solution.py:107
  172.9 2.1 %multiply_reduce_fusion = f32[]{:T(128)} fusion(f32[512,512]{1,0:T(8,128)} %all-gather.5.cloned.1.call-done), kind=kLoop, calls=%fused_computation.14 | loop fusion | flops 524287 | bytes 1048580 | tf_op jit(solution)/shard_map/reduce_sum | solution.py:111
  175.7 0.0 copy-start.2
  175.7 0.0 copy-start.1
  175.7 3.2 %subtract_multiply_fusion = (f32[512,512]{1,0:T(8,128)S(1)}, f32[512,512]{1,0:T(8,128)S(1)}) fusion(f32[512,512]{1,0:T(8,128)S(1)} %fusion.29, f32[512,512]{1,0:T(8,128)} %all-gather.5.cloned.1.call-done, f32[]{:T(128)S(6)} %sqrt.3), kind=kOutput, calls=%fused_computation.9 | convolution fusion | flops 1612709888 | bytes 4194308 | tf_op jit(solution)/shard_map/dot_general | solution.py:15
  179.0 0.0 copy-done.2
  179.0 0.8 fusion.24
  179.8 0.0 copy-done.1
  179.8 0.2 conditional.1
  180.0 13.7 %collective-permute-start.4 = (f32[32,512]{1,0:T(8,128)S(1)}, f32[32,512]{1,0:T(8,128)S(1)}, u32[]{:S(2)}, u32[]{:S(2)}) collective-permute-start(f32[32,512]{1,0:T(8,128)S(1)} %get-tuple-element.43), channel_id=1, source_target_pairs={{0,32},{32,0},{1,33},{33,1},{2,34},{34,2},{3,35},{35,3},{4,36},{36... | collective-permute-start | bytes 196616 | tf_op jit(solution)/shard_map/ppermute | solution.py:128
  193.8 0.9 collective-permute-done.4
  194.6 0.7 maximum_select_fusion.2
  (6 shorter events, 0.1 us)
Async XLA Ops:
  6.5 1.4 copy-start
  10.0 11.0 %collective-permute-start.1 = (f32[512,512]{1,0:T(8,128)S(1)}, f32[512,512]{1,0:T(8,128)S(1)}, u32[]{:S(2)}, u32[]{:S(2)}) collective-permute-start(f32[512,512]{1,0:T(8,128)S(1)} %get-tuple-element.48), channel_id=1, source_target_pairs={{0,32},{32,0},{1,33},{33,1},{2,34},{34,2},{3,35},{35,3},{4,36},{36... | collective-permute-start | bytes 3145736 | tf_op jit(solution)/shard_map/ppermute | solution.py:79
  22.4 3.7 %copy-start.4 = (f32[1,2,32,512]{3,2,1,0:T(8,128)S(1)}, f32[1,2,32,512]{3,2,1,0:T(8,128)}, u32[]{:S(2)}) copy-start(f32[1,2,32,512]{3,2,1,0:T(8,128)} %param.10) | copy-start | bytes 393220
  22.4 6.0 %copy-start.5 = (f32[1,2,32,512]{3,2,1,0:T(8,128)S(1)}, f32[1,2,32,512]{3,2,1,0:T(8,128)}, u32[]{:S(2)}) copy-start(f32[1,2,32,512]{3,2,1,0:T(8,128)} %param.9) | copy-start | bytes 393220
  22.4 32.9 %all-to-all-start = ((f32[8,64,512]{2,1,0:T(8,128)}), f32[8,64,512]{2,1,0:T(8,128)S(1)}, u32[]{:S(2)}, u32[]{:S(2)}) async-start(f32[8,64,512]{2,1,0:T(8,128)} %bitcast.8), calls=%async_computation | async-start | bytes 2097152 | tf_op jit(solution)/shard_map/all_to_all | solution.py:82
  26.1 41.0 %copy-start.9 = (s32[32]{0:T(128)S(1)}, s32[32]{0:T(128)}, u32[]{:S(2)}) copy-start(s32[32]{0:T(128)} %param.13) | copy-start | bytes 388
  26.1 41.1 %copy-start.7 = (s32[32,2]{0,1:T(2,128)S(1)}, s32[32,2]{0,1:T(2,128)}, u32[]{:S(2)}) copy-start(s32[32,2]{0,1:T(2,128)} %param.11) | copy-start | bytes 772
  26.1 4.4 %collective-permute-start.2 = (f32[32,512]{1,0:T(8,128)S(1)}, f32[32,512]{1,0:T(8,128)S(1)}, u32[]{:S(2)}, u32[]{:S(2)}) collective-permute-start(f32[32,512]{1,0:T(8,128)S(1)} %get-tuple-element.47), channel_id=1, source_target_pairs={{0,32},{32,0},{1,33},{33,1},{2,34},{34,2},{3,35},{35,3},{4,36},{36... | collective-permute-start | bytes 196616 | tf_op jit(solution)/shard_map/ppermute | solution.py:65
  28.5 26.9 %collective-permute-start = (f32[32,512]{1,0:T(8,128)S(1)}, f32[32,512]{1,0:T(8,128)S(1)}, u32[]{:S(2)}, u32[]{:S(2)}) collective-permute-start(f32[32,512]{1,0:T(8,128)S(1)} %get-tuple-element.45), channel_id=1, source_target_pairs={{0,32},{32,0},{1,33},{33,1},{2,34},{34,2},{3,35},{35,3},{4,36},{36... | collective-permute-start | bytes 196616 | tf_op jit(solution)/shard_map/ppermute | solution.py:80
  56.1 47.6 %copy-start.10 = (s32[64]{0:T(128)S(1)}, s32[64]{0:T(128)}, u32[]{:S(2)}) copy-start(s32[64]{0:T(128)} %param.12) | copy-start | bytes 772
  56.1 20.6 %all-to-all-start.1 = ((f32[32,2,8,128]{3,2,1,0:T(8,128)}), f32[32,2,8,128]{3,2,1,0:T(8,128)S(1)}, u32[]{:S(2)}, u32[]{:S(2)}) async-start(f32[32,2,8,128]{3,2,1,0:T(8,128)} %pad_maximum_fusion), calls=%async_computation.1 | async-start | bytes 524288 | tf_op jit(solution)/shard_map/all_to_all | solution.py:99
  67.1 63.9 %all-gather.3.cloned.1.call-start = ((), (), s32[]{:S(2)}) async-start(), calls=%async_computation.3 | async-start | bytes 1179648 | tf_op jit(solution)/shard_map/all_gather | solution.py:106
  67.3 16.7 %copy-start.8 = (s32[32]{0:T(128)}, s32[32]{0:T(128)S(1)}, u32[]{:S(2)}) copy-start(s32[32]{0:T(128)S(1)} %select_reduce_fusion.block_ref) | copy-start | bytes 388
  77.4 6.5 %copy-start.3 = (f32[32,8,128]{2,1,0:T(8,128)}, f32[32,8,128]{2,1,0:T(8,128)S(1)}, u32[]{:S(2)}) copy-start(f32[32,8,128]{2,1,0:T(8,128)S(1)} %get-tuple-element.40.own_ref) | copy-start | bytes 393220
  77.4 6.5 %collective-permute-start.3 = (f32[32,8,128]{2,1,0:T(8,128)S(1)}, f32[32,8,128]{2,1,0:T(8,128)S(1)}, u32[]{:S(2)}, u32[]{:S(2)}) collective-permute-start(f32[32,8,128]{2,1,0:T(8,128)S(1)} %get-tuple-element.40.own_ref), channel_id=1, source_target_pairs={{0,32},{32,0},{1,33},{33,1},{2,34},{34,2},{3,35},{35,3},{4,36},{36... | collective-permute-start | bytes 393224 | tf_op jit(solution)/shard_map/ppermute | solution.py:101
  83.9 0.6 copy-start.6
  101.0 71.9 %all-gather.5.cloned.1.call-start = ((), (), s32[]{:S(2)}) async-start(), calls=%async_computation.4 | async-start | bytes 1179648 | tf_op jit(solution)/shard_map/all_gather | solution.py:107
  175.7 3.3 %copy-start.2 = (f32[32,1,8,128]{3,2,1,0:T(8,128)S(1)}, f32[32,1,8,128]{3,2,1,0:T(8,128)}, u32[]{:S(2)}) copy-start(f32[32,1,8,128]{3,2,1,0:T(8,128)} %get-tuple-element.39) | copy-start | bytes 393220
  175.7 4.1 %copy-start.1 = (f32[512,512]{1,0:T(8,128)S(1)}, f32[512,512]{1,0:T(8,128)}, u32[]{:S(2)}) copy-start(f32[512,512]{1,0:T(8,128)} %fusion.15) | copy-start | bytes 3145732
  180.0 14.6 %collective-permute-start.4 = (f32[32,512]{1,0:T(8,128)S(1)}, f32[32,512]{1,0:T(8,128)S(1)}, u32[]{:S(2)}, u32[]{:S(2)}) collective-permute-start(f32[32,512]{1,0:T(8,128)S(1)} %get-tuple-element.43), channel_id=1, source_target_pairs={{0,32},{32,0},{1,33},{33,1},{2,34},{34,2},{3,35},{35,3},{4,36},{36... | collective-permute-start | bytes 196616 | tf_op jit(solution)/shard_map/ppermute | solution.py:128
Sparse Core Ops, SparseCore 0:
  101.1 29.8 all-gather.2
  133.1 39.7 all-gather.4

commit v2 on v1

v2 whole, which is shorter than its diff:
```python
import jax
import jax.numpy as jnp
from jax import lax
from jax.experimental import pallas as pl
from jax.experimental.pallas import tpu as pltpu
from jax.sharding import Mesh, PartitionSpec as P

HISTORY = 0.5
DAMPING = 0.001
WORKER = ("x", "z")
PLANE = ("y", "x", "z")
SWAP = [(0, 1), (1, 0)]


def dot(first, second):
    return jnp.dot(
        first, second, precision=lax.Precision.HIGHEST, preferred_element_type=jnp.float32
    )


SMEM = pl.BlockSpec(memory_space=pltpu.SMEM)
VMEM = pl.BlockSpec(memory_space=pltpu.VMEM)


def to_tiles(rows):
    height, width = rows.shape
    tiles = rows.reshape(height // 8, 8, width // 128, 128).transpose(0, 2, 1, 3)
    return tiles.reshape(-1, 8, 128)


def from_tiles(tiles, width):
    split = tiles.reshape(-1, width // 128, 8, 128).transpose(0, 2, 1, 3)
    return split.reshape(-1, width)


def deliver_kernel(block_ref, piece_ref, out_ref):
    for reader in range(out_ref.shape[1]):
        block = block_ref[reader]
        total = piece_ref[0, block]
        for term in range(1, piece_ref.shape[0]):
            total = total + piece_ref[term, block]
        for copy in range(out_ref.shape[0]):
            out_ref[copy, reader] = total


def deliver(blocks, pieces):
    return pl.pallas_call(
        deliver_kernel,
        out_shape=jax.ShapeDtypeStruct(pieces.shape, pieces.dtype),
        in_specs=[SMEM, VMEM],
        out_specs=VMEM,
    )(blocks, pieces)


def warm_kernel(owner_ref, mine_ref, own_ref, sibling_ref, out_ref):
    for reader in range(out_ref.shape[0]):
        owner = owner_ref[reader]
        out_ref[reader] = jnp.where(mine_ref[reader] != 0, own_ref[owner], sibling_ref[owner])


def pick_warm(owners, mine, own_slot, sibling_slot):
    return pl.pallas_call(
        warm_kernel,
        out_shape=jax.ShapeDtypeStruct(own_slot.shape, own_slot.dtype),
        in_specs=[SMEM, SMEM, VMEM, VMEM],
        out_specs=VMEM,
    )(owners, mine, own_slot, sibling_slot)


def local(grad, prev_stats, warm_roots, owner_items, counts, read_shard):
    gradients = grad[:, 0]
    width = gradients.shape[-1]
    y_count = lax.axis_size("y")
    y = lax.axis_index("y")
    core = lax.axis_index("core")
    worker = lax.axis_index(WORKER)
    even = core == 0
    share = width // y_count
    half = share // 2
    weight = (1.0 - HISTORY) / (y_count * 2 * gradients.shape[0])

    left = jnp.einsum("mik,mjk->ij", gradients, gradients, preferred_element_type=jnp.float32)
    right = jnp.einsum("mki,mkj->ij", gradients, gradients, preferred_element_type=jnp.float32)
    place = (jnp.arange(width, dtype=jnp.int32) // half == y * 2 + core)[:, None]
    previous = HISTORY * prev_stats[0]

    def partial(first_kind):
        gram = weight * jnp.where(first_kind, left, right)
        rows = jnp.where(first_kind, previous[0], previous[1])
        rows = jnp.broadcast_to(rows[None], (width // half, half, width)).reshape(width, width)
        return gram + jnp.where(place, rows, 0.0)

    chip_sum = partial(even) + lax.ppermute(partial(~even), "core", SWAP)
    tiles = to_tiles(chip_sum)

    ids = jnp.arange(read_shard.shape[0], dtype=jnp.int32)
    blocks = jnp.sum(jnp.where(read_shard[None, :] == ids[:, None], ids[None, :], 0), 1)
    matches = owner_items[None] == (2 * blocks + core)[:, None, None]
    owners = jnp.sum(jnp.where(matches, ids[None, :, None], 0), (1, 2))
    slots = jnp.sum(jnp.where(matches, jnp.arange(2, dtype=jnp.int32), 0), (1, 2))
    mine = (slots == core).astype(jnp.int32)

    warm = warm_roots[0]
    warm_got = lax.ppermute(jnp.where(even, warm[1], warm[0]), "core", SWAP)
    warm_kept = jnp.where(even, warm[0], warm[1])
    own_warm = jnp.where(
        even,
        jnp.concatenate([warm_kept, warm_got], 0),
        jnp.concatenate([warm_got, warm_kept], 0),
    )
    own_slot = lax.all_to_all(to_tiles(own_warm), WORKER, 0, 0, tiled=True)
    sibling_slot = lax.ppermute(own_slot, "core", SWAP)
    warm_tiles = pick_warm(owners, mine, own_slot, sibling_slot)
    warm_rows = from_tiles(lax.all_to_all(warm_tiles, WORKER, 0, 0, tiled=True), width)
    warm_start = lax.all_gather(warm_rows, "y", axis=0, tiled=True)

    pieces = lax.all_to_all(tiles, PLANE, 0, 0, tiled=True).reshape((y_count, -1) + tiles.shape[1:])
    tiles = lax.all_to_all(
        deliver(blocks, pieces).reshape(tiles.shape), PLANE, 0, 0, tiled=True
    )
    statistic = from_tiles(tiles, width)

    squared = dot(warm_start, warm_start)
    fourth = dot(squared, squared)
    frobenius = jnp.sqrt(jnp.sum(statistic * statistic) + 1e-06)
    identity = jnp.eye(width, dtype=jnp.float32)
    scaled = statistic / frobenius + DAMPING * identity
    coupled = dot(fourth, scaled)
    factor = (5.0 * identity - coupled) * 0.25
    estimate = dot(warm_rows, factor)
    iterations = counts[2 * blocks[worker] + core]

    def second_step():
        factor_sq = dot(factor, factor)
        coupled_next = dot(factor_sq, dot(factor_sq, coupled))
        factor_next = (5.0 * identity - coupled_next) * 0.25
        return dot(estimate, factor_next)

    root_rows = lax.cond(iterations >= 2, second_step, lambda: estimate)
    root_sent = jnp.where(even, root_rows[half:], root_rows[:half])
    root_kept = jnp.where(even, root_rows[:half], root_rows[half:])
    root_got = lax.ppermute(root_sent, "core", SWAP)
    result = jnp.where(
        even, jnp.stack([root_kept, root_got]), jnp.stack([root_got, root_kept])
    )
    return result[None]


def solution(mesh):
    cores = 2
    x_count = 4
    dp_count, worker_count = mesh.devices.shape
    chips = Mesh(
        mesh.devices.reshape(dp_count // cores, cores, x_count, worker_count // x_count),
        ("y", "core", "x", "z"),
    )
    dp = ("y", "core")
    return jax.shard_map(
        local,
        mesh=chips,
        in_specs=(
            P(dp, WORKER, None, None),
            P(WORKER, None, dp, None),
            P(WORKER, None, dp, None),
            P(),
            P(),
            P(),
        ),
        out_specs=P(WORKER, None, dp, None),
        check_vma=False,
    )
```

time: 203 us -> 171 us (0.84)
  the two profiles are of different devices: /device:TPU:1 before, /device:TPU:77 now
where the time goes in v2:
time: 171 us; the launch traced here: 170 us
  waiting for transfers between devices  63.6 us (37%)
  starting transfers between devices  61.3 us (36%)
  between operations  15.6 us (9%)
  matrix products  12.3 us (7%)
  other arithmetic  8.3 us (5%)
  local copies, waits for them, and re-layouts  4.44 us (3%)
  Pallas kernels  4.03 us (2%)
    all_to_all x1, waiting for transfers between devices, local(): lax.all_to_all(tiles, PLANE, 0, 0, tiled=True)  28.8 us
    all_to_all x1, waiting for transfers between devices, local(): lax.all_to_all(deliver(blocks, pieces).reshape(tiles.shape), PLANE, 0, 0,...  18.6 us
    all_to_all x1, starting transfers between devices, local(): lax.all_to_all(tiles, PLANE, 0, 0, tiled=True)  13.4 us
    ppermute x1, starting transfers between devices, local(): root_got = lax.ppermute(root_sent, 'core', SWAP)  12.4 us
    all_to_all x1, starting transfers between devices, local(): own_slot = lax.all_to_all(to_tiles(own_warm), WORKER, 0, 0, tiled=True)  12 us
    all_to_all x1, starting transfers between devices, local(): lax.all_to_all(deliver(blocks, pieces).reshape(tiles.shape), PLANE, 0, 0,...  9.96 us
    dot_general x4, matrix products, dot(): jnp.dot(first, second, precision=lax.Precision.HIGHEST, preferred_element...  8.93 us
    all_to_all x1, waiting for transfers between devices, local(): own_slot = lax.all_to_all(to_tiles(own_warm), WORKER, 0, 0, tiled=True)  7.27 us
  transfers between devices with their start and end apart: 9, of which 7 were waited for; matrix products, arithmetic and copies ran while one was open for 8% of the time, Pallas kernels for 2%

profile of v2, /device:TPU:77, one launch (start us, length us, event | category | flops | bytes accessed | tf_op | source)
XLA Modules:
  0.0 169.8 jit_solution(4724112136741267634)
XLA Ops:
  6.5 0.0 copy-start
  6.5 1.0 broadcast_multiply_fusion
  7.6 0.4 copy-done
  8.0 1.0 fusion.8
  9.0 0.0 copy-start.8
  9.0 0.0 copy-start.12
  9.1 0.0 copy-start.9
  9.1 2.4 %fusion.11 = (f32[512,512]{1,0:T(8,128)}, f32[512,512]{1,0:T(8,128)}) fusion(f32[512,512]{1,0:T(8,128)S(1)} %fusion.8, f32[32,512]{1,0:T(8,128)S(1)} %get-tuple-element.41, pred[512]{0:T(512)(128)(4,1)S(1)} %fusion.22, pred[]{:T(512)S(6)} %not.3, bf16[3,1,512,512]{3,2,1,0:T(8,128)(2,1)S(1)} %copy-done), kind=kOutput, calls=%fused_computation.10 | convolution fusion | flops 806354944 | bytes 4784641 | tf_op jit(solution)/shard_map/mik,mjk->ij/dot_general | solution.py:82
  11.5 2.6 %collective-permute-start.2 = (f32[512,512]{1,0:T(8,128)}, f32[512,512]{1,0:T(8,128)}, u32[]{:S(2)}, u32[]{:S(2)}) collective-permute-start(f32[512,512]{1,0:T(8,128)} %get-tuple-element.44), channel_id=1, source_target_pairs={{0,32},{32,0},{1,33},{33,1},{2,34},{34,2},{3,35},{35,3},{4,36},{36... | collective-permute-start | bytes 3145736 | tf_op jit(solution)/shard_map/ppermute | solution.py:93
  14.0 0.0 copy-done.8
  14.1 1.9 %collective-permute-start = (f32[32,512]{1,0:T(8,128)S(1)}, f32[32,512]{1,0:T(8,128)S(1)}, u32[]{:S(2)}, u32[]{:S(2)}) collective-permute-start(f32[32,512]{1,0:T(8,128)S(1)} %get-tuple-element.43), channel_id=1, source_target_pairs={{0,32},{32,0},{1,33},{33,1},{2,34},{34,2},{3,35},{35,3},{4,36},{36... | collective-permute-start | bytes 196616 | tf_op jit(solution)/shard_map/ppermute | solution.py:104
  16.0 0.0 copy-done.12
  16.0 0.1 select_reduce_fusion.block_ref
  16.1 0.0 copy-start.10
  16.1 1.1 collective-permute-done
  17.2 0.7 maximum_select_fusion
  17.9 12.0 %all-to-all-start = ((f32[32,8,128]{2,1,0:T(8,128)}), f32[32,8,128]{2,1,0:T(8,128)S(1)}, u32[]{:S(2)}, u32[]{:S(2)}) async-start(f32[32,8,128]{2,1,0:T(8,128)} %bitcast.7), calls=%async_computation | async-start | bytes 262144 | tf_op jit(solution)/shard_map/all_to_all | solution.py:111
  29.9 0.0 copy-done.9
  29.9 0.7 fusion.21
  30.6 7.3 %all-to-all-done.own_ref = f32[32,8,128]{2,1,0:T(8,128)S(1)} async-done(((f32[32,8,128]{2,1,0:T(8,128)}), f32[32,8,128]{2,1,0:T(8,128)S(1)}, u32[]{:S(2)}, u32[]{:S(2)}) %all-to-all-start) | async-done | bytes 131104 | tf_op jit(solution)/shard_map/all_to_all | solution.py:111
  37.9 0.0 copy-start.4
  37.9 3.2 %collective-permute-start.1 = (f32[32,8,128]{2,1,0:T(8,128)S(1)}, f32[32,8,128]{2,1,0:T(8,128)S(1)}, u32[]{:S(2)}, u32[]{:S(2)}) collective-permute-start(f32[32,8,128]{2,1,0:T(8,128)S(1)} %all-to-all-done.own_ref), channel_id=1, source_target_pairs={{0,32},{32,0},{1,33},{33,1},{2,34},{34,2},{3,35},{35,3},{4,36},{36... | collective-permute-start | bytes 393224 | tf_op jit(solution)/shard_map/ppermute | solution.py:112
  41.0 0.5 compare_convert_fusion.mine_ref
  41.6 0.4 collective-permute-done.1.sibling_ref
  42.0 0.0 copy-done.4
  42.0 0.6 copy-done.7
  42.6 1.7 shard_map.64
  44.3 5.8 %all-to-all-start.1 = ((f32[32,8,128]{2,1,0:T(8,128)}), f32[32,8,128]{2,1,0:T(8,128)S(1)}, u32[]{:S(2)}, u32[]{:S(2)}) async-start(f32[32,8,128]{2,1,0:T(8,128)} %shard_map.64), calls=%async_computation.1 | async-start | bytes 262144 | tf_op jit(solution)/shard_map/all_to_all | solution.py:114
  50.1 0.0 collective-permute-done.2
  50.2 2.5 %fusion.13 = f32[512,512]{1,0:T(8,128)} fusion(f32[512,512]{1,0:T(8,128)} %collective-permute-done.2, f32[512,512]{1,0:T(8,128)} %get-tuple-element.45, f32[512,512]{1,0:T(8,128)S(1)} %fusion.8, f32[32,512]{1,0:T(8,128)S(1)} %get-tuple-element.40, pred[512]{0:T(512)(128)(4,1)S(1)} %fusion.22, pred[]{:T(512)S(6)} %eq.50), kind=kLoop, calls=%fused_computation.13 | loop fusion | flops 1310720 | bytes 4260353 | tf_op jit(solution)/shard_map/add | solution.py:93
  52.6 0.0 copy-done.10
  52.6 5.8 %all-to-all-done.1 = f32[32,8,128]{2,1,0:T(8,128)S(1)} async-done(((f32[32,8,128]{2,1,0:T(8,128)}), f32[32,8,128]{2,1,0:T(8,128)S(1)}, u32[]{:S(2)}, u32[]{:S(2)}) %all-to-all-start.1) | async-done | bytes 131104 | tf_op jit(solution)/shard_map/all_to_all | solution.py:114
  58.4 0.0 copy-start.5
  58.4 13.4 %all-to-all-start.2 = ((f32[256,8,128]{2,1,0:T(8,128)}), f32[256,8,128]{2,1,0:T(8,128)S(1)}, u32[]{:S(2)}, u32[]{:S(2)}) async-start(f32[256,8,128]{2,1,0:T(8,128)} %bitcast.22), calls=%async_computation.2 | async-start | bytes 2097152 | tf_op jit(solution)/shard_map/all_to_all | solution.py:117
  71.9 0.0 all-gather.2.cloned.1.call-start
  71.9 0.0 copy-done.5
  71.9 0.7 all-gather.2.cloned.1.call-update
  72.6 28.8 %all-to-all-done.2 = f32[256,8,128]{2,1,0:T(8,128)S(1)} async-done(((f32[256,8,128]{2,1,0:T(8,128)}), f32[256,8,128]{2,1,0:T(8,128)S(1)}, u32[]{:S(2)}, u32[]{:S(2)}) %all-to-all-start.2) | async-done | bytes 1048608 | tf_op jit(solution)/shard_map/all_to_all | solution.py:117
  101.4 0.0 copy-start.1
  101.4 1.0 copy-done.1
  102.4 2.3 %shard_map.65 = f32[8,32,8,128]{3,2,1,0:T(8,128)} custom-call(s32[32]{0:T(128)} %copy-done.10, f32[8,32,8,128]{3,2,1,0:T(8,128)} %bitcast.77), custom_call_target="tpu_custom_call" | custom-call | tf_op jit(solution)/shard_map/pallas_call | solution.py:47
  104.8 0.0 copy-start.11
  104.8 0.0 copy-start.13
  104.8 10.0 %all-to-all-start.3 = ((f32[256,8,128]{2,1,0:T(8,128)}), f32[256,8,128]{2,1,0:T(8,128)S(1)}, u32[]{:S(2)}, u32[]{:S(2)}) async-start(f32[256,8,128]{2,1,0:T(8,128)} %bitcast.76), calls=%async_computation.3 | async-start | bytes 2097152 | tf_op jit(solution)/shard_map/all_to_all | solution.py:118
  114.7 0.0 copy-done.11
  114.7 0.6 dynamic_slice.6
  116.0 0.0 copy-done.13
  116.0 0.6 dynamic_slice.7
  117.3 1.1 fusion.17
  118.4 3.4 %fusion.31 = f32[512,512]{1,0:T(8,128)S(1)} fusion(f32[512,512]{1,0:T(8,128)} %all-gather.2.cloned.1.call-done), kind=kOutput, calls=%fused_computation.54 | convolution fusion | flops 1610612736 | bytes 2097152 | tf_op jit(solution)/shard_map/dot_general | solution.py:16
  121.8 2.9 %fusion.32 = f32[512,512]{1,0:T(8,128)} fusion(f32[512,512]{1,0:T(8,128)S(1)} %fusion.31), kind=kOutput, calls=%fused_computation.55 | convolution fusion | flops 1610612736 | bytes 2097152 | tf_op jit(solution)/shard_map/dot_general | solution.py:16
  124.6 18.6 %all-to-all-done.3 = f32[256,8,128]{2,1,0:T(8,128)S(1)} async-done(((f32[256,8,128]{2,1,0:T(8,128)}), f32[256,8,128]{2,1,0:T(8,128)S(1)}, u32[]{:S(2)}, u32[]{:S(2)}) %all-to-all-start.3) | async-done | bytes 1048608 | tf_op jit(solution)/shard_map/all_to_all | solution.py:118
  143.2 0.9 multiply_reduce_fusion
  144.8 0.0 copy-start.2
  144.8 0.1 broadcast_divide_fusion
  144.9 1.1 copy-done.2
  146.0 1.9 %subtract_multiply_fusion = (f32[512,512]{1,0:T(8,128)S(1)}, f32[512,512]{1,0:T(8,128)S(1)}) fusion(f32[512,512]{1,0:T(8,128)S(1)} %copy-done.2, f32[512,512]{1,0:T(8,128)S(1)} %bitcast.78), kind=kOutput, calls=%fused_computation.14 | convolution fusion | flops 1612447744 | bytes 4194304 | tf_op jit(solution)/shard_map/dot_general | solution.py:16
  147.9 0.0 copy-done.6
  147.9 0.8 fusion.28
  148.7 0.0 copy-done.3
  148.7 0.2 conditional.1
  149.0 12.4 %collective-permute-start.3 = (f32[32,512]{1,0:T(8,128)S(1)}, f32[32,512]{1,0:T(8,128)S(1)}, u32[]{:S(2)}, u32[]{:S(2)}) collective-permute-start(f32[32,512]{1,0:T(8,128)S(1)} %get-tuple-element.39), channel_id=1, source_target_pairs={{0,32},{32,0},{1,33},{33,1},{2,34},{34,2},{3,35},{35,3},{4,36},{36... | collective-permute-start | bytes 196616 | tf_op jit(solution)/shard_map/ppermute | solution.py:142
  161.4 0.9 collective-permute-done.3
  162.3 0.7 maximum_select_fusion.1
  (9 shorter events, 0.1 us)
Async XLA Ops:
  6.5 1.5 copy-start
  9.0 5.0 %copy-start.8 = (f32[1,2,32,512]{3,2,1,0:T(8,128)S(1)}, f32[1,2,32,512]{3,2,1,0:T(8,128)}, u32[]{:S(2)}) copy-start(f32[1,2,32,512]{3,2,1,0:T(8,128)} %param.10) | copy-start | bytes 393220
  9.0 6.9 %copy-start.12 = (s32[32]{0:T(128)S(1)}, s32[32]{0:T(128)}, u32[]{:S(2)}) copy-start(s32[32]{0:T(128)} %param.13) | copy-start | bytes 388
  9.1 20.8 %copy-start.9 = (s32[32,2]{0,1:T(2,128)S(1)}, s32[32,2]{0,1:T(2,128)}, u32[]{:S(2)}) copy-start(s32[32,2]{0,1:T(2,128)} %param.11) | copy-start | bytes 772
  11.5 38.7 %collective-permute-start.2 = (f32[512,512]{1,0:T(8,128)}, f32[512,512]{1,0:T(8,128)}, u32[]{:S(2)}, u32[]{:S(2)}) collective-permute-start(f32[512,512]{1,0:T(8,128)} %get-tuple-element.44), channel_id=1, source_target_pairs={{0,32},{32,0},{1,33},{33,1},{2,34},{34,2},{3,35},{35,3},{4,36},{36... | collective-permute-start | bytes 3145736 | tf_op jit(solution)/shard_map/ppermute | solution.py:93
  14.1 3.1 %collective-permute-start = (f32[32,512]{1,0:T(8,128)S(1)}, f32[32,512]{1,0:T(8,128)S(1)}, u32[]{:S(2)}, u32[]{:S(2)}) collective-permute-start(f32[32,512]{1,0:T(8,128)S(1)} %get-tuple-element.43), channel_id=1, source_target_pairs={{0,32},{32,0},{1,33},{33,1},{2,34},{34,2},{3,35},{35,3},{4,36},{36... | collective-permute-start | bytes 196616 | tf_op jit(solution)/shard_map/ppermute | solution.py:104
  16.1 36.5 %copy-start.10 = (s32[32]{0:T(128)}, s32[32]{0:T(128)S(1)}, u32[]{:S(2)}) copy-start(s32[32]{0:T(128)S(1)} %select_reduce_fusion.block_ref) | copy-start | bytes 388
  17.9 20.0 %all-to-all-start = ((f32[32,8,128]{2,1,0:T(8,128)}), f32[32,8,128]{2,1,0:T(8,128)S(1)}, u32[]{:S(2)}, u32[]{:S(2)}) async-start(f32[32,8,128]{2,1,0:T(8,128)} %bitcast.7), calls=%async_computation | async-start | bytes 262144 | tf_op jit(solution)/shard_map/all_to_all | solution.py:111
  37.9 4.1 %copy-start.4 = (f32[32,8,128]{2,1,0:T(8,128)}, f32[32,8,128]{2,1,0:T(8,128)S(1)}, u32[]{:S(2)}) copy-start(f32[32,8,128]{2,1,0:T(8,128)S(1)} %all-to-all-done.own_ref) | copy-start | bytes 393220
  37.9 4.1 %collective-permute-start.1 = (f32[32,8,128]{2,1,0:T(8,128)S(1)}, f32[32,8,128]{2,1,0:T(8,128)S(1)}, u32[]{:S(2)}, u32[]{:S(2)}) collective-permute-start(f32[32,8,128]{2,1,0:T(8,128)S(1)} %all-to-all-done.own_ref), channel_id=1, source_target_pairs={{0,32},{32,0},{1,33},{33,1},{2,34},{34,2},{3,35},{35,3},{4,36},{36... | collective-permute-start | bytes 393224 | tf_op jit(solution)/shard_map/ppermute | solution.py:112
  42.0 0.6 copy-start.7
  44.3 14.1 %all-to-all-start.1 = ((f32[32,8,128]{2,1,0:T(8,128)}), f32[32,8,128]{2,1,0:T(8,128)S(1)}, u32[]{:S(2)}, u32[]{:S(2)}) async-start(f32[32,8,128]{2,1,0:T(8,128)} %shard_map.64), calls=%async_computation.1 | async-start | bytes 262144 | tf_op jit(solution)/shard_map/all_to_all | solution.py:114
  58.4 13.5 %copy-start.5 = (f32[32,8,128]{2,1,0:T(8,128)}, f32[32,8,128]{2,1,0:T(8,128)S(1)}, u32[]{:S(2)}) copy-start(f32[32,8,128]{2,1,0:T(8,128)S(1)} %all-to-all-done.1) | copy-start | bytes 393220
  58.4 43.0 %all-to-all-start.2 = ((f32[256,8,128]{2,1,0:T(8,128)}), f32[256,8,128]{2,1,0:T(8,128)S(1)}, u32[]{:S(2)}, u32[]{:S(2)}) async-start(f32[256,8,128]{2,1,0:T(8,128)} %bitcast.22), calls=%async_computation.2 | async-start | bytes 2097152 | tf_op jit(solution)/shard_map/all_to_all | solution.py:117
  71.9 46.5 %all-gather.2.cloned.1.call-start = ((), (), s32[]{:S(2)}) async-start(), calls=%async_computation.4 | async-start | bytes 1179648 | tf_op jit(solution)/shard_map/all_gather | solution.py:115
  101.4 1.0 copy-start.1
  104.8 10.0 %copy-start.11 = (s32[32]{0:T(128)S(1)}, s32[32]{0:T(128)}, u32[]{:S(2)}) copy-start(s32[32]{0:T(128)} %copy-done.10) | copy-start | bytes 388
  104.8 11.2 %copy-start.13 = (s32[64]{0:T(128)S(1)}, s32[64]{0:T(128)}, u32[]{:S(2)}) copy-start(s32[64]{0:T(128)} %param.12) | copy-start | bytes 772
  104.8 38.5 %all-to-all-start.3 = ((f32[256,8,128]{2,1,0:T(8,128)}), f32[256,8,128]{2,1,0:T(8,128)S(1)}, u32[]{:S(2)}, u32[]{:S(2)}) async-start(f32[256,8,128]{2,1,0:T(8,128)} %bitcast.76), calls=%async_computation.3 | async-start | bytes 2097152 | tf_op jit(solution)/shard_map/all_to_all | solution.py:118
  144.8 1.2 copy-start.2
  146.0 1.9 %copy-start.6 = (f32[32,8,128]{2,1,0:T(8,128)S(1)}, f32[32,8,128]{2,1,0:T(8,128)}, u32[]{:S(2)}) copy-start(f32[32,8,128]{2,1,0:T(8,128)} %copy-done.5) | copy-start | bytes 393220
  146.0 2.7 %copy-start.3 = (f32[512,512]{1,0:T(8,128)S(1)}, f32[512,512]{1,0:T(8,128)}, u32[]{:S(2)}) copy-start(f32[512,512]{1,0:T(8,128)} %fusion.17) | copy-start | bytes 3145732
  149.0 13.3 %collective-permute-start.3 = (f32[32,512]{1,0:T(8,128)S(1)}, f32[32,512]{1,0:T(8,128)S(1)}, u32[]{:S(2)}, u32[]{:S(2)}) collective-permute-start(f32[32,512]{1,0:T(8,128)S(1)} %get-tuple-element.39), channel_id=1, source_target_pairs={{0,32},{32,0},{1,33},{33,1},{2,34},{34,2},{3,35},{35,3},{4,36},{36... | collective-permute-start | bytes 196616 | tf_op jit(solution)/shard_map/ppermute | solution.py:142
Sparse Core Ops, SparseCore 0:
  74.8 40.2 all-gather.1

commit v3 on v2

v3 whole, which is shorter than its diff:
```python
import jax
import jax.numpy as jnp
from jax import lax
from jax.experimental import pallas as pl
from jax.experimental.pallas import tpu as pltpu
from jax.sharding import Mesh, PartitionSpec as P

HISTORY = 0.5
DAMPING = 0.001
WORKER = ("x", "z")
PLANE = ("y", "x", "z")
SWAP = [(0, 1), (1, 0)]
BLOCK = 128
SMEM = pl.BlockSpec(memory_space=pltpu.SMEM)
VMEM = pl.BlockSpec(memory_space=pltpu.VMEM)


def dot(first, second, precision=lax.Precision.HIGHEST):
    return jnp.dot(first, second, precision=precision, preferred_element_type=jnp.float32)


def shape_of(*shape):
    return jax.ShapeDtypeStruct(shape, jnp.float32)


def upper_blocks(width):
    count = width // BLOCK
    pairs = [(i, j) for i in range(count) for j in range(i, count)]
    return [
        (pl.ds(number * BLOCK, BLOCK), pl.ds(i * BLOCK, BLOCK), pl.ds(j * BLOCK, BLOCK))
        for number, (i, j) in enumerate(pairs)
    ]


def upper_kernel(weight, core_ref, left_ref, right_ref, kept_ref, sent_ref):
    even = core_ref[0] == 0
    for packed, rows, columns in upper_blocks(left_ref.shape[0]):
        left = left_ref[rows, columns] * weight
        right = right_ref[rows, columns] * weight
        kept_ref[packed, :] = jnp.where(even, left, right)
        sent_ref[packed, :] = jnp.where(even, right, left)


def pack_upper(core, left, right, weight):
    rows = len(upper_blocks(left.shape[0])) * BLOCK

    def kernel(*refs):
        upper_kernel(weight, *refs)

    return pl.pallas_call(
        kernel,
        out_shape=[shape_of(rows, BLOCK)] * 2,
        in_specs=[SMEM, VMEM, VMEM],
        out_specs=[VMEM] * 2,
    )(core, left, right)


def scaled_kernel(packed_ref, carried_ref, out_ref):
    width = out_ref.shape[0]
    share = carried_ref.shape[2]

    def previous(rows, columns):
        first = rows.start // share
        parts = [carried_ref[first + n, 1, :, columns] for n in range(BLOCK // share)]
        return HISTORY * jnp.concatenate(parts, 0)

    total = jnp.zeros((1, BLOCK), jnp.float32)
    for packed, rows, columns in upper_blocks(width):
        sums = packed_ref[packed, :]
        value = sums + previous(rows, columns)
        out_ref[rows, columns] = value
        total = total + jnp.sum(value * value, axis=0, keepdims=True)
        if rows.start != columns.start:
            value = sums.T + previous(columns, rows)
            out_ref[columns, rows] = value
            total = total + jnp.sum(value * value, axis=0, keepdims=True)
    inverse = 1.0 / jnp.sqrt(jnp.sum(total, axis=1, keepdims=True) + 1e-06)
    row = lax.broadcasted_iota(jnp.int32, (BLOCK, width), 0)
    column = lax.broadcasted_iota(jnp.int32, (BLOCK, width), 1)
    for first in range(0, width, BLOCK):
        diagonal = jnp.where(column == row + first, DAMPING, 0.0)
        out_ref[pl.ds(first, BLOCK), :] = out_ref[pl.ds(first, BLOCK), :] * inverse + diagonal


def scaled_statistic(packed, carried):
    width = carried.shape[-1]
    return pl.pallas_call(
        scaled_kernel,
        out_shape=shape_of(width, width),
        in_specs=[VMEM] * 2,
        out_specs=VMEM,
    )(packed, carried)


def deliver_kernel(block_ref, piece_ref, out_ref):
    readers = block_ref.shape[0]
    copies = piece_ref.shape[0] // readers
    for reader in range(readers):
        block = block_ref[reader]
        total = piece_ref[block]
        for term in range(1, copies):
            total = total + piece_ref[term * readers + block]
        for copy in range(copies):
            out_ref[copy * readers + reader] = total


def deliver(blocks, pieces):
    return pl.pallas_call(
        deliver_kernel,
        out_shape=shape_of(*pieces.shape),
        in_specs=[SMEM, VMEM],
        out_specs=VMEM,
    )(blocks, pieces)


def spread_kernel(warm_ref, prev_ref, out_ref):
    for number, in_ref in enumerate((warm_ref, prev_ref)):
        _, rows, width = in_ref.shape
        for half in range(2):
            for j in range(out_ref.shape[0]):
                i, t = divmod(j, width // BLOCK)
                out_ref[j, number, pl.ds(4 * half, 4), :] = in_ref[
                    half, pl.ds(4 * i, 4), pl.ds(BLOCK * t, BLOCK)
                ]


def spread_tiles(warm, prev):
    count = warm.shape[1] * warm.shape[2] // (4 * BLOCK)
    return pl.pallas_call(
        spread_kernel,
        out_shape=shape_of(count, 2, 8, BLOCK),
        in_specs=[VMEM] * 2,
        out_specs=VMEM,
    )(warm, prev)


def pick_kernel(block_ref, owner_ref, slot_ref, tile_ref, out_ref):
    for reader in range(out_ref.shape[0]):
        for kind in range(2):
            place = 2 * reader + kind
            first = pl.multiple_of(4 * slot_ref[place], 4)
            out_ref[reader, 0, pl.ds(4 * kind, 4), :] = tile_ref[
                owner_ref[place], 0, pl.ds(first, 4), :
            ]
        out_ref[reader, 1] = tile_ref[block_ref[reader], 1]


def pick(blocks, owners, slots, tiles):
    return pl.pallas_call(
        pick_kernel,
        out_shape=shape_of(*tiles.shape),
        in_specs=[SMEM] * 3 + [VMEM],
        out_specs=VMEM,
    )(blocks, owners, slots, tiles)


def rows_kernel(core_ref, tile_ref, kept_ref, sent_ref):
    width = kept_ref.shape[2]
    for out_ref, kind in ((kept_ref, core_ref[0]), (sent_ref, 1 - core_ref[0])):
        first = pl.multiple_of(4 * kind, 4)
        for number in range(2):
            for j in range(tile_ref.shape[0]):
                i, t = divmod(j, width // BLOCK)
                out_ref[number, pl.ds(4 * i, 4), pl.ds(BLOCK * t, BLOCK)] = tile_ref[
                    j, number, pl.ds(first, 4), :
                ]


def rows_of_kinds(core, tiles, rows, width):
    return pl.pallas_call(
        rows_kernel,
        out_shape=[shape_of(2, rows, width)] * 2,
        in_specs=[SMEM, VMEM],
        out_specs=[VMEM] * 2,
    )(core, tiles)


def local(grad, prev_stats, warm_roots, owner_items, counts, read_shard):
    gradients = grad[:, 0]
    width = gradients.shape[-1]
    y_count = lax.axis_size("y")
    core = lax.axis_index("core")
    worker = lax.axis_index(WORKER)
    even = core == 0
    core_place = core.reshape(1)
    share = width // y_count
    half = share // 2
    weight = (1.0 - HISTORY) / (y_count * 2 * gradients.shape[0])

    ids = jnp.arange(read_shard.shape[0], dtype=jnp.int32)
    blocks = jnp.sum(jnp.where(read_shard[None, :] == ids[:, None], ids[None, :], 0), 1)
    items = (2 * blocks[:, None] + jnp.arange(2, dtype=jnp.int32)).reshape(-1)
    matches = owner_items[None] == items[:, None, None]
    owners = jnp.sum(jnp.where(matches, ids[None, :, None], 0), (1, 2))
    slots = jnp.sum(jnp.where(matches, jnp.arange(2, dtype=jnp.int32), 0), (1, 2))

    tiles = spread_tiles(warm_roots[0], prev_stats[0])
    tiles = lax.all_to_all(tiles, WORKER, 0, 0, tiled=True)
    tiles = lax.all_to_all(pick(blocks, owners, slots, tiles), WORKER, 0, 0, tiled=True)
    kept, sent = rows_of_kinds(core_place, tiles, half, width)
    got = lax.ppermute(sent, "core", SWAP)
    carried = jnp.where(
        even, jnp.concatenate([kept, got], 1), jnp.concatenate([got, kept], 1)
    )
    warm_rows = carried[0]
    carried = lax.all_gather(carried, "y", axis=0, tiled=False)
    warm_start = carried[:, 0].reshape(width, width)

    left = jnp.einsum("mik,mjk->ij", gradients, gradients, preferred_element_type=jnp.float32)
    right = jnp.einsum("mki,mkj->ij", gradients, gradients, preferred_element_type=jnp.float32)
    kept, sent = pack_upper(core_place, left, right, weight)
    packed = kept + lax.ppermute(sent, "core", SWAP)
    peers = y_count * read_shard.shape[0]
    pieces = lax.all_to_all(packed.reshape(peers, 1, -1), PLANE, 0, 0, tiled=True)
    pieces = lax.all_to_all(deliver(blocks, pieces), PLANE, 0, 0, tiled=True)
    scaled = scaled_statistic(pieces.reshape(packed.shape), carried)

    squared = dot(warm_start, warm_start)
    fourth = dot(squared, squared)
    identity = jnp.eye(width, dtype=jnp.float32)
    coupled = dot(fourth, scaled)
    factor = (5.0 * identity - coupled) * 0.25
    high = lax.Precision.HIGH
    estimate = dot(warm_rows, factor, high)
    iterations = counts[2 * blocks[worker] + core]

    def second_step():
        factor_sq = dot(factor, factor, high)
        coupled_next = dot(factor_sq, dot(factor_sq, coupled, high), high)
        factor_next = (5.0 * identity - coupled_next) * 0.25
        return dot(estimate, factor_next, high)

    root_rows = lax.cond(iterations >= 2, second_step, lambda: estimate)
    root_sent = jnp.where(even, root_rows[half:], root_rows[:half])
    root_kept = jnp.where(even, root_rows[:half], root_rows[half:])
    root_got = lax.ppermute(root_sent, "core", SWAP)
    result = jnp.where(
        even, jnp.stack([root_kept, root_got]), jnp.stack([root_got, root_kept])
    )
    return result[None]


def solution(mesh):
    cores = 2
    x_count = 4
    dp_count, worker_count = mesh.devices.shape
    chips = Mesh(
        mesh.devices.reshape(dp_count // cores, cores, x_count, worker_count // x_count),
        ("y", "core", "x", "z"),
    )
    dp = ("y", "core")
    return jax.shard_map(
        local,
        mesh=chips,
        in_specs=(
            P(dp, WORKER, None, None),
            P(WORKER, None, dp, None),
            P(WORKER, None, dp, None),
            P(),
            P(),
            P(),
        ),
        out_specs=P(WORKER, None, dp, None),
        check_vma=False,
    )
```

time: 171 us -> 175 us (1.023)
  the two profiles are of different devices: /device:TPU:77 before, /device:TPU:1 now
where the time goes in v3:
time: 175 us; the launch traced here: 174 us
  starting transfers between devices  46.4 us (27%)
  blocking collectives  42.6 us (24%)
  waiting for transfers between devices  31.9 us (18%)
  between operations  14.9 us (9%)
  Pallas kernels  13.3 us (8%)
  matrix products  12.5 us (7%)
  other arithmetic  6.76 us (4%)
  local copies, waits for them, and re-layouts  5.61 us (3%)
    all_to_all x1, blocking collectives, local(): lax.all_to_all(packed.reshape(peers, 1, -1), PLANE, 0, 0, tiled=True)  42.6 us
    all_to_all x1, starting transfers between devices, local(): tiles = lax.all_to_all(tiles, WORKER, 0, 0, tiled=True)  13.7 us
    all_to_all x1, waiting for transfers between devices, local(): pieces = lax.all_to_all(deliver(blocks, pieces), PLANE, 0, 0, tiled=True)  10.9 us
    all_to_all x1, starting transfers between devices, local(): pieces = lax.all_to_all(deliver(blocks, pieces), PLANE, 0, 0, tiled=True)  9.97 us
    all_to_all x1, waiting for transfers between devices, local(): lax.all_to_all(pick(blocks, owners, slots, tiles), WORKER, 0, 0, tiled=True)  9.61 us
    ppermute x1, starting transfers between devices, local(): root_got = lax.ppermute(root_sent, 'core', SWAP)  8.62 us
    dot_general x4, matrix products, dot(): jnp.dot(first, second, precision=precision, preferred_element_type=jnp.fl...  8.57 us
    all_to_all x1, waiting for transfers between devices, local(): tiles = lax.all_to_all(tiles, WORKER, 0, 0, tiled=True)  7.44 us
  transfers between devices with their start and end apart: 7, of which 6 were waited for; matrix products, arithmetic and copies ran while one was open for 8% of the time, Pallas kernels for 3%

profile of v3, /device:TPU:1, one launch (start us, length us, event | category | flops | bytes accessed | tf_op | source)
XLA Modules:
  0.0 174.0 jit_solution(11229166178585458035)
XLA Ops:
  6.5 0.0 copy-start
  6.5 1.8 %shard_map.64 = f32[32,2,8,128]{3,2,1,0:T(8,128)} custom-call(f32[2,32,512]{2,1,0:T(8,128)} %bitcast.50, f32[2,32,512]{2,1,0:T(8,128)} %bitcast.51), custom_call_target="tpu_custom_call" | custom-call | tf_op jit(solution)/shard_map/pallas_call | solution.py:129
  8.4 13.7 %all-to-all-start = ((f32[32,2,8,128]{3,2,1,0:T(8,128)}), f32[32,2,8,128]{3,2,1,0:T(8,128)S(1)}, u32[]{:S(2)}, u32[]{:S(2)}) async-start(f32[32,2,8,128]{3,2,1,0:T(8,128)} %shard_map.64), calls=%async_computation | async-start | bytes 524288 | tf_op jit(solution)/shard_map/all_to_all | solution.py:198
  22.1 0.8 select_reduce_fusion.block_ref
  22.9 0.0 copy-start.6
  22.9 0.1 iota_add_fusion
  22.9 0.1 add.42
  23.1 1.3 fusion.20
  24.3 7.4 %all-to-all-done.tile_ref = f32[32,2,8,128]{3,2,1,0:T(8,128)S(1)} async-done(((f32[32,2,8,128]{3,2,1,0:T(8,128)}), f32[32,2,8,128]{3,2,1,0:T(8,128)S(1)}, u32[]{:S(2)}, u32[]{:S(2)}) %all-to-all-start) | async-done | bytes 262176 | tf_op jit(solution)/shard_map/all_to_all | solution.py:198
  31.8 0.0 copy-start.3
  31.8 0.0 copy-done.6
  31.8 0.7 copy-done.3
  32.5 1.8 %shard_map.65 = f32[32,2,8,128]{3,2,1,0:T(8,128)} custom-call(s32[32]{0:T(128)} %copy-done.6, s32[64]{0:T(128)} %get-tuple-element.45.owner_ref, s32[64]{0:T(128)} %get-tuple-element.44.slot_ref, f32[32,2,8,128]{3,2,1,0:T(8,128)} %copy-done.3), custom_call_target="tpu_custom_call" | custom-call | tf_op jit(solution)/shard_map/pallas_call | solution.py:149
  34.3 6.3 %all-to-all-start.1 = ((f32[32,2,8,128]{3,2,1,0:T(8,128)}), f32[32,2,8,128]{3,2,1,0:T(8,128)S(1)}, u32[]{:S(2)}, u32[]{:S(2)}) async-start(f32[32,2,8,128]{3,2,1,0:T(8,128)} %shard_map.65), calls=%async_computation.1 | async-start | bytes 524288 | tf_op jit(solution)/shard_map/all_to_all | solution.py:199
  40.5 0.0 all-gather.2.cloned.1.call-start
  40.6 9.6 %all-to-all-done.1.tile_ref = f32[32,2,8,128]{3,2,1,0:T(8,128)S(1)} async-done(((f32[32,2,8,128]{3,2,1,0:T(8,128)}), f32[32,2,8,128]{3,2,1,0:T(8,128)S(1)}, u32[]{:S(2)}, u32[]{:S(2)}) %all-to-all-start.1) | async-done | bytes 262176 | tf_op jit(solution)/shard_map/all_to_all | solution.py:199
  50.2 0.0 copy-start.4
  50.2 0.7 copy-done.4
  50.9 1.7 shard_map.66
  52.6 5.5 %collective-permute-start = (f32[2,32,512]{2,1,0:T(8,128)}, f32[2,32,512]{2,1,0:T(8,128)S(1)}, u32[]{:S(2)}, u32[]{:S(2)}) collective-permute-start(f32[2,32,512]{2,1,0:T(8,128)} %get-tuple-element.38), channel_id=1, source_target_pairs={{0,32},{32,0},{1,33},{33,1},{2,34},{34,2},{3,35},{35,3},{4,36},{36... | collective-permute-start | bytes 393224 | tf_op jit(solution)/shard_map/ppermute | solution.py:201
  58.1 1.2 collective-permute-done
  59.3 1.7 maximum_select_fusion
  61.0 0.0 all-gather.2.cloned.1.call-update
  61.0 0.0 copy-done
  61.0 2.0 %fusion.5.refs_1_ = f32[512,512]{1,0:T(8,128)} fusion(bf16[3,1,512,512]{3,2,1,0:T(8,128)(2,1)S(1)} %copy-done), kind=kOutput, calls=%fused_computation.7 | convolution fusion | flops 805306368 | bytes 2621440 | tf_op jit(solution)/shard_map/mik,mjk->ij/dot_general | solution.py:209
  63.0 2.0 %fusion.8.refs_2_ = f32[512,512]{1,0:T(8,128)} fusion(bf16[3,1,512,512]{3,2,1,0:T(8,128)(2,1)S(1)} %copy-done), kind=kOutput, calls=%fused_computation.8 | convolution fusion | flops 805306368 | bytes 2621440 | tf_op jit(solution)/shard_map/mki,mkj->ij/dot_general | solution.py:210
  65.0 2.8 %shard_map.67 = (f32[1280,128]{1,0:T(8,128)}, f32[1280,128]{1,0:T(8,128)}) custom-call(s32[1]{0:T(128)} %bitcast.3.core_ref.refs_0_, f32[512,512]{1,0:T(8,128)} %fusion.5.refs_1_, f32[512,512]{1,0:T(8,128)} %fusion.8.refs_2_), custom_call_target="tpu_custom_call" | custom-call | tf_op jit(solution)/shard_map/pallas_call | solution.py:50
  67.8 2.3 %collective-permute-start.1 = (f32[1280,128]{1,0:T(8,128)}, f32[1280,128]{1,0:T(8,128)S(1)}, u32[]{:S(2)}, u32[]{:S(2)}) collective-permute-start(f32[1280,128]{1,0:T(8,128)} %get-tuple-element.40), channel_id=1, source_target_pairs={{0,32},{32,0},{1,33},{33,1},{2,34},{34,2},{3,35},{35,3},{4,36},{36... | collective-permute-start | bytes 1966088 | tf_op jit(solution)/shard_map/ppermute | solution.py:212
  70.0 1.9 %collective-permute-done.1 = f32[1280,128]{1,0:T(8,128)S(1)} collective-permute-done((f32[1280,128]{1,0:T(8,128)}, f32[1280,128]{1,0:T(8,128)S(1)}, u32[]{:S(2)}, u32[]{:S(2)}) %collective-permute-start.1) | collective-permute-done | bytes 655392 | tf_op jit(solution)/shard_map/ppermute | solution.py:212
  72.0 1.2 add.43
  73.1 42.6 %all_to_all.20.piece_ref = f32[256,1,640]{2,1,0:T(1,128)} all-to-all(f32[256,1,640]{2,1,0:T(1,128)S(1)} %bitcast.46), channel_id=1, replica_groups=mesh['y'=8,'core'=2,'x'=4,'z'=8] {'y','x','z'}, dimensions={0} | all-to-all | bytes 1310720 | tf_op jit(solution)/shard_map/all_to_all | solution.py:214
  115.7 0.0 copy-start.7
  115.7 0.0 copy-start.8
  115.7 2.1 %shard_map.68 = f32[256,1,640]{2,1,0:T(1,128)} custom-call(s32[32]{0:T(128)} %copy-done.6, f32[256,1,640]{2,1,0:T(1,128)} %all_to_all.20.piece_ref), custom_call_target="tpu_custom_call" | custom-call | tf_op jit(solution)/shard_map/pallas_call | solution.py:108
  117.8 10.0 %all-to-all-start.3 = ((f32[256,1,640]{2,1,0:T(1,128)}), f32[256,1,640]{2,1,0:T(1,128)S(1)}, u32[]{:S(2)}, u32[]{:S(2)}) async-start(f32[256,1,640]{2,1,0:T(1,128)} %shard_map.68), calls=%async_computation.3 | async-start | bytes 1310720 | tf_op jit(solution)/shard_map/all_to_all | solution.py:215
  127.8 0.0 copy-done.7
  127.8 0.7 dynamic_slice.6
  129.2 0.0 copy-done.8
  129.2 0.6 dynamic_slice.7
  130.5 1.1 fusion.11
  131.6 0.0 all-gather.2.cloned.1.call-done.carried_ref
  131.6 0.0 slice-start
  131.6 1.2 slice-done
  132.8 1.8 %fusion.24 = f32[512,512]{1,0:T(8,128)S(1)} fusion(f32[512,512]{1,0:T(8,128)S(1)} %bitcast.45), kind=kOutput, calls=%fused_computation.35 | convolution fusion | flops 1610612736 | bytes 2097152 | tf_op jit(solution)/shard_map/dot_general | solution.py:19
  134.6 2.8 %fusion.25 = f32[512,512]{1,0:T(8,128)} fusion(f32[512,512]{1,0:T(8,128)S(1)} %fusion.24), kind=kOutput, calls=%fused_computation.36 | convolution fusion | flops 1610612736 | bytes 2097152 | tf_op jit(solution)/shard_map/dot_general | solution.py:19
  137.5 10.9 %all-to-all-done.3 = f32[256,1,640]{2,1,0:T(1,128)S(1)} async-done(((f32[256,1,640]{2,1,0:T(1,128)}), f32[256,1,640]{2,1,0:T(1,128)S(1)}, u32[]{:S(2)}, u32[]{:S(2)}) %all-to-all-start.3) | async-done | bytes 655392 | tf_op jit(solution)/shard_map/all_to_all | solution.py:215
  148.3 0.0 copy-start.2
  148.4 0.9 copy-done.2
  149.2 3.1 %shard_map.69 = f32[512,512]{1,0:T(8,128)} custom-call(f32[1280,128]{1,0:T(8,128)} %bitcast.47, f32[8,2,64,512]{3,2,1,0:T(8,128)} %all-gather.2.cloned.1.call-done.carried_ref), custom_call_target="tpu_custom_call" | custom-call | tf_op jit(solution)/shard_map/pallas_call | solution.py:87
  152.4 0.0 copy-start.5
  152.4 3.4 %subtract_multiply_fusion = (f32[512,512]{1,0:T(8,128)S(1)}, f32[512,512]{1,0:T(8,128)S(1)}) fusion(f32[512,512]{1,0:T(8,128)} %fusion.25, f32[512,512]{1,0:T(8,128)} %shard_map.69), kind=kOutput, calls=%fused_computation.9 | convolution fusion | flops 1611661312 | bytes 4194304 | tf_op jit(solution)/shard_map/dot_general | solution.py:19
  155.8 0.0 copy-start.1
  155.8 0.0 copy-done.5
  155.8 0.5 fusion.14
  156.3 0.7 copy-done.1
  157.0 8.6 %collective-permute-start.2 = (f32[32,512]{1,0:T(8,128)S(1)}, f32[32,512]{1,0:T(8,128)S(1)}, u32[]{:S(2)}, u32[]{:S(2)}) collective-permute-start(f32[32,512]{1,0:T(8,128)S(1)} %get-tuple-element.47), channel_id=1, source_target_pairs={{0,32},{32,0},{1,33},{33,1},{2,34},{34,2},{3,35},{35,3},{4,36},{36... | collective-permute-start | bytes 196616 | tf_op jit(solution)/shard_map/ppermute | solution.py:236
  165.6 0.9 collective-permute-done.2
  166.5 0.7 maximum_select_fusion.1
  (3 shorter events, 0.0 us)
Async XLA Ops:
  6.5 54.5 %copy-start = (bf16[3,1,512,512]{3,2,1,0:T(8,128)(2,1)S(1)}, bf16[3,1,512,512]{3,2,1,0:T(8,128)(2,1)}, u32[]{:S(2)}) copy-start(bf16[3,1,512,512]{3,2,1,0:T(8,128)(2,1)} %param.8) | copy-start | bytes 4718596
  8.4 23.4 %all-to-all-start = ((f32[32,2,8,128]{3,2,1,0:T(8,128)}), f32[32,2,8,128]{3,2,1,0:T(8,128)S(1)}, u32[]{:S(2)}, u32[]{:S(2)}) async-start(f32[32,2,8,128]{3,2,1,0:T(8,128)} %shard_map.64), calls=%async_computation | async-start | bytes 524288 | tf_op jit(solution)/shard_map/all_to_all | solution.py:198
  22.9 8.9 %copy-start.6 = (s32[32]{0:T(128)}, s32[32]{0:T(128)S(1)}, u32[]{:S(2)}) copy-start(s32[32]{0:T(128)S(1)} %select_reduce_fusion.block_ref) | copy-start | bytes 388
  31.8 0.7 copy-start.3
  34.3 16.0 %all-to-all-start.1 = ((f32[32,2,8,128]{3,2,1,0:T(8,128)}), f32[32,2,8,128]{3,2,1,0:T(8,128)S(1)}, u32[]{:S(2)}, u32[]{:S(2)}) async-start(f32[32,2,8,128]{3,2,1,0:T(8,128)} %shard_map.65), calls=%async_computation.1 | async-start | bytes 524288 | tf_op jit(solution)/shard_map/all_to_all | solution.py:199
  40.5 91.0 %all-gather.2.cloned.1.call-start = ((), (), s32[]{:S(2)}) async-start(), calls=%async_computation.4 | async-start | bytes 2359296 | tf_op jit(solution)/shard_map/all_gather | solution.py:206
  50.2 0.7 copy-start.4
  52.6 6.7 %collective-permute-start = (f32[2,32,512]{2,1,0:T(8,128)}, f32[2,32,512]{2,1,0:T(8,128)S(1)}, u32[]{:S(2)}, u32[]{:S(2)}) collective-permute-start(f32[2,32,512]{2,1,0:T(8,128)} %get-tuple-element.38), channel_id=1, source_target_pairs={{0,32},{32,0},{1,33},{33,1},{2,34},{34,2},{3,35},{35,3},{4,36},{36... | collective-permute-start | bytes 393224 | tf_op jit(solution)/shard_map/ppermute | solution.py:201
  67.8 4.2 %collective-permute-start.1 = (f32[1280,128]{1,0:T(8,128)}, f32[1280,128]{1,0:T(8,128)S(1)}, u32[]{:S(2)}, u32[]{:S(2)}) collective-permute-start(f32[1280,128]{1,0:T(8,128)} %get-tuple-element.40), channel_id=1, source_target_pairs={{0,32},{32,0},{1,33},{33,1},{2,34},{34,2},{3,35},{35,3},{4,36},{36... | collective-permute-start | bytes 1966088 | tf_op jit(solution)/shard_map/ppermute | solution.py:212
  115.7 12.1 %copy-start.7 = (s32[32]{0:T(128)S(1)}, s32[32]{0:T(128)}, u32[]{:S(2)}) copy-start(s32[32]{0:T(128)} %copy-done.6) | copy-start | bytes 388
  115.7 13.5 %copy-start.8 = (s32[64]{0:T(128)S(1)}, s32[64]{0:T(128)}, u32[]{:S(2)}) copy-start(s32[64]{0:T(128)} %param.12) | copy-start | bytes 772
  117.8 30.5 %all-to-all-start.3 = ((f32[256,1,640]{2,1,0:T(1,128)}), f32[256,1,640]{2,1,0:T(1,128)S(1)}, u32[]{:S(2)}, u32[]{:S(2)}) async-start(f32[256,1,640]{2,1,0:T(1,128)} %shard_map.68), calls=%async_computation.3 | async-start | bytes 1310720 | tf_op jit(solution)/shard_map/all_to_all | solution.py:215
  131.6 1.2 slice-start
  148.3 0.9 copy-start.2
  152.4 3.4 %copy-start.5 = (f32[2,32,512]{2,1,0:T(8,128)S(1)}, f32[2,32,512]{2,1,0:T(8,128)}, u32[]{:S(2)}) copy-start(f32[2,32,512]{2,1,0:T(8,128)} %get-tuple-element.37) | copy-start | bytes 393220
  155.8 1.2 copy-start.1
  157.0 9.5 %collective-permute-start.2 = (f32[32,512]{1,0:T(8,128)S(1)}, f32[32,512]{1,0:T(8,128)S(1)}, u32[]{:S(2)}, u32[]{:S(2)}) collective-permute-start(f32[32,512]{1,0:T(8,128)S(1)} %get-tuple-element.47), channel_id=1, source_target_pairs={{0,32},{32,0},{1,33},{33,1},{2,34},{34,2},{3,35},{35,3},{4,36},{36... | collective-permute-start | bytes 196616 | tf_op jit(solution)/shard_map/ppermute | solution.py:236
Sparse Core Ops, SparseCore 0:
  61.1 48.9 all-gather.1

commit v4 on v2

v4 whole, which is shorter than its diff:
```python
import jax
import jax.numpy as jnp
from jax import lax
from jax.experimental import pallas as pl
from jax.experimental.pallas import tpu as pltpu
from jax.sharding import Mesh, PartitionSpec as P

HISTORY = 0.5
DAMPING = 0.001
WORKER = ("x", "z")
PLANE = ("y", "x", "z")
SWAP = [(0, 1), (1, 0)]
LANES = 128
HALF_LANES = 64
TILE = 8
SMEM = pl.BlockSpec(memory_space=pltpu.SMEM)
VMEM = pl.BlockSpec(memory_space=pltpu.VMEM)


def dot(first, second, precision=lax.Precision.HIGHEST):
    return jnp.dot(first, second, precision=precision, preferred_element_type=jnp.float32)


def shape_of(*shape):
    return jax.ShapeDtypeStruct(shape, jnp.float32)


def low_lanes(rows=TILE):
    return lax.broadcasted_iota(jnp.int32, (rows, LANES), 1) < HALF_LANES


def turn(value):
    return pltpu.roll(value, HALF_LANES, 1)


def tile_columns(width):
    return [pl.ds(LANES * t, LANES) for t in range(width // LANES)]


def pair_kinds(low, first, second):
    return (
        jnp.where(low, first, turn(second)),
        jnp.where(low, turn(first), second),
    )


def halves_kernel(weight, place_ref, left_ref, right_ref, prev_ref, kept_ref, sent_ref):
    y, core = place_ref[0], place_ref[1]
    half = prev_ref.shape[1]
    columns = tile_columns(left_ref.shape[1])
    messages = 2 * len(columns)
    groups = half // TILE
    low = low_lanes()
    for chunk in range(left_ref.shape[0] // (2 * half)):
        for out_ref, part in ((kept_ref, core), (sent_ref, 1 - core)):
            for group in range(groups):
                first = pl.multiple_of(2 * half * chunk + half * part + TILE * group, TILE)
                for t, lanes in enumerate(columns):
                    left = left_ref[pl.ds(first, TILE), lanes] * weight
                    right = right_ref[pl.ds(first, TILE), lanes] * weight
                    number = (chunk * groups + group) * messages + 2 * t
                    out_ref[number], out_ref[number + 1] = pair_kinds(low, left, right)
    for group in range(groups):
        rows = pl.ds(TILE * group, TILE)
        for t, lanes in enumerate(columns):
            pair = pair_kinds(
                low, HISTORY * prev_ref[0, rows, lanes], HISTORY * prev_ref[1, rows, lanes]
            )
            number = (y * groups + group) * messages + 2 * t
            kept_ref[number] += pair[0]
            kept_ref[number + 1] += pair[1]


def split_halves(place, left, right, prev, weight):
    messages = left.shape[0] * left.shape[1] // (TILE * LANES)

    def kernel(*refs):
        halves_kernel(weight, *refs)

    return pl.pallas_call(
        kernel,
        out_shape=[shape_of(messages, TILE, LANES)] * 2,
        in_specs=[SMEM, VMEM, VMEM, VMEM],
        out_specs=[VMEM] * 2,
    )(place, left, right, prev)


def message_kernel(place_ref, kept_ref, got_ref, warm_ref, out_ref):
    y = place_ref[0]
    columns = tile_columns(warm_ref.shape[2])
    workers = kept_ref.shape[0] // TILE
    for number in range(kept_ref.shape[0]):
        chunk, worker = divmod(number, workers)
        first = (TILE + 1) * number
        out_ref[pl.ds(first, TILE), :] = kept_ref[number] + got_ref[number]
        slot = (y + chunk) % 2
        row = (chunk // 2) * (workers // len(columns)) + worker // len(columns)
        out_ref[pl.ds(first + TILE, 1), :] = warm_ref[
            slot, pl.ds(row, 1), columns[worker % len(columns)]
        ]


def build_messages(place, kept, got, warm):
    return pl.pallas_call(
        message_kernel,
        out_shape=shape_of(kept.shape[0] * (TILE + 1), LANES),
        in_specs=[SMEM, VMEM, VMEM, VMEM],
        out_specs=VMEM,
    )(place, kept, got, warm)


def deliver_kernel(place_ref, block_ref, owner_ref, slot_ref, in_ref, out_ref, sum_ref, row_ref):
    y = place_ref[0]
    workers = block_ref.shape[0]
    chunks = in_ref.shape[0] // (workers * (TILE + 1))
    stride = workers * (TILE + 1)
    low = low_lanes()
    upper = lax.broadcasted_iota(jnp.int32, (TILE, LANES), 0) < TILE // 2
    for worker in range(workers):
        first = (TILE + 1) * worker
        total = in_ref[pl.ds(first, TILE), :]
        for chunk in range(1, chunks):
            total = total + in_ref[pl.ds(first + stride * chunk, TILE), :]
        sum_ref[worker] = total
    for number in range(chunks * workers):
        row_ref[number] = in_ref[pl.ds((TILE + 1) * number + TILE, 1), :]
    for reader in range(workers):
        tile = sum_ref[block_ref[reader]]
        for kind in range(2):
            place = 2 * reader + kind
            parity = (slot_ref[place] + y) % 2
            rows = [
                row_ref[(2 * n + parity) * workers + owner_ref[place]]
                for n in range(chunks // 2)
            ]
            warm = jnp.concatenate(rows + rows, 0)
            warm = jnp.where(upper, turn(warm), warm)
            value = jnp.where(low, tile if kind == 0 else turn(tile), warm)
            for chunk in range(kind, chunks, 2):
                out_ref[chunk * workers + reader] = value


def deliver(place, blocks, owners, slots, messages):
    workers = blocks.shape[0]
    count = messages.shape[0] // (TILE + 1)
    return pl.pallas_call(
        deliver_kernel,
        out_shape=shape_of(count, TILE, LANES),
        in_specs=[SMEM] * 4 + [VMEM],
        out_specs=VMEM,
        scratch_shapes=[
            pltpu.VMEM((workers, TILE, LANES), jnp.float32),
            pltpu.VMEM((count, 1, LANES), jnp.float32),
        ],
    )(place, blocks, owners, slots, messages)


def whole_kernel(place_ref, own_ref, other_ref, scaled_ref, warm_ref):
    core, slot = place_ref[1], place_ref[2]
    width = scaled_ref.shape[0]
    columns = tile_columns(width)
    count = len(columns)
    chunks = TILE
    workers = own_ref.shape[0] // TILE // chunks
    share = width // chunks
    half = share // 2
    groups = half // TILE
    low = low_lanes()
    total = jnp.zeros((TILE, LANES), jnp.float32)
    for part in range(2):
        own = core == part

        def read(rows):
            return jnp.where(own, own_ref[rows, :], other_ref[rows, :])

        for chunk in range(chunks):
            for group in range(groups):
                for t, lanes in enumerate(columns):
                    number = chunk * workers + (group * count + t) * 2
                    value = jnp.where(
                        low,
                        read(pl.ds(TILE * number, TILE)),
                        turn(read(pl.ds(TILE * (number + 1), TILE))),
                    )
                    first = share * chunk + half * part + TILE * group
                    scaled_ref[pl.ds(first, TILE), lanes] = value
                    total = total + value * value
            parity = (slot + chunk) % 2
            for t, lanes in enumerate(columns):
                for n in range(chunks // 2):
                    start = TILE * (chunk * workers + t) + n
                    lower = read(pl.ds(start, TILE, stride=TILE * count))
                    higher = read(pl.ds(start + TILE // 2, TILE, stride=TILE * count))
                    first = share * (2 * n + parity) + half * part + TILE * (chunk // 2)
                    first = pl.multiple_of(first, TILE)
                    warm_ref[pl.ds(first, TILE), lanes] = jnp.where(low, turn(lower), higher)
    total = jnp.sum(jnp.sum(total, axis=0, keepdims=True), axis=1, keepdims=True)
    inverse = 1.0 / jnp.sqrt(total + 1e-06)
    row = lax.broadcasted_iota(jnp.int32, (share, width), 0)
    column = lax.broadcasted_iota(jnp.int32, (share, width), 1)
    for first in range(0, width, share):
        diagonal = jnp.where(column == row + first, DAMPING, 0.0)
        scaled_ref[pl.ds(first, share), :] = scaled_ref[pl.ds(first, share), :] * inverse + diagonal


def whole(place, own, other, width):
    return pl.pallas_call(
        whole_kernel,
        out_shape=[shape_of(width, width)] * 2,
        in_specs=[SMEM, VMEM, VMEM],
        out_specs=[VMEM] * 2,
    )(place, own, other)


def local(grad, prev_stats, warm_roots, owner_items, counts, read_shard):
    gradients = grad[:, 0]
    width = gradients.shape[-1]
    y_count = lax.axis_size("y")
    y = lax.axis_index("y")
    core = lax.axis_index("core")
    worker = lax.axis_index(WORKER)
    half = width // y_count // 2
    kind = y % 2
    weight = (1.0 - HISTORY) / (y_count * 2 * gradients.shape[0])

    ids = jnp.arange(read_shard.shape[0], dtype=jnp.int32)
    blocks = jnp.sum(jnp.where(read_shard[None, :] == ids[:, None], ids[None, :], 0), 1)
    items = (2 * blocks[:, None] + jnp.arange(2, dtype=jnp.int32)).reshape(-1)
    matches = owner_items[None] == items[:, None, None]
    owners = jnp.sum(jnp.where(matches, ids[None, :, None], 0), (1, 2))
    slots = jnp.sum(jnp.where(matches, jnp.arange(2, dtype=jnp.int32), 0), (1, 2))
    place = jnp.stack([y, core, slots[2 * worker + kind]])
    iterations = counts[2 * blocks[worker] + kind]

    left = jnp.einsum("mik,mjk->ij", gradients, gradients, preferred_element_type=jnp.float32)
    right = jnp.einsum("mki,mkj->ij", gradients, gradients, preferred_element_type=jnp.float32)
    kept, sent = split_halves(place, left, right, prev_stats[0], weight)
    got = lax.ppermute(sent, "core", SWAP)
    messages = build_messages(place, kept, got, warm_roots[0])
    peers = kept.shape[0]
    arrived = lax.all_to_all(messages.reshape(peers, 1, -1), PLANE, 0, 0, tiled=True)

    tiles = deliver(place, blocks, owners, slots, arrived.reshape(messages.shape))
    own = lax.all_to_all(tiles, PLANE, 0, 0, tiled=True)
    other = lax.ppermute(own, "core", SWAP)
    scaled, warm_start = whole(
        place, own.reshape(-1, LANES), other.reshape(-1, LANES), width
    )

    squared = dot(warm_start, warm_start)
    fourth = dot(squared, squared)
    identity = jnp.eye(width, dtype=jnp.float32)
    coupled = dot(fourth, scaled)
    factor = (5.0 * identity - coupled) * 0.25
    high = lax.Precision.HIGH
    warm_rows = lax.dynamic_slice(
        warm_start.reshape(y_count, 2, half, width), (y - kind, core, 0, 0), (2, 1, half, width)
    )
    estimate = dot(warm_rows.reshape(2 * half, width), factor, high)

    def second_step():
        factor_sq = dot(factor, factor, high)
        coupled_next = dot(factor_sq, dot(factor_sq, coupled, high), high)
        factor_next = (5.0 * identity - coupled_next) * 0.25
        return dot(estimate, factor_next, high)

    root_rows = lax.cond(iterations >= 2, second_step, lambda: estimate)
    first = kind == 0
    root_sent = jnp.where(first, root_rows[half:], root_rows[:half])
    root_kept = jnp.where(first, root_rows[:half], root_rows[half:])
    root_got = lax.ppermute(root_sent, "y", [(i, i ^ 1) for i in range(y_count)])
    result = jnp.where(
        first, jnp.stack([root_kept, root_got]), jnp.stack([root_got, root_kept])
    )
    return result[None]


def solution(mesh):
    cores = 2
    x_count = 4
    dp_count, worker_count = mesh.devices.shape
    chips = Mesh(
        mesh.devices.reshape(dp_count // cores, cores, x_count, worker_count // x_count),
        ("y", "core", "x", "z"),
    )
    dp = ("y", "core")
    return jax.shard_map(
        local,
        mesh=chips,
        in_specs=(
            P(dp, WORKER, None, None),
            P(WORKER, None, dp, None),
            P(WORKER, None, dp, None),
            P(),
            P(),
            P(),
        ),
        out_specs=P(WORKER, None, dp, None),
        check_vma=False,
    )
```

time: 171 us -> 152 us (0.89)
  the two profiles are of different devices: /device:TPU:77 before, /device:TPU:1 now
where the time goes in v4:
time: 152 us
  blocking collectives  89 us (59%)
  starting transfers between devices  16.4 us (11%)
  matrix products  15 us (10%)
  Pallas kernels  14.5 us (10%)
  waiting for transfers between devices  6.16 us (4%)
  local copies, waits for them, and re-layouts  5.37 us (4%)
  other arithmetic  3.8 us (2%)
    all_to_all x1, blocking collectives, local(): lax.all_to_all(messages.reshape(peers, 1, -1), PLANE, 0, 0, tiled=True)  50.5 us
    all_to_all x1, blocking collectives, local(): own = lax.all_to_all(tiles, PLANE, 0, 0, tiled=True)  38.6 us
    dot_general x8, matrix products, dot(): jnp.dot(first, second, precision=precision, preferred_element_type=jnp.fl...  11 us
    ppermute x1, starting transfers between devices, local(): got = lax.ppermute(sent, 'core', SWAP)  8.77 us
    ppermute x1, starting transfers between devices, local(): other = lax.ppermute(own, 'core', SWAP)  5.7 us
    pallas_call x1, Pallas kernels, whole(): pl.pallas_call(whole_kernel, out_shape=[shape_of(width, width)] * 2, in_s...  5.47 us
    ppermute x1, waiting for transfers between devices, local(): lax.ppermute(root_sent, 'y', [(i, i ^ 1) for i in range(y_count)])  3.68 us
    pallas_call x1, Pallas kernels, split_halves(): pl.pallas_call(kernel, out_shape=[shape_of(messages, TILE, LANES)] * 2, i...  3.5 us
  transfers between devices with their start and end apart: 3, of which 2 were waited for; matrix products, arithmetic and copies ran while one was open for 1% of the time, Pallas kernels for 0%

profile of v4, /device:TPU:1, one launch (start us, length us, event | category | flops | bytes accessed | tf_op | source)
XLA Modules:
  0.0 151.7 jit_solution(2707464392694582723)
XLA Ops:
  0.0 0.0 copy-start
  0.0 1.4 copy-done
  1.4 2.0 %fusion.5.refs_1_ = f32[512,512]{1,0:T(8,128)} fusion(bf16[3,1,512,512]{3,2,1,0:T(8,128)(2,1)S(1)} %copy-done), kind=kOutput, calls=%fused_computation.7 | convolution fusion | flops 805306368 | bytes 2621440 | tf_op jit(solution)/shard_map/mik,mjk->ij/dot_general | solution.py:235
  3.4 0.0 copy-start.9
  3.4 0.0 copy-start.6
  3.4 2.0 %fusion.8.refs_2_ = f32[512,512]{1,0:T(8,128)} fusion(bf16[3,1,512,512]{3,2,1,0:T(8,128)(2,1)S(1)} %copy-done), kind=kOutput, calls=%fused_computation.8 | convolution fusion | flops 805306368 | bytes 2621440 | tf_op jit(solution)/shard_map/mki,mkj->ij/dot_general | solution.py:236
  5.4 0.0 copy-done.9
  5.4 0.1 select_reduce_fusion.block_ref
  5.5 0.0 copy-start.7
  5.5 0.1 iota_add_fusion
  5.6 0.1 add.56
  5.7 0.0 copy-done.6
  5.8 0.6 fusion.13
  6.3 0.0 copy-start.5
  6.4 0.6 dynamic_slice.14
  7.0 1.2 pad_add_fusion.refs_0_.place_ref
  8.2 3.5 %shard_map.64 = (f32[256,8,128]{2,1,0:T(8,128)}, f32[256,8,128]{2,1,0:T(8,128)}) custom-call(s32[3]{0:T(128)} %pad_add_fusion.refs_0_.place_ref, f32[512,512]{1,0:T(8,128)} %fusion.5.refs_1_, f32[512,512]{1,0:T(8,128)} %fusion.8.refs_2_, f32[2,32,512]{2,1,0:T(8,128)} %bitcast.49), custom_call_target="tpu_custom_call" | custom-call | tf_op jit(solution)/shard_map/pallas_call | solution.py:80
  11.7 8.8 %collective-permute-start = (f32[256,8,128]{2,1,0:T(8,128)}, f32[256,8,128]{2,1,0:T(8,128)S(1)}, u32[]{:S(2)}, u32[]{:S(2)}) collective-permute-start(f32[256,8,128]{2,1,0:T(8,128)} %get-tuple-element.38), channel_id=1, source_target_pairs={{0,32},{32,0},{1,33},{33,1},{2,34},{34,2},{3,35},{35,3},{4,36},{36... | collective-permute-start | bytes 3145736 | tf_op jit(solution)/shard_map/ppermute | solution.py:238
  20.5 2.5 %collective-permute-done.got_ref = f32[256,8,128]{2,1,0:T(8,128)S(1)} collective-permute-done((f32[256,8,128]{2,1,0:T(8,128)}, f32[256,8,128]{2,1,0:T(8,128)S(1)}, u32[]{:S(2)}, u32[]{:S(2)}) %collective-permute-start) | collective-permute-done | bytes 1048608 | tf_op jit(solution)/shard_map/ppermute | solution.py:238
  23.0 0.0 copy-start.3
  23.0 1.0 copy-done.3
  24.0 2.7 %shard_map.65 = f32[2304,128]{1,0:T(8,128)} custom-call(s32[3]{0:T(128)} %pad_add_fusion.refs_0_.place_ref, f32[256,8,128]{2,1,0:T(8,128)} %get-tuple-element.37.kept_ref, f32[256,8,128]{2,1,0:T(8,128)} %copy-done.3, f32[2,32,512]{2,1,0:T(8,128)} %bitcast.50), custom_call_target="tpu_custom_call" | custom-call | tf_op jit(solution)/shard_map/pallas_call | solution.py:104
  26.7 0.0 copy-done.7
  26.7 0.0 copy-done.5
  26.7 50.5 %all_to_all.10 = f32[256,1,1152]{2,1,0:T(1,128)} all-to-all(f32[256,1,1152]{2,1,0:T(1,128)} %bitcast.47), channel_id=1, replica_groups=mesh['y'=8,'core'=2,'x'=4,'z'=8] {'y','x','z'}, dimensions={0} | all-to-all | bytes 2359296 | tf_op jit(solution)/shard_map/all_to_all | solution.py:241
  77.2 2.7 %shard_map.66 = f32[256,8,128]{2,1,0:T(8,128)} custom-call(s32[3]{0:T(128)} %pad_add_fusion.refs_0_.place_ref, s32[32]{0:T(128)} %copy-done.7, s32[64]{0:T(128)} %get-tuple-element.44.owner_ref, s32[64]{0:T(128)} %copy-done.5, f32[2304,128]{1,0:T(8,128)} %bitcast.46), custom_call_target="tpu_custom_call" | custom-call | tf_op jit(solution)/shard_map/pallas_call | solution.py:146
  79.9 0.0 copy-start.8
  79.9 0.0 copy-start.10
  79.9 38.6 %all_to_all.11 = f32[256,8,128]{2,1,0:T(8,128)S(1)} all-to-all(f32[256,8,128]{2,1,0:T(8,128)} %shard_map.66), channel_id=1, replica_groups=mesh['y'=8,'core'=2,'x'=4,'z'=8] {'y','x','z'}, dimensions={0} | all-to-all | bytes 2097152 | tf_op jit(solution)/shard_map/all_to_all | solution.py:244
  118.5 0.0 copy-start.1
  118.5 5.7 %collective-permute-start.1 = (f32[256,8,128]{2,1,0:T(8,128)S(1)}, f32[256,8,128]{2,1,0:T(8,128)}, u32[]{:S(2)}, u32[]{:S(2)}) collective-permute-start(f32[256,8,128]{2,1,0:T(8,128)S(1)} %all_to_all.11), channel_id=1, source_target_pairs={{0,32},{32,0},{1,33},{33,1},{2,34},{34,2},{3,35},{35,3},{4,36},{36... | collective-permute-start | bytes 3145736 | tf_op jit(solution)/shard_map/ppermute | solution.py:245
  124.2 0.0 copy-done.8
  124.2 0.6 dynamic_slice.12
  125.5 0.0 copy-done.10
  125.5 0.6 dynamic_slice.13
  126.7 1.1 fusion.11
  127.8 0.0 collective-permute-done.1
  127.8 0.0 copy-done.1
  127.8 5.5 %shard_map.67 = (f32[512,512]{1,0:T(8,128)}, f32[512,512]{1,0:T(8,128)}) custom-call(s32[3]{0:T(128)} %pad_add_fusion.refs_0_.place_ref, f32[2048,128]{1,0:T(8,128)} %bitcast.48, f32[2048,128]{1,0:T(8,128)} %bitcast.13.other_ref), custom_call_target="tpu_custom_call" | custom-call | tf_op jit(solution)/shard_map/pallas_call | solution.py:207
  133.3 3.4 %fusion.17 = f32[512,512]{1,0:T(8,128)S(1)} fusion(f32[512,512]{1,0:T(8,128)} %get-tuple-element.39), kind=kOutput, calls=%fused_computation.28 | convolution fusion | flops 1610612736 | bytes 2097152 | tf_op jit(solution)/shard_map/dot_general | solution.py:21
  136.7 0.0 copy-start.4
  136.7 1.8 %fusion.18 = f32[512,512]{1,0:T(8,128)S(1)} fusion(f32[512,512]{1,0:T(8,128)S(1)} %fusion.17), kind=kOutput, calls=%fused_computation.29 | convolution fusion | flops 1610612736 | bytes 2097152 | tf_op jit(solution)/shard_map/dot_general | solution.py:21
  138.5 0.0 copy-done.4
  138.6 1.9 %subtract_multiply_fusion = (f32[512,512]{1,0:T(8,128)S(1)}, f32[512,512]{1,0:T(8,128)S(1)}) fusion(f32[512,512]{1,0:T(8,128)S(1)} %fusion.18, f32[512,512]{1,0:T(8,128)S(1)} %copy-done.4), kind=kOutput, calls=%fused_computation.9 | convolution fusion | flops 1611661312 | bytes 4194304 | tf_op jit(solution)/shard_map/dot_general | solution.py:21
  140.4 0.0 copy-start.2
  140.4 1.0 constant_dynamic-slice_fusion
  141.4 0.5 fusion.14
  141.9 0.0 copy-done.2
  141.9 3.5 %conditional.1 = (f32[64,512]{1,0:T(8,128)S(1)}) conditional(s32[]{:T(128)} %bitcast.2, f32[64,512]{1,0:T(8,128)S(1)} %fusion.14, (f32[512,512]{1,0:T(8,128)S(1)}, f32[512,512]{1,0:T(8,128)S(1)}, f32[512,512]{1,0:T(8,128)S(1)}, f32[64,512]{1,0:T(8,128)S(1)}) %tuple.29), branch_computations={%region_3.4_spmd, %region_4.5_spmd} | conditional | flops 2517368832 | bytes 11010056 | solution.py:267
  141.9 1.0 fusion.15
  143.0 1.0 fusion.16
  144.0 1.0 fusion
  145.0 0.4 convolution_bitcast_fusion
  145.5 1.9 %collective-permute-start.2 = (f32[32,512]{1,0:T(8,128)S(1)}, f32[32,512]{1,0:T(8,128)S(1)}, u32[]{:S(2)}, u32[]{:S(2)}) collective-permute-start(f32[32,512]{1,0:T(8,128)S(1)} %get-tuple-element.47), channel_id=1, source_target_pairs={{0,64},{64,0},{128,192},{192,128},{256,320},{320,256},{384,448},{4... | collective-permute-start | bytes 196616 | tf_op jit(solution)/shard_map/ppermute | solution.py:271
  147.4 3.7 %collective-permute-done.2 = f32[32,512]{1,0:T(8,128)S(1)} collective-permute-done((f32[32,512]{1,0:T(8,128)S(1)}, f32[32,512]{1,0:T(8,128)S(1)}, u32[]{:S(2)}, u32[]{:S(2)}) %collective-permute-start.2) | collective-permute-done | bytes 65568 | tf_op jit(solution)/shard_map/ppermute | solution.py:271
  151.1 0.7 maximum_select_fusion
  (3 shorter events, 0.0 us)
Async XLA Ops:
  0.0 1.4 copy-start
  3.4 2.0 %copy-start.9 = (s32[32]{0:T(128)S(1)}, s32[32]{0:T(128)}, u32[]{:S(2)}) copy-start(s32[32]{0:T(128)} %param.13) | copy-start | bytes 388
  3.4 2.3 %copy-start.6 = (s32[32,2]{0,1:T(2,128)S(1)}, s32[32,2]{0,1:T(2,128)}, u32[]{:S(2)}) copy-start(s32[32,2]{0,1:T(2,128)} %param.11) | copy-start | bytes 772
  5.5 21.2 %copy-start.7 = (s32[32]{0:T(128)}, s32[32]{0:T(128)S(1)}, u32[]{:S(2)}) copy-start(s32[32]{0:T(128)S(1)} %select_reduce_fusion.block_ref) | copy-start | bytes 388
  6.3 20.4 %copy-start.5 = (s32[64]{0:T(128)}, s32[64]{0:T(128)S(1)}, u32[]{:S(2)}) copy-start(s32[64]{0:T(128)S(1)} %get-tuple-element.45.slot_ref) | copy-start | bytes 772
  11.7 11.2 %collective-permute-start = (f32[256,8,128]{2,1,0:T(8,128)}, f32[256,8,128]{2,1,0:T(8,128)S(1)}, u32[]{:S(2)}, u32[]{:S(2)}) collective-permute-start(f32[256,8,128]{2,1,0:T(8,128)} %get-tuple-element.38), channel_id=1, source_target_pairs={{0,32},{32,0},{1,33},{33,1},{2,34},{34,2},{3,35},{35,3},{4,36},{36... | collective-permute-start | bytes 3145736 | tf_op jit(solution)/shard_map/ppermute | solution.py:238
  23.0 1.0 copy-start.3
  79.9 44.3 %copy-start.8 = (s32[32]{0:T(128)S(1)}, s32[32]{0:T(128)}, u32[]{:S(2)}) copy-start(s32[32]{0:T(128)} %copy-done.7) | copy-start | bytes 388
  79.9 45.6 %copy-start.10 = (s32[64]{0:T(128)S(1)}, s32[64]{0:T(128)}, u32[]{:S(2)}) copy-start(s32[64]{0:T(128)} %param.12) | copy-start | bytes 772
  118.5 9.3 %copy-start.1 = (f32[256,8,128]{2,1,0:T(8,128)}, f32[256,8,128]{2,1,0:T(8,128)S(1)}, u32[]{:S(2)}) copy-start(f32[256,8,128]{2,1,0:T(8,128)S(1)} %all_to_all.11) | copy-start | bytes 3145732
  118.5 9.3 %collective-permute-start.1 = (f32[256,8,128]{2,1,0:T(8,128)S(1)}, f32[256,8,128]{2,1,0:T(8,128)}, u32[]{:S(2)}, u32[]{:S(2)}) collective-permute-start(f32[256,8,128]{2,1,0:T(8,128)S(1)} %all_to_all.11), channel_id=1, source_target_pairs={{0,32},{32,0},{1,33},{33,1},{2,34},{34,2},{3,35},{35,3},{4,36},{36... | collective-permute-start | bytes 3145736 | tf_op jit(solution)/shard_map/ppermute | solution.py:245
  136.7 1.9 %copy-start.4 = (f32[512,512]{1,0:T(8,128)S(1)}, f32[512,512]{1,0:T(8,128)}, u32[]{:S(2)}) copy-start(f32[512,512]{1,0:T(8,128)} %get-tuple-element.40) | copy-start | bytes 3145732
  140.4 1.5 copy-start.2
  145.5 5.6 %collective-permute-start.2 = (f32[32,512]{1,0:T(8,128)S(1)}, f32[32,512]{1,0:T(8,128)S(1)}, u32[]{:S(2)}, u32[]{:S(2)}) collective-permute-start(f32[32,512]{1,0:T(8,128)S(1)} %get-tuple-element.47), channel_id=1, source_target_pairs={{0,64},{64,0},{128,192},{192,128},{256,320},{320,256},{384,448},{4... | collective-permute-start | bytes 196616 | tf_op jit(solution)/shard_map/ppermute | solution.py:271

commit v5 on v4

v5 whole, which is shorter than its diff:
```python
import jax
import jax.numpy as jnp
from jax import lax
from jax.experimental import pallas as pl
from jax.experimental.pallas import tpu as pltpu
from jax.sharding import Mesh, PartitionSpec as P

HISTORY = 0.5
DAMPING = 0.001
WORKER = ("x", "z")
PLANE = ("yh", "yl", "x", "z")
LINE = ("yl", "x", "z")
SWAP = [(0, 1), (1, 0)]
LANES = 128
TILE = 8
EXTRA = 2
SMEM = pl.BlockSpec(memory_space=pltpu.SMEM)
VMEM = pl.BlockSpec(memory_space=pltpu.VMEM)
PARAMS = pltpu.CompilerParams(vmem_limit_bytes=12 * 1024 * 1024)


def dot(first, second, precision=lax.Precision.HIGHEST):
    return jnp.dot(first, second, precision=precision, preferred_element_type=jnp.float32)


def shape_of(*shape):
    return jax.ShapeDtypeStruct(shape, jnp.float32)


def tile_columns(width):
    return [pl.ds(LANES * t, LANES) for t in range(width // LANES)]


def halves_kernel(weight, place_ref, left_ref, right_ref, prev_ref, kept_ref, sent_ref):
    y, core = place_ref[0], place_ref[1]
    width = left_ref.shape[1]
    half = prev_ref.shape[1]
    groups = half // TILE
    columns = tile_columns(width)
    chunks = left_ref.shape[0] // (2 * half)
    count = chunks * groups * len(columns)
    for out_ref, part in ((kept_ref, core), (sent_ref, 1 - core)):
        for chunk in range(chunks):
            for group in range(groups):
                first = pl.multiple_of(2 * half * chunk + half * part + TILE * group, TILE)
                for t, lanes in enumerate(columns):
                    number = (chunk * groups + group) * len(columns) + t
                    out_ref[number] = left_ref[pl.ds(first, TILE), lanes] * weight
                    out_ref[count + number] = right_ref[pl.ds(first, TILE), lanes] * weight
    for kind in range(2):
        for group in range(groups):
            for t, lanes in enumerate(columns):
                number = (y * groups + group) * len(columns) + t + count * kind
                kept_ref[number] += HISTORY * prev_ref[kind, pl.ds(TILE * group, TILE), lanes]


def split_halves(place, left, right, prev, weight):
    messages = left.shape[0] * left.shape[1] // (TILE * LANES)

    def kernel(*refs):
        halves_kernel(weight, *refs)

    return pl.pallas_call(
        kernel,
        out_shape=[shape_of(messages, TILE, LANES)] * 2,
        in_specs=[SMEM, VMEM, VMEM, VMEM],
        out_specs=[VMEM] * 2,
        compiler_params=PARAMS,
    )(place, left, right, prev)


def message_kernel(kept_ref, got_ref, warm_ref, out_ref):
    _, rows, width = warm_ref.shape
    columns = tile_columns(width)
    size = TILE + EXTRA
    for number in range(kept_ref.shape[0]):
        out_ref[pl.ds(size * number, TILE), :] = kept_ref[number] + got_ref[number]
    for kind in range(2):
        for slot in range(EXTRA):
            for t, lanes in enumerate(columns):
                for first in range(0, rows, TILE):
                    number = (kind * rows + first) * len(columns) + t
                    out_ref[
                        pl.ds(size * number + TILE + slot, TILE, stride=size * len(columns)), :
                    ] = warm_ref[slot, pl.ds(first, TILE), lanes]


def build_messages(kept, got, warm):
    return pl.pallas_call(
        message_kernel,
        out_shape=shape_of(kept.shape[0] * (TILE + EXTRA), LANES),
        in_specs=[VMEM] * 3,
        out_specs=VMEM,
        compiler_params=PARAMS,
    )(kept, got, warm)


def deliver_kernel(kind_ref, block_ref, owner_ref, slot_ref, in_ref, out_ref, dense_ref, sum_ref, warm_ref):
    kind = kind_ref[0]
    workers = block_ref.shape[0]
    size = TILE + EXTRA
    stride = workers * size
    chunks = in_ref.shape[0] // stride
    for first in range(0, stride, TILE):
        total = in_ref[pl.ds(first, TILE), :]
        for chunk in range(1, chunks):
            total = total + in_ref[pl.ds(first + stride * chunk, TILE), :]
        dense_ref[pl.ds(first, TILE), :] = total
    for worker in range(workers):
        sum_ref[worker] = dense_ref[pl.ds(size * worker, TILE), :]
        for slot in range(EXTRA):
            first = size * worker + TILE + slot
            warm_ref[EXTRA * worker + slot] = in_ref[pl.ds(first, chunks, stride=stride), :]
    for reader in range(workers):
        place = 2 * reader + kind
        sums = sum_ref[block_ref[reader]]
        warm = warm_ref[EXTRA * owner_ref[place] + slot_ref[place]]
        for number in range(reader, out_ref.shape[0], workers):
            out_ref[number, pl.ds(0, TILE), :] = sums
            out_ref[number, pl.ds(TILE, TILE), :] = warm


def deliver(kind, blocks, owners, slots, messages):
    workers = blocks.shape[0]
    rows = messages.shape[0]
    return pl.pallas_call(
        deliver_kernel,
        out_shape=shape_of(rows // (TILE + EXTRA) // 2, 2 * TILE, LANES),
        in_specs=[SMEM] * 4 + [VMEM],
        out_specs=VMEM,
        scratch_shapes=[
            pltpu.VMEM((workers * (TILE + EXTRA), LANES), jnp.float32),
            pltpu.VMEM((workers, TILE, LANES), jnp.float32),
            pltpu.VMEM((workers * EXTRA, TILE, LANES), jnp.float32),
        ],
        compiler_params=PARAMS,
    )(kind, blocks, owners, slots, messages)


def whole_kernel(core_ref, own_ref, other_ref, scaled_ref, warm_ref):
    width = scaled_ref.shape[0]
    columns = tile_columns(width)
    chunks = TILE
    share = width // chunks
    half = share // 2
    groups = half // TILE

    def assemble(*halves):
        total = jnp.zeros((TILE, LANES), jnp.float32)
        for part, in_ref in enumerate(halves):
            for chunk in range(chunks):
                for group in range(groups):
                    rows = pl.ds(share * chunk + half * part + TILE * group, TILE)
                    for t, lanes in enumerate(columns):
                        number = (chunk * groups + group) * len(columns) + t
                        value = in_ref[pl.ds(2 * TILE * number, TILE), :]
                        scaled_ref[rows, lanes] = value
                        total = total + value * value
                        first = 2 * TILE * (TILE * group * len(columns) + t) + TILE + chunk
                        warm_ref[rows, lanes] = in_ref[
                            pl.ds(first, TILE, stride=2 * TILE * len(columns)), :
                        ]
        total = jnp.sum(jnp.sum(total, axis=0, keepdims=True), axis=1, keepdims=True)
        inverse = 1.0 / jnp.sqrt(total + 1e-06)
        row = lax.broadcasted_iota(jnp.int32, (share, width), 0)
        column = lax.broadcasted_iota(jnp.int32, (share, width), 1)
        for first in range(0, width, share):
            diagonal = jnp.where(column == row + first, DAMPING, 0.0)
            rows = pl.ds(first, share)
            scaled_ref[rows, :] = scaled_ref[rows, :] * inverse + diagonal

    @pl.when(core_ref[0] == 0)
    def _():
        assemble(own_ref, other_ref)

    @pl.when(core_ref[0] != 0)
    def _():
        assemble(other_ref, own_ref)


def whole(core, own, other, width):
    return pl.pallas_call(
        whole_kernel,
        out_shape=[shape_of(width, width)] * 2,
        in_specs=[SMEM, VMEM, VMEM],
        out_specs=[VMEM] * 2,
        compiler_params=PARAMS,
    )(core, own, other)


def local(grad, prev_stats, warm_roots, owner_items, counts, read_shard):
    gradients = grad[:, 0]
    width = gradients.shape[-1]
    kinds, lines = lax.axis_size("yh"), lax.axis_size("yl")
    y_count = kinds * lines
    kind = lax.axis_index("yh")
    y = kind * lines + lax.axis_index("yl")
    core = lax.axis_index("core")
    worker = lax.axis_index(WORKER)
    half = width // y_count // 2
    weight = (1.0 - HISTORY) / (y_count * 2 * gradients.shape[0])

    left = jnp.einsum("mik,mjk->ij", gradients, gradients, preferred_element_type=jnp.float32)
    right = jnp.einsum("mki,mkj->ij", gradients, gradients, preferred_element_type=jnp.float32)
    kept, sent = split_halves(jnp.stack([y, core]), left, right, prev_stats[0], weight)
    got = lax.ppermute(sent, "core", SWAP)
    messages = build_messages(kept, got, warm_roots[0])
    peers = kept.shape[0]
    arrived = lax.all_to_all(messages.reshape(peers, 1, -1), PLANE, 0, 0, tiled=True)

    ids = jnp.arange(read_shard.shape[0], dtype=jnp.int32)
    blocks = jnp.sum(jnp.where(read_shard[None, :] == ids[:, None], ids[None, :], 0), 1)
    items = (2 * blocks[:, None] + jnp.arange(2, dtype=jnp.int32)).reshape(-1)
    matches = owner_items[None] == items[:, None, None]
    owners = jnp.sum(jnp.where(matches, ids[None, :, None], 0), (1, 2))
    slots = jnp.sum(jnp.where(matches, jnp.arange(2, dtype=jnp.int32), 0), (1, 2))
    iterations = counts[2 * blocks[worker] + kind]

    tiles = deliver(
        kind.reshape(1), blocks, owners, slots, arrived.reshape(messages.shape)
    )
    own = lax.all_to_all(tiles, LINE, 0, 0, tiled=True)
    other = lax.ppermute(own, "core", SWAP)
    scaled, warm_start = whole(
        core.reshape(1), own.reshape(-1, LANES), other.reshape(-1, LANES), width
    )

    squared = dot(warm_start, warm_start)
    fourth = dot(squared, squared)
    identity = jnp.eye(width, dtype=jnp.float32)
    coupled = dot(fourth, scaled)
    factor = (5.0 * identity - coupled) * 0.25
    high = lax.Precision.HIGH
    warm_rows = lax.dynamic_slice(
        warm_start.reshape(kinds, lines, 2, half, width),
        (0, y - kind * lines, core, 0, 0),
        (kinds, 1, 1, half, width),
    )
    estimate = dot(warm_rows.reshape(kinds * half, width), factor, high)

    def second_step():
        factor_sq = dot(factor, factor, high)
        coupled_next = dot(factor_sq, dot(factor_sq, coupled, high), high)
        factor_next = (5.0 * identity - coupled_next) * 0.25
        return dot(estimate, factor_next, high)

    root_rows = lax.cond(iterations >= 2, second_step, lambda: estimate)
    first = kind == 0
    root_sent = jnp.where(first, root_rows[half:], root_rows[:half])
    root_kept = jnp.where(first, root_rows[:half], root_rows[half:])
    root_got = lax.ppermute(root_sent, "yh", SWAP)
    result = jnp.where(
        first, jnp.stack([root_kept, root_got]), jnp.stack([root_got, root_kept])
    )
    return result[None]


def solution(mesh):
    kinds, cores, x_count = 2, 2, 4
    dp_count, worker_count = mesh.devices.shape
    chips = Mesh(
        mesh.devices.reshape(
            kinds, dp_count // (kinds * cores), cores, x_count, worker_count // x_count
        ),
        ("yh", "yl", "core", "x", "z"),
    )
    dp = ("yh", "yl", "core")
    return jax.shard_map(
        local,
        mesh=chips,
        in_specs=(
            P(dp, WORKER, None, None),
            P(WORKER, None, dp, None),
            P(WORKER, None, dp, None),
            P(),
            P(),
            P(),
        ),
        out_specs=P(WORKER, None, dp, None),
        check_vma=False,
    )
```

time: 152 us -> 134 us (0.88)
  blocking collectives: 89 us -> 35.4 us
  waiting for transfers between devices: 6.16 us -> 43.3 us
  starting transfers between devices: 16.4 us -> 33.9 us
  Pallas kernels: 14.5 us -> 5.1 us
  matrix products: 15 us -> 9.01 us
  other arithmetic: 3.8 us -> 1.15 us
    all_to_all x2 -> x1, blocking collectives: 89 us -> 35.4 us  [local(): own = lax.all_to_all(tiles, LINE, 0, 0, tiled=True)]
    all_to_all x0 -> x1, waiting for transfers between devices: none -> 35.5 us  [local(): lax.all_to_all(messages.reshape(peers, 1, -1), PLANE, 0, 0, tiled=True)]
    all_to_all x0 -> x1, starting transfers between devices: none -> 17.1 us  [local(): lax.all_to_all(messages.reshape(peers, 1, -1), PLANE, 0, 0, tiled=True)]
    dot_general x8 -> x4, matrix products: 11 us -> 6.02 us  [dot(): jnp.dot(first, second, precision=precision, preferred_element_type=jnp.fl...]
    pallas_call x1, Pallas kernels: 5.47 us -> 2.18 us  [whole(): pl.pallas_call(whole_kernel, out_shape=[shape_of(width, width)] * 2, in_s...]
    pallas_call x1, Pallas kernels: 3.5 us -> 0.83 us  [split_halves(): pl.pallas_call(kernel, out_shape=[shape_of(messages, TILE, LANES)] * 2, i...]
    ppermute x1, starting transfers between devices: 1.92 us -> 3.89 us  [local(): root_got = lax.ppermute(root_sent, 'yh', SWAP)]
    pallas_call x1, Pallas kernels: 2.74 us -> 0.84 us  [deliver(): pl.pallas_call(deliver_kernel, out_shape=shape_of(rows // (TILE + EXTRA)...]
  transfers between devices with their start and end apart: 3 -> 4, of which waited for: 2 -> 3; matrix products, arithmetic and copies ran while one was open for 1% -> 1% of each run, Pallas kernels for 0% -> 0%
where the time goes in v5:
time: 134 us; the launch traced here: 133 us
  waiting for transfers between devices  43.3 us (32%)
  blocking collectives  35.4 us (26%)
  starting transfers between devices  33.9 us (25%)
  matrix products  9.01 us (7%)
  Pallas kernels  5.1 us (4%)
  local copies, waits for them, and re-layouts  3.96 us (3%)
  between operations  1.5 us (1%)
    all_to_all x1, waiting for transfers between devices, local(): lax.all_to_all(messages.reshape(peers, 1, -1), PLANE, 0, 0, tiled=True)  35.5 us
    all_to_all x1, blocking collectives, local(): own = lax.all_to_all(tiles, LINE, 0, 0, tiled=True)  35.4 us
    all_to_all x1, starting transfers between devices, local(): lax.all_to_all(messages.reshape(peers, 1, -1), PLANE, 0, 0, tiled=True)  17.1 us
    ppermute x1, starting transfers between devices, local(): got = lax.ppermute(sent, 'core', SWAP)  8.78 us
    dot_general x4, matrix products, dot(): jnp.dot(first, second, precision=precision, preferred_element_type=jnp.fl...  6.02 us
    ppermute x1, waiting for transfers between devices, local(): root_got = lax.ppermute(root_sent, 'yh', SWAP)  5.46 us
    ppermute x1, starting transfers between devices, local(): other = lax.ppermute(own, 'core', SWAP)  4.12 us
    ppermute x1, starting transfers between devices, local(): root_got = lax.ppermute(root_sent, 'yh', SWAP)  3.89 us
  transfers between devices with their start and end apart: 4, of which 3 were waited for; matrix products, arithmetic and copies ran while one was open for 1% of the time, Pallas kernels for 0%

profile of v5, /device:TPU:1, one launch (start us, length us, event | category | flops | bytes accessed | tf_op | source)
XLA Modules:
  0.0 133.3 jit_solution(3376211132155164208)
XLA Ops:
  0.0 0.0 copy-start
  0.0 1.4 %copy-done = bf16[3,1,512,512]{3,2,1,0:T(8,128)(2,1)S(1)} copy-done((bf16[3,1,512,512]{3,2,1,0:T(8,128)(2,1)S(1)}, bf16[3,1,512,512]{3,2,1,0:T(8,128)(2,1)}, u32[]{:S(2)}) %copy-start) | copy-done | bytes 1572888
  1.4 1.0 fusion.5.refs_1_
  2.4 0.0 copy-start.3
  2.4 0.0 copy-start.2
  2.4 2.0 %fusion.8.refs_2_ = f32[512,512]{1,0:T(8,128)} fusion(bf16[3,1,512,512]{3,2,1,0:T(8,128)(2,1)S(1)} %copy-done), kind=kOutput, calls=%fused_computation.8 | convolution fusion | flops 805306368 | bytes 2621440 | tf_op jit(solution)/shard_map/mki,mkj->ij/dot_general | solution.py:204
  4.4 0.1 pad_add_fusion.refs_0_
  4.5 0.0 copy-done.3
  4.5 0.0 copy-start.1
  4.5 1.2 copy-done.1
  5.7 0.8 shard_map.64
  6.6 8.8 %collective-permute-start = (f32[256,8,128]{2,1,0:T(8,128)S(1)}, f32[256,8,128]{2,1,0:T(8,128)S(1)}, u32[]{:S(2)}, u32[]{:S(2)}) collective-permute-start(f32[256,8,128]{2,1,0:T(8,128)S(1)} %get-tuple-element.38), channel_id=1, source_target_pairs={{0,32},{32,0},{1,33},{33,1},{2,34},{34,2},{3,35},{35,3},{4,36},{36... | collective-permute-start | bytes 3145736 | tf_op jit(solution)/shard_map/ppermute | solution.py:206
  15.4 2.3 %collective-permute-done.got_ref = f32[256,8,128]{2,1,0:T(8,128)S(1)} collective-permute-done((f32[256,8,128]{2,1,0:T(8,128)S(1)}, f32[256,8,128]{2,1,0:T(8,128)S(1)}, u32[]{:S(2)}, u32[]{:S(2)}) %collective-permute-start) | collective-permute-done | bytes 1048608 | tf_op jit(solution)/shard_map/ppermute | solution.py:206
  17.6 0.0 copy-done.2
  17.6 1.3 shard_map.65
  18.9 0.0 copy-start.5
  18.9 0.0 copy-start.4
  18.9 17.1 %all-to-all-start = ((f32[256,1,1280]{2,1,0:T(1,128)}), f32[256,1,1280]{2,1,0:T(1,128)S(1)}, u32[]{:S(2)}, u32[]{:S(2)}) async-start(f32[256,1,1280]{2,1,0:T(1,128)} %bitcast.11), calls=%async_computation | async-start | bytes 2621440 | tf_op jit(solution)/shard_map/all_to_all | solution.py:209
  36.0 0.0 copy-done.5
  36.0 0.1 select_reduce_fusion.block_ref
  36.2 0.1 iota_add_fusion
  36.2 0.1 add.48
  36.3 0.0 copy-done.4
  36.4 0.1 fusion.13
  36.4 35.5 %all-to-all-done = f32[256,1,1280]{2,1,0:T(1,128)S(1)} async-done(((f32[256,1,1280]{2,1,0:T(1,128)}), f32[256,1,1280]{2,1,0:T(1,128)S(1)}, u32[]{:S(2)}, u32[]{:S(2)}) %all-to-all-start) | async-done | bytes 1310752 | tf_op jit(solution)/shard_map/all_to_all | solution.py:209
  72.0 0.8 shard_map.66
  72.8 0.0 copy-start.6
  72.8 35.4 %all_to_all.10 = f32[128,16,128]{2,1,0:T(8,128)S(1)} all-to-all(f32[128,16,128]{2,1,0:T(8,128)S(1)} %shard_map.66), channel_id=1, replica_groups=mesh['yh'=2,'yl'=4,'core'=2,'x'=4,'z'=8] {'yl','x','z'}, dimensions={0} | all-to-all | bytes 2097152 | tf_op jit(solution)/shard_map/all_to_all | solution.py:222
  108.2 4.1 %collective-permute-start.1 = (f32[128,16,128]{2,1,0:T(8,128)S(1)}, f32[128,16,128]{2,1,0:T(8,128)}, u32[]{:S(2)}, u32[]{:S(2)}) collective-permute-start(f32[128,16,128]{2,1,0:T(8,128)S(1)} %all_to_all.10), channel_id=1, source_target_pairs={{0,32},{32,0},{1,33},{33,1},{2,34},{34,2},{3,35},{35,3},{4,36},{36... | collective-permute-start | bytes 3145736 | tf_op jit(solution)/shard_map/ppermute | solution.py:223
  112.4 0.6 dynamic_slice.9
  113.6 0.0 copy-done.6
  113.6 0.6 dynamic_slice.10
  114.8 0.1 fusion.11
  115.0 0.0 collective-permute-done.1
  115.0 2.2 %shard_map.67 = (f32[512,512]{1,0:T(8,128)S(1)}, f32[512,512]{1,0:T(8,128)S(1)}) custom-call(s32[1]{0:T(128)} %bitcast.3.core_ref, f32[2048,128]{1,0:T(8,128)S(1)} %bitcast.48, f32[2048,128]{1,0:T(8,128)} %bitcast.14.other_ref), custom_call_target="tpu_custom_call" | custom-call | tf_op jit(solution)/shard_map/pallas_call | solution.py:182
  117.2 1.8 %fusion.17 = f32[512,512]{1,0:T(8,128)S(1)} fusion(f32[512,512]{1,0:T(8,128)S(1)} %get-tuple-element.39), kind=kOutput, calls=%fused_computation.28 | convolution fusion | flops 1610612736 | bytes 2097152 | tf_op jit(solution)/shard_map/dot_general | solution.py:23
  119.0 1.8 %fusion.18 = f32[512,512]{1,0:T(8,128)S(1)} fusion(f32[512,512]{1,0:T(8,128)S(1)} %fusion.17), kind=kOutput, calls=%fused_computation.29 | convolution fusion | flops 1610612736 | bytes 2097152 | tf_op jit(solution)/shard_map/dot_general | solution.py:23
  120.9 1.9 %subtract_multiply_fusion = (f32[512,512]{1,0:T(8,128)S(1)}, f32[512,512]{1,0:T(8,128)S(1)}) fusion(f32[512,512]{1,0:T(8,128)S(1)} %fusion.18, f32[512,512]{1,0:T(8,128)S(1)} %get-tuple-element.40), kind=kOutput, calls=%fused_computation.9 | convolution fusion | flops 1611661312 | bytes 4194304 | tf_op jit(solution)/shard_map/dot_general | solution.py:23
  122.7 0.5 fusion.14
  123.3 3.9 %collective-permute-start.2 = (f32[32,512]{1,0:T(8,128)S(1)}, f32[32,512]{1,0:T(8,128)S(1)}, u32[]{:S(2)}, u32[]{:S(2)}) collective-permute-start(f32[32,512]{1,0:T(8,128)S(1)} %get-tuple-element.47), channel_id=1, source_target_pairs={{0,256},{256,0},{1,257},{257,1},{2,258},{258,2},{3,259},{259,3},{4... | collective-permute-start | bytes 196616 | tf_op jit(solution)/shard_map/ppermute | solution.py:251
  127.2 5.5 %collective-permute-done.2 = f32[32,512]{1,0:T(8,128)S(1)} collective-permute-done((f32[32,512]{1,0:T(8,128)S(1)}, f32[32,512]{1,0:T(8,128)S(1)}, u32[]{:S(2)}, u32[]{:S(2)}) %collective-permute-start.2) | collective-permute-done | bytes 65568 | tf_op jit(solution)/shard_map/ppermute | solution.py:251
  132.6 0.7 maximum_select_fusion
  (4 shorter events, 0.0 us)
Async XLA Ops:
  0.0 1.4 %copy-start = (bf16[3,1,512,512]{3,2,1,0:T(8,128)(2,1)S(1)}, bf16[3,1,512,512]{3,2,1,0:T(8,128)(2,1)}, u32[]{:S(2)}) copy-start(bf16[3,1,512,512]{3,2,1,0:T(8,128)(2,1)} %param.8) | copy-start | bytes 4718596
  2.4 2.1 %copy-start.3 = (f32[1,2,32,512]{3,2,1,0:T(8,128)S(1)}, f32[1,2,32,512]{3,2,1,0:T(8,128)}, u32[]{:S(2)}) copy-start(f32[1,2,32,512]{3,2,1,0:T(8,128)} %param.9) | copy-start | bytes 393220
  2.4 15.2 %copy-start.2 = (f32[1,2,32,512]{3,2,1,0:T(8,128)S(1)}, f32[1,2,32,512]{3,2,1,0:T(8,128)}, u32[]{:S(2)}) copy-start(f32[1,2,32,512]{3,2,1,0:T(8,128)} %param.10) | copy-start | bytes 393220
  4.5 1.2 copy-start.1
  6.6 11.1 %collective-permute-start = (f32[256,8,128]{2,1,0:T(8,128)S(1)}, f32[256,8,128]{2,1,0:T(8,128)S(1)}, u32[]{:S(2)}, u32[]{:S(2)}) collective-permute-start(f32[256,8,128]{2,1,0:T(8,128)S(1)} %get-tuple-element.38), channel_id=1, source_target_pairs={{0,32},{32,0},{1,33},{33,1},{2,34},{34,2},{3,35},{35,3},{4,36},{36... | collective-permute-start | bytes 3145736 | tf_op jit(solution)/shard_map/ppermute | solution.py:206
  18.9 17.1 %copy-start.5 = (s32[32]{0:T(128)S(1)}, s32[32]{0:T(128)}, u32[]{:S(2)}) copy-start(s32[32]{0:T(128)} %param.13) | copy-start | bytes 388
  18.9 17.5 %copy-start.4 = (s32[32,2]{0,1:T(2,128)S(1)}, s32[32,2]{0,1:T(2,128)}, u32[]{:S(2)}) copy-start(s32[32,2]{0,1:T(2,128)} %param.11) | copy-start | bytes 772
  18.9 53.1 %all-to-all-start = ((f32[256,1,1280]{2,1,0:T(1,128)}), f32[256,1,1280]{2,1,0:T(1,128)S(1)}, u32[]{:S(2)}, u32[]{:S(2)}) async-start(f32[256,1,1280]{2,1,0:T(1,128)} %bitcast.11), calls=%async_computation | async-start | bytes 2621440 | tf_op jit(solution)/shard_map/all_to_all | solution.py:209
  72.8 40.8 %copy-start.6 = (s32[64]{0:T(128)S(1)}, s32[64]{0:T(128)}, u32[]{:S(2)}) copy-start(s32[64]{0:T(128)} %param.12) | copy-start | bytes 772
  108.2 6.8 %collective-permute-start.1 = (f32[128,16,128]{2,1,0:T(8,128)S(1)}, f32[128,16,128]{2,1,0:T(8,128)}, u32[]{:S(2)}, u32[]{:S(2)}) collective-permute-start(f32[128,16,128]{2,1,0:T(8,128)S(1)} %all_to_all.10), channel_id=1, source_target_pairs={{0,32},{32,0},{1,33},{33,1},{2,34},{34,2},{3,35},{35,3},{4,36},{36... | collective-permute-start | bytes 3145736 | tf_op jit(solution)/shard_map/ppermute | solution.py:223
  123.3 9.4 %collective-permute-start.2 = (f32[32,512]{1,0:T(8,128)S(1)}, f32[32,512]{1,0:T(8,128)S(1)}, u32[]{:S(2)}, u32[]{:S(2)}) collective-permute-start(f32[32,512]{1,0:T(8,128)S(1)} %get-tuple-element.47), channel_id=1, source_target_pairs={{0,256},{256,0},{1,257},{257,1},{2,258},{258,2},{3,259},{259,3},{4... | collective-permute-start | bytes 196616 | tf_op jit(solution)/shard_map/ppermute | solution.py:251

commit v6 on v5

--- a/solution.py
+++ b/solution.py
@@ -8,15 +8,15 @@
 HISTORY = 0.5
 DAMPING = 0.001
 WORKER = ("x", "z")
-PLANE = ("yh", "yl", "x", "z")
-LINE = ("yl", "x", "z")
+PLANE = ("x", "z", "yh", "yl")
+LINE = ("x", "z", "yl")
 SWAP = [(0, 1), (1, 0)]
 LANES = 128
 TILE = 8
 EXTRA = 2
 SMEM = pl.BlockSpec(memory_space=pltpu.SMEM)
 VMEM = pl.BlockSpec(memory_space=pltpu.VMEM)
-PARAMS = pltpu.CompilerParams(vmem_limit_bytes=12 * 1024 * 1024)
+PARAMS = pltpu.CompilerParams(vmem_limit_bytes=5 * 1024 * 1024)
 
 
 def dot(first, second, precision=lax.Precision.HIGHEST):
@@ -70,19 +70,22 @@
 
 
 def message_kernel(kept_ref, got_ref, warm_ref, out_ref):
-    _, rows, width = warm_ref.shape
-    columns = tile_columns(width)
+    columns = tile_columns(warm_ref.shape[2])
     size = TILE + EXTRA
+    chunks = TILE
+    workers = kept_ref.shape[0] // chunks
     for number in range(kept_ref.shape[0]):
-        out_ref[pl.ds(size * number, TILE), :] = kept_ref[number] + got_ref[number]
-    for kind in range(2):
+        chunk, worker = divmod(number, workers)
+        first = size * (chunks * worker + chunk)
+        out_ref[pl.ds(first, TILE), :] = kept_ref[number] + got_ref[number]
+    for chunk in range(chunks):
+        rows = pl.ds(TILE * (chunk % (chunks // 2)), TILE)
         for slot in range(EXTRA):
             for t, lanes in enumerate(columns):
-                for first in range(0, rows, TILE):
-                    number = (kind * rows + first) * len(columns) + t
-                    out_ref[
-                        pl.ds(size * number + TILE + slot, TILE, stride=size * len(columns)), :
-                    ] = warm_ref[slot, pl.ds(first, TILE), lanes]
+                first = size * (chunks * t + chunk) + TILE + slot
+                out_ref[
+                    pl.ds(first, TILE, stride=size * chunks * len(columns)), :
+                ] = warm_ref[slot, rows, lanes]
 
 
 def build_messages(kept, got, warm):
@@ -95,27 +98,26 @@
     )(kept, got, warm)
 
 
-def deliver_kernel(kind_ref, block_ref, owner_ref, slot_ref, in_ref, out_ref, dense_ref, sum_ref, warm_ref):
+def deliver_kernel(kind_ref, block_ref, owner_ref, slot_ref, in_ref, out_ref, sum_ref, warm_ref):
     kind = kind_ref[0]
     workers = block_ref.shape[0]
     size = TILE + EXTRA
-    stride = workers * size
-    chunks = in_ref.shape[0] // stride
-    for first in range(0, stride, TILE):
-        total = in_ref[pl.ds(first, TILE), :]
+    chunks = in_ref.shape[0] // (workers * size)
+    copies = out_ref.shape[0] // workers
+    for worker in range(workers):
+        base = size * chunks * worker
+        total = in_ref[pl.ds(base, TILE), :]
         for chunk in range(1, chunks):
-            total = total + in_ref[pl.ds(first + stride * chunk, TILE), :]
-        dense_ref[pl.ds(first, TILE), :] = total
-    for worker in range(workers):
-        sum_ref[worker] = dense_ref[pl.ds(size * worker, TILE), :]
+            total = total + in_ref[pl.ds(base + size * chunk, TILE), :]
+        sum_ref[worker] = total
         for slot in range(EXTRA):
-            first = size * worker + TILE + slot
-            warm_ref[EXTRA * worker + slot] = in_ref[pl.ds(first, chunks, stride=stride), :]
+            first = base + TILE + slot
+            warm_ref[EXTRA * worker + slot] = in_ref[pl.ds(first, chunks, stride=size), :]
     for reader in range(workers):
         place = 2 * reader + kind
         sums = sum_ref[block_ref[reader]]
         warm = warm_ref[EXTRA * owner_ref[place] + slot_ref[place]]
-        for number in range(reader, out_ref.shape[0], workers):
+        for number in range(copies * reader, copies * (reader + 1)):
             out_ref[number, pl.ds(0, TILE), :] = sums
             out_ref[number, pl.ds(TILE, TILE), :] = warm
 
@@ -129,7 +131,6 @@
         in_specs=[SMEM] * 4 + [VMEM],
         out_specs=VMEM,
         scratch_shapes=[
-            pltpu.VMEM((workers * (TILE + EXTRA), LANES), jnp.float32),
             pltpu.VMEM((workers, TILE, LANES), jnp.float32),
             pltpu.VMEM((workers * EXTRA, TILE, LANES), jnp.float32),
         ],
@@ -147,18 +148,22 @@
 
     def assemble(*halves):
         total = jnp.zeros((TILE, LANES), jnp.float32)
+        size = 2 * TILE
+        lines = chunks // 2
         for part, in_ref in enumerate(halves):
             for chunk in range(chunks):
                 for group in range(groups):
                     rows = pl.ds(share * chunk + half * part + TILE * group, TILE)
                     for t, lanes in enumerate(columns):
-                        number = (chunk * groups + group) * len(columns) + t
-                        value = in_ref[pl.ds(2 * TILE * number, TILE), :]
+                        line, worker = divmod(
+                            (chunk * groups + group) * len(columns) + t, TILE * len(columns)
+                        )
+                        value = in_ref[pl.ds(size * (lines * worker + line), TILE), :]
                         scaled_ref[rows, lanes] = value
                         total = total + value * value
-                        first = 2 * TILE * (TILE * group * len(columns) + t) + TILE + chunk
+                        first = size * (lines * t + group) + TILE + chunk
                         warm_ref[rows, lanes] = in_ref[
-                            pl.ds(first, TILE, stride=2 * TILE * len(columns)), :
+                            pl.ds(first, TILE, stride=size * lines * len(columns)), :
                         ]
         total = jnp.sum(jnp.sum(total, axis=0, keepdims=True), axis=1, keepdims=True)
         inverse = 1.0 / jnp.sqrt(total + 1e-06)
@@ -239,10 +244,10 @@
     estimate = dot(warm_rows.reshape(kinds * half, width), factor, high)
 
     def second_step():
-        factor_sq = dot(factor, factor, high)
-        coupled_next = dot(factor_sq, dot(factor_sq, coupled, high), high)
-        factor_next = (5.0 * identity - coupled_next) * 0.25
-        return dot(estimate, factor_next, high)
+        rows = estimate
+        for matrix in (factor, factor, factor, factor, coupled):
+            rows = dot(rows, matrix, high)
+        return (5.0 * estimate - rows) * 0.25
 
     root_rows = lax.cond(iterations >= 2, second_step, lambda: estimate)
     first = kind == 0

time: 134 us -> 138 us (1.030)
  matrix products: 9.01 us -> 11.2 us
  blocking collectives: 35.4 us -> 37.4 us
    dot_general x4 -> x9, matrix products: 6.02 us -> 8.19 us  [dot(): jnp.dot(first, second, precision=precision, preferred_element_type=jnp.fl...]
    all_to_all x1, blocking collectives: 35.4 us -> 37.4 us  [local(): own = lax.all_to_all(tiles, LINE, 0, 0, tiled=True)]
    ppermute x1, waiting for transfers between devices: 5.46 us -> 7.05 us  [local(): root_got = lax.ppermute(root_sent, 'yh', SWAP)]
where the time goes in v6:
time: 138 us
  waiting for transfers between devices  44.1 us (32%)
  blocking collectives  37.4 us (27%)
  starting transfers between devices  33.7 us (24%)
  matrix products  11.2 us (8%)
  Pallas kernels  4.99 us (4%)
  local copies, waits for them, and re-layouts  3.96 us (3%)
  between operations  1.49 us (1%)
    all_to_all x1, blocking collectives, local(): own = lax.all_to_all(tiles, LINE, 0, 0, tiled=True)  37.4 us
    all_to_all x1, waiting for transfers between devices, local(): lax.all_to_all(messages.reshape(peers, 1, -1), PLANE, 0, 0, tiled=True)  34.8 us
    all_to_all x1, starting transfers between devices, local(): lax.all_to_all(messages.reshape(peers, 1, -1), PLANE, 0, 0, tiled=True)  17.1 us
    ppermute x1, starting transfers between devices, local(): got = lax.ppermute(sent, 'core', SWAP)  8.79 us
    dot_general x9, matrix products, dot(): jnp.dot(first, second, precision=precision, preferred_element_type=jnp.fl...  8.19 us
    ppermute x1, waiting for transfers between devices, local(): root_got = lax.ppermute(root_sent, 'yh', SWAP)  7.05 us
    ppermute x1, starting transfers between devices, local(): other = lax.ppermute(own, 'core', SWAP)  4.08 us
    ppermute x1, starting transfers between devices, local(): root_got = lax.ppermute(root_sent, 'yh', SWAP)  3.66 us
  transfers between devices with their start and end apart: 4, of which 3 were waited for; matrix products, arithmetic and copies ran while one was open for 1% of the time, Pallas kernels for 0%

profile of v6, /device:TPU:1, one launch (start us, length us, event | category | flops | bytes accessed | tf_op | source)
XLA Modules:
  0.0 137.9 jit_solution(7326812518372992277)
XLA Ops:
  0.0 0.0 copy-start
  0.0 1.4 %copy-done = bf16[3,1,512,512]{3,2,1,0:T(8,128)(2,1)S(1)} copy-done((bf16[3,1,512,512]{3,2,1,0:T(8,128)(2,1)S(1)}, bf16[3,1,512,512]{3,2,1,0:T(8,128)(2,1)}, u32[]{:S(2)}) %copy-start) | copy-done | bytes 1572888
  1.4 1.0 fusion.8.refs_2_
  2.4 0.0 copy-start.3
  2.4 0.0 copy-start.2
  2.4 2.0 %fusion.5.refs_1_ = f32[512,512]{1,0:T(8,128)} fusion(bf16[3,1,512,512]{3,2,1,0:T(8,128)(2,1)S(1)} %copy-done), kind=kOutput, calls=%fused_computation.6 | convolution fusion | flops 805306368 | bytes 2621440 | tf_op jit(solution)/shard_map/mik,mjk->ij/dot_general | solution.py:208
  4.4 0.1 pad_add_fusion.refs_0_
  4.5 0.0 copy-done.3
  4.5 0.0 copy-start.1
  4.5 1.2 copy-done.1
  5.7 0.8 shard_map.64
  6.5 8.8 %collective-permute-start = (f32[256,8,128]{2,1,0:T(8,128)S(1)}, f32[256,8,128]{2,1,0:T(8,128)S(1)}, u32[]{:S(2)}, u32[]{:S(2)}) collective-permute-start(f32[256,8,128]{2,1,0:T(8,128)S(1)} %get-tuple-element.47), channel_id=1, source_target_pairs={{0,32},{32,0},{1,33},{33,1},{2,34},{34,2},{3,35},{35,3},{4,36},{36... | collective-permute-start | bytes 3145736 | tf_op jit(solution)/shard_map/ppermute | solution.py:211
  15.3 2.3 %collective-permute-done.got_ref = f32[256,8,128]{2,1,0:T(8,128)S(1)} collective-permute-done((f32[256,8,128]{2,1,0:T(8,128)S(1)}, f32[256,8,128]{2,1,0:T(8,128)S(1)}, u32[]{:S(2)}, u32[]{:S(2)}) %collective-permute-start) | collective-permute-done | bytes 1048608 | tf_op jit(solution)/shard_map/ppermute | solution.py:211
  17.6 0.0 copy-done.2
  17.6 1.4 shard_map.65
  18.9 0.0 copy-start.5
  18.9 0.0 copy-start.4
  18.9 17.1 %all-to-all-start = ((f32[256,1,1280]{2,1,0:T(1,128)}), f32[256,1,1280]{2,1,0:T(1,128)S(1)}, u32[]{:S(2)}, u32[]{:S(2)}) async-start(f32[256,1,1280]{2,1,0:T(1,128)} %bitcast.10), calls=%async_computation | async-start | bytes 2621440 | tf_op jit(solution)/shard_map/all_to_all | solution.py:214
  36.1 0.0 copy-done.5
  36.1 0.1 select_reduce_fusion.block_ref
  36.2 0.1 iota_add_fusion
  36.3 0.1 add.48
  36.4 0.0 copy-done.4
  36.4 0.1 fusion.12
  36.5 34.8 %all-to-all-done = f32[256,1,1280]{2,1,0:T(1,128)S(1)} async-done(((f32[256,1,1280]{2,1,0:T(1,128)}), f32[256,1,1280]{2,1,0:T(1,128)S(1)}, u32[]{:S(2)}, u32[]{:S(2)}) %all-to-all-start) | async-done | bytes 1310752 | tf_op jit(solution)/shard_map/all_to_all | solution.py:214
  71.3 0.7 shard_map.66
  72.0 0.0 copy-start.6
  72.0 37.4 %all_to_all.10 = f32[128,16,128]{2,1,0:T(8,128)S(1)} all-to-all(f32[128,16,128]{2,1,0:T(8,128)S(1)} %shard_map.66), channel_id=1, replica_groups=mesh['yh'=2,'yl'=4,'core'=2,'x'=4,'z'=8] {'x','z','yl'}, dimensions={0} | all-to-all | bytes 2097152 | tf_op jit(solution)/shard_map/all_to_all | solution.py:227
  109.4 4.1 %collective-permute-start.1 = (f32[128,16,128]{2,1,0:T(8,128)S(1)}, f32[128,16,128]{2,1,0:T(8,128)}, u32[]{:S(2)}, u32[]{:S(2)}) collective-permute-start(f32[128,16,128]{2,1,0:T(8,128)S(1)} %all_to_all.10), channel_id=1, source_target_pairs={{0,32},{32,0},{1,33},{33,1},{2,34},{34,2},{3,35},{35,3},{4,36},{36... | collective-permute-start | bytes 3145736 | tf_op jit(solution)/shard_map/ppermute | solution.py:228
  113.5 0.6 dynamic_slice.9
  114.8 0.0 copy-done.6
  114.8 0.6 dynamic_slice.10
  116.0 0.0 collective-permute-done.1
  116.0 2.2 %shard_map.67 = (f32[512,512]{1,0:T(8,128)S(1)}, f32[512,512]{1,0:T(8,128)S(1)}) custom-call(s32[1]{0:T(128)} %bitcast.2.core_ref, f32[2048,128]{1,0:T(8,128)S(1)} %bitcast.48, f32[2048,128]{1,0:T(8,128)} %bitcast.13.other_ref), custom_call_target="tpu_custom_call" | custom-call | tf_op jit(solution)/shard_map/pallas_call | solution.py:187
  118.2 1.8 %fusion.18 = f32[512,512]{1,0:T(8,128)S(1)} fusion(f32[512,512]{1,0:T(8,128)S(1)} %get-tuple-element.48), kind=kOutput, calls=%fused_computation.28 | convolution fusion | flops 1610612736 | bytes 2097152 | tf_op jit(solution)/shard_map/dot_general | solution.py:23
  120.1 1.8 %fusion.19 = f32[512,512]{1,0:T(8,128)S(1)} fusion(f32[512,512]{1,0:T(8,128)S(1)} %fusion.18), kind=kOutput, calls=%fused_computation.29 | convolution fusion | flops 1610612736 | bytes 2097152 | tf_op jit(solution)/shard_map/dot_general | solution.py:23
  121.9 1.9 %subtract_multiply_fusion = (f32[512,512]{1,0:T(8,128)S(1)}, f32[512,512]{1,0:T(8,128)S(1)}) fusion(f32[512,512]{1,0:T(8,128)S(1)} %fusion.19, f32[512,512]{1,0:T(8,128)S(1)} %get-tuple-element.49), kind=kOutput, calls=%fused_computation.8 | convolution fusion | flops 1611661312 | bytes 4194304 | tf_op jit(solution)/shard_map/dot_general | solution.py:23
  123.8 0.5 fusion.13
  124.3 2.2 %conditional.1 = (f32[64,512]{1,0:T(8,128)S(1)}) conditional(s32[]{:T(128)} %bitcast.1, f32[64,512]{1,0:T(8,128)S(1)} %fusion.13, (f32[64,512]{1,0:T(8,128)S(1)}, f32[512,512]{1,0:T(8,128)S(1)}, f32[512,512]{1,0:T(8,128)S(1)}) %tuple.29), branch_computations={%region_3.4_spmd, %region_4.5_spmd} | conditional | flops 503414784 | bytes 6684680 | solution.py:252
  124.3 0.4 fusion.14
  124.7 0.4 fusion.15
  125.2 0.4 fusion.16
  125.6 0.4 fusion.17
  126.0 0.4 fusion
  126.5 3.7 %collective-permute-start.2 = (f32[32,512]{1,0:T(8,128)S(1)}, f32[32,512]{1,0:T(8,128)S(1)}, u32[]{:S(2)}, u32[]{:S(2)}) collective-permute-start(f32[32,512]{1,0:T(8,128)S(1)} %get-tuple-element.53), channel_id=1, source_target_pairs={{0,256},{256,0},{1,257},{257,1},{2,258},{258,2},{3,259},{259,3},{4... | collective-permute-start | bytes 196616 | tf_op jit(solution)/shard_map/ppermute | solution.py:256
  130.2 7.0 %collective-permute-done.2 = f32[32,512]{1,0:T(8,128)S(1)} collective-permute-done((f32[32,512]{1,0:T(8,128)S(1)}, f32[32,512]{1,0:T(8,128)S(1)}, u32[]{:S(2)}, u32[]{:S(2)}) %collective-permute-start.2) | collective-permute-done | bytes 65568 | tf_op jit(solution)/shard_map/ppermute | solution.py:256
  137.2 0.7 maximum_select_fusion
  (3 shorter events, 0.0 us)
Async XLA Ops:
  0.0 1.4 %copy-start = (bf16[3,1,512,512]{3,2,1,0:T(8,128)(2,1)S(1)}, bf16[3,1,512,512]{3,2,1,0:T(8,128)(2,1)}, u32[]{:S(2)}) copy-start(bf16[3,1,512,512]{3,2,1,0:T(8,128)(2,1)} %param.8) | copy-start | bytes 4718596
  2.4 2.1 %copy-start.3 = (f32[1,2,32,512]{3,2,1,0:T(8,128)S(1)}, f32[1,2,32,512]{3,2,1,0:T(8,128)}, u32[]{:S(2)}) copy-start(f32[1,2,32,512]{3,2,1,0:T(8,128)} %param.9) | copy-start | bytes 393220
  2.4 15.1 %copy-start.2 = (f32[1,2,32,512]{3,2,1,0:T(8,128)S(1)}, f32[1,2,32,512]{3,2,1,0:T(8,128)}, u32[]{:S(2)}) copy-start(f32[1,2,32,512]{3,2,1,0:T(8,128)} %param.10) | copy-start | bytes 393220
  4.5 1.2 copy-start.1
  6.5 11.1 %collective-permute-start = (f32[256,8,128]{2,1,0:T(8,128)S(1)}, f32[256,8,128]{2,1,0:T(8,128)S(1)}, u32[]{:S(2)}, u32[]{:S(2)}) collective-permute-start(f32[256,8,128]{2,1,0:T(8,128)S(1)} %get-tuple-element.47), channel_id=1, source_target_pairs={{0,32},{32,0},{1,33},{33,1},{2,34},{34,2},{3,35},{35,3},{4,36},{36... | collective-permute-start | bytes 3145736 | tf_op jit(solution)/shard_map/ppermute | solution.py:211
  18.9 17.1 %copy-start.5 = (s32[32]{0:T(128)S(1)}, s32[32]{0:T(128)}, u32[]{:S(2)}) copy-start(s32[32]{0:T(128)} %param.13) | copy-start | bytes 388
  18.9 17.5 %copy-start.4 = (s32[32,2]{0,1:T(2,128)S(1)}, s32[32,2]{0,1:T(2,128)}, u32[]{:S(2)}) copy-start(s32[32,2]{0,1:T(2,128)} %param.11) | copy-start | bytes 772
  18.9 52.4 %all-to-all-start = ((f32[256,1,1280]{2,1,0:T(1,128)}), f32[256,1,1280]{2,1,0:T(1,128)S(1)}, u32[]{:S(2)}, u32[]{:S(2)}) async-start(f32[256,1,1280]{2,1,0:T(1,128)} %bitcast.10), calls=%async_computation | async-start | bytes 2621440 | tf_op jit(solution)/shard_map/all_to_all | solution.py:214
  72.0 42.8 %copy-start.6 = (s32[64]{0:T(128)S(1)}, s32[64]{0:T(128)}, u32[]{:S(2)}) copy-start(s32[64]{0:T(128)} %param.12) | copy-start | bytes 772
  109.4 6.6 %collective-permute-start.1 = (f32[128,16,128]{2,1,0:T(8,128)S(1)}, f32[128,16,128]{2,1,0:T(8,128)}, u32[]{:S(2)}, u32[]{:S(2)}) collective-permute-start(f32[128,16,128]{2,1,0:T(8,128)S(1)} %all_to_all.10), channel_id=1, source_target_pairs={{0,32},{32,0},{1,33},{33,1},{2,34},{34,2},{3,35},{35,3},{4,36},{36... | collective-permute-start | bytes 3145736 | tf_op jit(solution)/shard_map/ppermute | solution.py:228
  126.5 10.7 %collective-permute-start.2 = (f32[32,512]{1,0:T(8,128)S(1)}, f32[32,512]{1,0:T(8,128)S(1)}, u32[]{:S(2)}, u32[]{:S(2)}) collective-permute-start(f32[32,512]{1,0:T(8,128)S(1)} %get-tuple-element.53), channel_id=1, source_target_pairs={{0,256},{256,0},{1,257},{257,1},{2,258},{258,2},{3,259},{259,3},{4... | collective-permute-start | bytes 196616 | tf_op jit(solution)/shard_map/ppermute | solution.py:256

commit v7 on v5

--- a/solution.py
+++ b/solution.py
@@ -16,7 +16,7 @@
 EXTRA = 2
 SMEM = pl.BlockSpec(memory_space=pltpu.SMEM)
 VMEM = pl.BlockSpec(memory_space=pltpu.VMEM)
-PARAMS = pltpu.CompilerParams(vmem_limit_bytes=12 * 1024 * 1024)
+PARAMS = pltpu.CompilerParams(vmem_limit_bytes=8 * 1024 * 1024)
 
 
 def dot(first, second, precision=lax.Precision.HIGHEST):
@@ -31,22 +31,39 @@
     return [pl.ds(LANES * t, LANES) for t in range(width // LANES)]
 
 
-def halves_kernel(weight, place_ref, left_ref, right_ref, prev_ref, kept_ref, sent_ref):
+def halves_kernel(weight, place_ref, grad_ref, prev_ref, kept_ref, sent_ref, gram_ref):
     y, core = place_ref[0], place_ref[1]
-    width = left_ref.shape[1]
+    terms, width, _ = grad_ref.shape
     half = prev_ref.shape[1]
     groups = half // TILE
     columns = tile_columns(width)
-    chunks = left_ref.shape[0] // (2 * half)
+    chunks = width // (2 * half)
     count = chunks * groups * len(columns)
+    step = 2 * LANES
+    for kind in range(2):
+        for first in range(0, width, step):
+            part = pl.ds(first, step)
+            total = jnp.zeros((step, width), jnp.float32)
+            for term in range(terms):
+                if kind == 0:
+                    rows, axis = grad_ref[term, part, :], 1
+                else:
+                    rows, axis = grad_ref[term, :, part], 0
+                total = total + lax.dot_general(
+                    rows,
+                    grad_ref[term],
+                    (((axis,), (axis,)), ((), ())),
+                    preferred_element_type=jnp.float32,
+                )
+            gram_ref[kind, part, :] = total * weight
     for out_ref, part in ((kept_ref, core), (sent_ref, 1 - core)):
-        for chunk in range(chunks):
-            for group in range(groups):
-                first = pl.multiple_of(2 * half * chunk + half * part + TILE * group, TILE)
-                for t, lanes in enumerate(columns):
-                    number = (chunk * groups + group) * len(columns) + t
-                    out_ref[number] = left_ref[pl.ds(first, TILE), lanes] * weight
-                    out_ref[count + number] = right_ref[pl.ds(first, TILE), lanes] * weight
+        for kind in range(2):
+            for chunk in range(chunks):
+                for group in range(groups):
+                    first = pl.multiple_of(2 * half * chunk + half * part + TILE * group, TILE)
+                    for t, lanes in enumerate(columns):
+                        number = (chunk * groups + group) * len(columns) + t + count * kind
+                        out_ref[number] = gram_ref[kind, pl.ds(first, TILE), lanes]
     for kind in range(2):
         for group in range(groups):
             for t, lanes in enumerate(columns):
@@ -54,8 +71,9 @@
                 kept_ref[number] += HISTORY * prev_ref[kind, pl.ds(TILE * group, TILE), lanes]
 
 
-def split_halves(place, left, right, prev, weight):
-    messages = left.shape[0] * left.shape[1] // (TILE * LANES)
+def gram_halves(place, gradients, prev, weight):
+    width = gradients.shape[1]
+    messages = width * width // (TILE * LANES)
 
     def kernel(*refs):
         halves_kernel(weight, *refs)
@@ -63,10 +81,11 @@
     return pl.pallas_call(
         kernel,
         out_shape=[shape_of(messages, TILE, LANES)] * 2,
-        in_specs=[SMEM, VMEM, VMEM, VMEM],
+        in_specs=[SMEM, VMEM, VMEM],
         out_specs=[VMEM] * 2,
-        compiler_params=PARAMS,
-    )(place, left, right, prev)
+        scratch_shapes=[pltpu.VMEM((2, width, width), jnp.float32)],
+        compiler_params=PARAMS,
+    )(place, gradients, prev)
 
 
 def message_kernel(kept_ref, got_ref, warm_ref, out_ref):
@@ -200,9 +219,7 @@
     half = width // y_count // 2
     weight = (1.0 - HISTORY) / (y_count * 2 * gradients.shape[0])
 
-    left = jnp.einsum("mik,mjk->ij", gradients, gradients, preferred_element_type=jnp.float32)
-    right = jnp.einsum("mki,mkj->ij", gradients, gradients, preferred_element_type=jnp.float32)
-    kept, sent = split_halves(jnp.stack([y, core]), left, right, prev_stats[0], weight)
+    kept, sent = gram_halves(jnp.stack([y, core]), gradients, prev_stats[0], weight)
     got = lax.ppermute(sent, "core", SWAP)
     messages = build_messages(kept, got, warm_roots[0])
     peers = kept.shape[0]
@@ -239,10 +256,10 @@
     estimate = dot(warm_rows.reshape(kinds * half, width), factor, high)
 
     def second_step():
-        factor_sq = dot(factor, factor, high)
-        coupled_next = dot(factor_sq, dot(factor_sq, coupled, high), high)
-        factor_next = (5.0 * identity - coupled_next) * 0.25
-        return dot(estimate, factor_next, high)
+        rows = estimate
+        for matrix in (factor, factor, factor, factor, coupled):
+            rows = dot(rows, matrix, high)
+        return (5.0 * estimate - rows) * 0.25
 
     root_rows = lax.cond(iterations >= 2, second_step, lambda: estimate)
     first = kind == 0

time: 134 us -> 133 us (level)
  waiting for transfers between devices: 43.3 us -> 45.3 us
  starting transfers between devices: 33.9 us -> 32 us
    dot_general x2 -> x0, matrix products: 2.99 us -> none  [the longest x1 1.99 us: local(): jnp.einsum('mki,mkj->ij', gradients, gradients, preferred_element_type=jn...]
    dot_general x4 -> x9, matrix products: 6.02 us -> 8.2 us  [dot(): jnp.dot(first, second, precision=precision, preferred_element_type=jnp.fl...]
    ppermute x1, waiting for transfers between devices: 5.46 us -> 7.54 us  [local(): root_got = lax.ppermute(root_sent, 'yh', SWAP)]
    ppermute x1, starting transfers between devices: 3.89 us -> 1.92 us  [local(): root_got = lax.ppermute(root_sent, 'yh', SWAP)]
    pallas_call x1, Pallas kernels: 0.83 us -> 2.51 us  [gram_halves(): pl.pallas_call(kernel, out_shape=[shape_of(messages, TILE, LANES)] * 2, i...]
where the time goes in v7:
time: 133 us
  waiting for transfers between devices  45.3 us (34%)
  blocking collectives  35.4 us (27%)
  starting transfers between devices  32 us (24%)
  matrix products  8.2 us (6%)
  Pallas kernels  5.55 us (4%)
  local copies, waits for them, and re-layouts  3.63 us (3%)
  between operations  1.48 us (1%)
    all_to_all x1, waiting for transfers between devices, local(): lax.all_to_all(messages.reshape(peers, 1, -1), PLANE, 0, 0, tiled=True)  35.5 us
    all_to_all x1, blocking collectives, local(): own = lax.all_to_all(tiles, LINE, 0, 0, tiled=True)  35.4 us
    all_to_all x1, starting transfers between devices, local(): lax.all_to_all(messages.reshape(peers, 1, -1), PLANE, 0, 0, tiled=True)  17.1 us
    ppermute x1, starting transfers between devices, local(): got = lax.ppermute(sent, 'core', SWAP)  8.79 us
    dot_general x9, matrix products, dot(): jnp.dot(first, second, precision=precision, preferred_element_type=jnp.fl...  8.2 us
    ppermute x1, waiting for transfers between devices, local(): root_got = lax.ppermute(root_sent, 'yh', SWAP)  7.54 us
    ppermute x1, starting transfers between devices, local(): other = lax.ppermute(own, 'core', SWAP)  4.12 us
  transfers between devices with their start and end apart: 4, of which 3 were waited for; matrix products, arithmetic and copies ran while one was open for 1% of the time, Pallas kernels for 0%

profile of v7, /device:TPU:1, one launch (start us, length us, event | category | flops | bytes accessed | tf_op | source)
XLA Modules:
  0.0 132.6 jit_solution(12400904632860205757)
XLA Ops:
  0.0 0.1 pad_add_fusion.refs_0_
  0.1 0.0 copy-start
  0.1 1.4 %copy-done = bf16[3,1,512,512]{3,2,1,0:T(8,128)(2,1)S(1)} copy-done((bf16[3,1,512,512]{3,2,1,0:T(8,128)(2,1)S(1)}, bf16[3,1,512,512]{3,2,1,0:T(8,128)(2,1)}, u32[]{:S(2)}) %copy-start) | copy-done | bytes 1572888
  1.5 0.0 copy-start.2
  1.5 0.9 copy-done.2
  2.4 0.0 copy-start.1
  2.4 2.5 %shard_map.64 = (f32[256,8,128]{2,1,0:T(8,128)S(1)}, f32[256,8,128]{2,1,0:T(8,128)S(1)}) custom-call(s32[2]{0:T(128)S(1)} %pad_add_fusion.refs_0_, bf16[3,512,512]{2,1,0:T(8,128)(2,1)S(1)} %bitcast.37, f32[2,32,512]{2,1,0:T(8,128)S(1)} %bitcast.40), custom_call_target="tpu_custom_call" | custom-call | tf_op jit(solution)/shard_map/pallas_call | solution.py:81
  4.9 8.8 %collective-permute-start = (f32[256,8,128]{2,1,0:T(8,128)S(1)}, f32[256,8,128]{2,1,0:T(8,128)S(1)}, u32[]{:S(2)}, u32[]{:S(2)}) collective-permute-start(f32[256,8,128]{2,1,0:T(8,128)S(1)} %get-tuple-element.47), channel_id=1, source_target_pairs={{0,32},{32,0},{1,33},{33,1},{2,34},{34,2},{3,35},{35,3},{4,36},{36... | collective-permute-start | bytes 3145736 | tf_op jit(solution)/shard_map/ppermute | solution.py:223
  13.7 2.3 %collective-permute-done.got_ref = f32[256,8,128]{2,1,0:T(8,128)S(1)} collective-permute-done((f32[256,8,128]{2,1,0:T(8,128)S(1)}, f32[256,8,128]{2,1,0:T(8,128)S(1)}, u32[]{:S(2)}, u32[]{:S(2)}) %collective-permute-start) | collective-permute-done | bytes 1048608 | tf_op jit(solution)/shard_map/ppermute | solution.py:223
  16.0 0.0 copy-done.1
  16.0 1.2 shard_map.65
  17.2 0.0 copy-start.4
  17.2 0.0 copy-start.3
  17.2 17.1 %all-to-all-start = ((f32[256,1,1280]{2,1,0:T(1,128)}), f32[256,1,1280]{2,1,0:T(1,128)S(1)}, u32[]{:S(2)}, u32[]{:S(2)}) async-start(f32[256,1,1280]{2,1,0:T(1,128)} %bitcast.8), calls=%async_computation | async-start | bytes 2621440 | tf_op jit(solution)/shard_map/all_to_all | solution.py:226
  34.4 0.0 copy-done.4
  34.4 0.1 select_reduce_fusion.block_ref
  34.5 0.1 iota_add_fusion
  34.6 0.1 add.48
  34.7 0.0 copy-done.3
  34.7 0.1 fusion.2
  34.8 35.5 %all-to-all-done = f32[256,1,1280]{2,1,0:T(1,128)S(1)} async-done(((f32[256,1,1280]{2,1,0:T(1,128)}), f32[256,1,1280]{2,1,0:T(1,128)S(1)}, u32[]{:S(2)}, u32[]{:S(2)}) %all-to-all-start) | async-done | bytes 1310752 | tf_op jit(solution)/shard_map/all_to_all | solution.py:226
  70.3 0.8 shard_map.66
  71.2 0.0 copy-start.5
  71.2 35.4 %all_to_all.10 = f32[128,16,128]{2,1,0:T(8,128)S(1)} all-to-all(f32[128,16,128]{2,1,0:T(8,128)S(1)} %shard_map.66), channel_id=1, replica_groups=mesh['yh'=2,'yl'=4,'core'=2,'x'=4,'z'=8] {'yl','x','z'}, dimensions={0} | all-to-all | bytes 2097152 | tf_op jit(solution)/shard_map/all_to_all | solution.py:239
  106.5 4.1 %collective-permute-start.1 = (f32[128,16,128]{2,1,0:T(8,128)S(1)}, f32[128,16,128]{2,1,0:T(8,128)S(1)}, u32[]{:S(2)}, u32[]{:S(2)}) collective-permute-start(f32[128,16,128]{2,1,0:T(8,128)S(1)} %all_to_all.10), channel_id=1, source_target_pairs={{0,32},{32,0},{1,33},{33,1},{2,34},{34,2},{3,35},{35,3},{4,36},{36... | collective-permute-start | bytes 3145736 | tf_op jit(solution)/shard_map/ppermute | solution.py:240
  110.7 0.6 dynamic_slice.9
  111.9 0.0 copy-done.5
  111.9 0.6 dynamic_slice.10
  113.2 0.0 collective-permute-done.1
  113.2 1.0 shard_map.67
  114.2 1.8 %fusion.8 = f32[512,512]{1,0:T(8,128)S(1)} fusion(f32[512,512]{1,0:T(8,128)S(1)} %get-tuple-element.48), kind=kOutput, calls=%fused_computation.22 | convolution fusion | flops 1610612736 | bytes 2097152 | tf_op jit(solution)/shard_map/dot_general | solution.py:23
  116.0 1.8 %fusion.9 = f32[512,512]{1,0:T(8,128)S(1)} fusion(f32[512,512]{1,0:T(8,128)S(1)} %fusion.8), kind=kOutput, calls=%fused_computation.23 | convolution fusion | flops 1610612736 | bytes 2097152 | tf_op jit(solution)/shard_map/dot_general | solution.py:23
  117.9 1.9 %subtract_multiply_fusion = (f32[512,512]{1,0:T(8,128)S(1)}, f32[512,512]{1,0:T(8,128)S(1)}) fusion(f32[512,512]{1,0:T(8,128)S(1)} %fusion.9, f32[512,512]{1,0:T(8,128)S(1)} %get-tuple-element.49), kind=kOutput, calls=%fused_computation.2 | convolution fusion | flops 1611661312 | bytes 4194304 | tf_op jit(solution)/shard_map/dot_general | solution.py:23
  119.7 0.5 fusion.3
  120.2 2.2 %conditional.1 = (f32[64,512]{1,0:T(8,128)S(1)}) conditional(s32[]{:T(128)} %bitcast.1, f32[64,512]{1,0:T(8,128)S(1)} %fusion.3, (f32[64,512]{1,0:T(8,128)S(1)}, f32[512,512]{1,0:T(8,128)S(1)}, f32[512,512]{1,0:T(8,128)S(1)}) %tuple.29), branch_computations={%region_3.4_spmd, %region_4.5_spmd} | conditional | flops 503414784 | bytes 6684680 | solution.py:264
  120.2 0.4 fusion.4
  120.7 0.4 fusion.5
  121.1 0.4 fusion.6
  121.6 0.4 fusion.7
  122.0 0.4 fusion
  122.5 1.9 %collective-permute-start.2 = (f32[32,512]{1,0:T(8,128)S(1)}, f32[32,512]{1,0:T(8,128)S(1)}, u32[]{:S(2)}, u32[]{:S(2)}) collective-permute-start(f32[32,512]{1,0:T(8,128)S(1)} %get-tuple-element.53), channel_id=1, source_target_pairs={{0,256},{256,0},{1,257},{257,1},{2,258},{258,2},{3,259},{259,3},{4... | collective-permute-start | bytes 196616 | tf_op jit(solution)/shard_map/ppermute | solution.py:268
  124.4 7.5 %collective-permute-done.2 = f32[32,512]{1,0:T(8,128)S(1)} collective-permute-done((f32[32,512]{1,0:T(8,128)S(1)}, f32[32,512]{1,0:T(8,128)S(1)}, u32[]{:S(2)}, u32[]{:S(2)}) %collective-permute-start.2) | collective-permute-done | bytes 65568 | tf_op jit(solution)/shard_map/ppermute | solution.py:268
  131.9 0.7 maximum_select_fusion
  (3 shorter events, 0.0 us)
Async XLA Ops:
  0.1 1.4 %copy-start = (bf16[3,1,512,512]{3,2,1,0:T(8,128)(2,1)S(1)}, bf16[3,1,512,512]{3,2,1,0:T(8,128)(2,1)}, u32[]{:S(2)}) copy-start(bf16[3,1,512,512]{3,2,1,0:T(8,128)(2,1)} %param.8) | copy-start | bytes 4718596
  1.5 0.9 copy-start.2
  2.4 13.6 %copy-start.1 = (f32[1,2,32,512]{3,2,1,0:T(8,128)S(1)}, f32[1,2,32,512]{3,2,1,0:T(8,128)}, u32[]{:S(2)}) copy-start(f32[1,2,32,512]{3,2,1,0:T(8,128)} %param.10) | copy-start | bytes 393220
  4.9 11.1 %collective-permute-start = (f32[256,8,128]{2,1,0:T(8,128)S(1)}, f32[256,8,128]{2,1,0:T(8,128)S(1)}, u32[]{:S(2)}, u32[]{:S(2)}) collective-permute-start(f32[256,8,128]{2,1,0:T(8,128)S(1)} %get-tuple-element.47), channel_id=1, source_target_pairs={{0,32},{32,0},{1,33},{33,1},{2,34},{34,2},{3,35},{35,3},{4,36},{36... | collective-permute-start | bytes 3145736 | tf_op jit(solution)/shard_map/ppermute | solution.py:223
  17.2 17.1 %copy-start.4 = (s32[32]{0:T(128)S(1)}, s32[32]{0:T(128)}, u32[]{:S(2)}) copy-start(s32[32]{0:T(128)} %param.13) | copy-start | bytes 388
  17.2 17.5 %copy-start.3 = (s32[32,2]{0,1:T(2,128)S(1)}, s32[32,2]{0,1:T(2,128)}, u32[]{:S(2)}) copy-start(s32[32,2]{0,1:T(2,128)} %param.11) | copy-start | bytes 772
  17.2 53.1 %all-to-all-start = ((f32[256,1,1280]{2,1,0:T(1,128)}), f32[256,1,1280]{2,1,0:T(1,128)S(1)}, u32[]{:S(2)}, u32[]{:S(2)}) async-start(f32[256,1,1280]{2,1,0:T(1,128)} %bitcast.8), calls=%async_computation | async-start | bytes 2621440 | tf_op jit(solution)/shard_map/all_to_all | solution.py:226
  71.2 40.8 %copy-start.5 = (s32[64]{0:T(128)S(1)}, s32[64]{0:T(128)}, u32[]{:S(2)}) copy-start(s32[64]{0:T(128)} %param.12) | copy-start | bytes 772
  106.5 6.6 %collective-permute-start.1 = (f32[128,16,128]{2,1,0:T(8,128)S(1)}, f32[128,16,128]{2,1,0:T(8,128)S(1)}, u32[]{:S(2)}, u32[]{:S(2)}) collective-permute-start(f32[128,16,128]{2,1,0:T(8,128)S(1)} %all_to_all.10), channel_id=1, source_target_pairs={{0,32},{32,0},{1,33},{33,1},{2,34},{34,2},{3,35},{35,3},{4,36},{36... | collective-permute-start | bytes 3145736 | tf_op jit(solution)/shard_map/ppermute | solution.py:240
  122.5 9.5 %collective-permute-start.2 = (f32[32,512]{1,0:T(8,128)S(1)}, f32[32,512]{1,0:T(8,128)S(1)}, u32[]{:S(2)}, u32[]{:S(2)}) collective-permute-start(f32[32,512]{1,0:T(8,128)S(1)} %get-tuple-element.53), channel_id=1, source_target_pairs={{0,256},{256,0},{1,257},{257,1},{2,258},{258,2},{3,259},{259,3},{4... | collective-permute-start | bytes 196616 | tf_op jit(solution)/shard_map/ppermute | solution.py:268

commit v8 on v7

--- a/solution.py
+++ b/solution.py
@@ -31,10 +31,9 @@
     return [pl.ds(LANES * t, LANES) for t in range(width // LANES)]
 
 
-def halves_kernel(weight, place_ref, grad_ref, prev_ref, kept_ref, sent_ref, gram_ref):
-    y, core = place_ref[0], place_ref[1]
+def halves_kernel(weight, half, core_ref, grad_ref, kept_ref, sent_ref, gram_ref):
+    core = core_ref[0]
     terms, width, _ = grad_ref.shape
-    half = prev_ref.shape[1]
     groups = half // TILE
     columns = tile_columns(width)
     chunks = width // (2 * half)
@@ -64,36 +63,39 @@
                     for t, lanes in enumerate(columns):
                         number = (chunk * groups + group) * len(columns) + t + count * kind
                         out_ref[number] = gram_ref[kind, pl.ds(first, TILE), lanes]
-    for kind in range(2):
-        for group in range(groups):
-            for t, lanes in enumerate(columns):
-                number = (y * groups + group) * len(columns) + t + count * kind
-                kept_ref[number] += HISTORY * prev_ref[kind, pl.ds(TILE * group, TILE), lanes]
-
-
-def gram_halves(place, gradients, prev, weight):
+
+
+def gram_halves(core, gradients, half, weight):
     width = gradients.shape[1]
     messages = width * width // (TILE * LANES)
 
     def kernel(*refs):
-        halves_kernel(weight, *refs)
+        halves_kernel(weight, half, *refs)
 
     return pl.pallas_call(
         kernel,
         out_shape=[shape_of(messages, TILE, LANES)] * 2,
-        in_specs=[SMEM, VMEM, VMEM],
+        in_specs=[SMEM, VMEM],
         out_specs=[VMEM] * 2,
         scratch_shapes=[pltpu.VMEM((2, width, width), jnp.float32)],
         compiler_params=PARAMS,
-    )(place, gradients, prev)
-
-
-def message_kernel(kept_ref, got_ref, warm_ref, out_ref):
+    )(core, gradients)
+
+
+def message_kernel(y_ref, kept_ref, got_ref, prev_ref, warm_ref, out_ref):
     _, rows, width = warm_ref.shape
     columns = tile_columns(width)
     size = TILE + EXTRA
     for number in range(kept_ref.shape[0]):
         out_ref[pl.ds(size * number, TILE), :] = kept_ref[number] + got_ref[number]
+    count = kept_ref.shape[0] // 2
+    shares = rows // TILE * len(columns)
+    for kind in range(2):
+        for part in range(shares):
+            group, t = divmod(part, len(columns))
+            number = count * kind + y_ref[0] * shares + part
+            value = HISTORY * prev_ref[kind, pl.ds(TILE * group, TILE), columns[t]]
+            out_ref[pl.ds(size * number, TILE), :] = kept_ref[number] + got_ref[number] + value
     for kind in range(2):
         for slot in range(EXTRA):
             for t, lanes in enumerate(columns):
@@ -104,14 +106,14 @@
                     ] = warm_ref[slot, pl.ds(first, TILE), lanes]
 
 
-def build_messages(kept, got, warm):
+def build_messages(y, kept, got, prev, warm):
     return pl.pallas_call(
         message_kernel,
         out_shape=shape_of(kept.shape[0] * (TILE + EXTRA), LANES),
-        in_specs=[VMEM] * 3,
+        in_specs=[SMEM] + [VMEM] * 4,
         out_specs=VMEM,
         compiler_params=PARAMS,
-    )(kept, got, warm)
+    )(y, kept, got, prev, warm)
 
 
 def deliver_kernel(kind_ref, block_ref, owner_ref, slot_ref, in_ref, out_ref, dense_ref, sum_ref, warm_ref):
@@ -219,9 +221,9 @@
     half = width // y_count // 2
     weight = (1.0 - HISTORY) / (y_count * 2 * gradients.shape[0])
 
-    kept, sent = gram_halves(jnp.stack([y, core]), gradients, prev_stats[0], weight)
+    kept, sent = gram_halves(core.reshape(1), gradients, half, weight)
     got = lax.ppermute(sent, "core", SWAP)
-    messages = build_messages(kept, got, warm_roots[0])
+    messages = build_messages(y.reshape(1), kept, got, prev_stats[0], warm_roots[0])
     peers = kept.shape[0]
     arrived = lax.all_to_all(messages.reshape(peers, 1, -1), PLANE, 0, 0, tiled=True)
 
@@ -248,12 +250,14 @@
     coupled = dot(fourth, scaled)
     factor = (5.0 * identity - coupled) * 0.25
     high = lax.Precision.HIGH
-    warm_rows = lax.dynamic_slice(
-        warm_start.reshape(kinds, lines, 2, half, width),
-        (0, y - kind * lines, core, 0, 0),
-        (kinds, 1, 1, half, width),
-    )
-    estimate = dot(warm_rows.reshape(kinds * half, width), factor, high)
+    across = y_count - 1 - y
+    warm_rows = warm_start.reshape(y_count, 2, half, width)
+    warm_rows = [
+        lax.dynamic_slice(warm_rows, (chunk, core, 0, 0), (1, 1, half, width))
+        for chunk in (y, across)
+    ]
+    warm_rows = jnp.concatenate(warm_rows, 0).reshape(2 * half, width)
+    estimate = dot(warm_rows, factor, high)
 
     def second_step():
         rows = estimate
@@ -262,12 +266,11 @@
         return (5.0 * estimate - rows) * 0.25
 
     root_rows = lax.cond(iterations >= 2, second_step, lambda: estimate)
-    first = kind == 0
-    root_sent = jnp.where(first, root_rows[half:], root_rows[:half])
-    root_kept = jnp.where(first, root_rows[:half], root_rows[half:])
-    root_got = lax.ppermute(root_sent, "yh", SWAP)
+    pairs = [(i, y_count - 1 - i) for i in range(y_count)]
+    root_kept = root_rows[:half]
+    root_got = lax.ppermute(root_rows[half:], ("yh", "yl"), pairs)
     result = jnp.where(
-        first, jnp.stack([root_kept, root_got]), jnp.stack([root_got, root_kept])
+        kind == 0, jnp.stack([root_kept, root_got]), jnp.stack([root_got, root_kept])
     )
     return result[None]
 

time: 133 us -> 128 us (0.962); the launches traced: 133 us -> 126 us
  waiting for transfers between devices: 45.3 us -> 40.5 us
  matrix products: 8.2 us -> 6.02 us
  starting transfers between devices: 32 us -> 34 us
    ppermute x1, waiting for transfers between devices: 7.54 us -> 2.73 us  [local(): root_got = lax.ppermute(root_rows[half:], ('yh', 'yl'), pairs)]
    dot_general x9 -> x4, matrix products: 8.2 us -> 6.02 us  [dot(): jnp.dot(first, second, precision=precision, preferred_element_type=jnp.fl...]
    ppermute x1, starting transfers between devices: 1.92 us -> 3.92 us  [local(): root_got = lax.ppermute(root_rows[half:], ('yh', 'yl'), pairs)]
where the time goes in v8:
time: 128 us; the launch traced here: 126 us
  waiting for transfers between devices  40.5 us (32%)
  blocking collectives  35.4 us (28%)
  starting transfers between devices  34 us (27%)
  matrix products  6.02 us (5%)
  Pallas kernels  5.02 us (4%)
  local copies, waits for them, and re-layouts  2.75 us (2%)
  between operations  1.5 us (1%)
    all_to_all x1, waiting for transfers between devices, local(): lax.all_to_all(messages.reshape(peers, 1, -1), PLANE, 0, 0, tiled=True)  35.5 us
    all_to_all x1, blocking collectives, local(): own = lax.all_to_all(tiles, LINE, 0, 0, tiled=True)  35.4 us
    all_to_all x1, starting transfers between devices, local(): lax.all_to_all(messages.reshape(peers, 1, -1), PLANE, 0, 0, tiled=True)  17.1 us
    ppermute x1, starting transfers between devices, local(): got = lax.ppermute(sent, 'core', SWAP)  8.79 us
    dot_general x4, matrix products, dot(): jnp.dot(first, second, precision=precision, preferred_element_type=jnp.fl...  6.02 us
    ppermute x1, starting transfers between devices, local(): other = lax.ppermute(own, 'core', SWAP)  4.12 us
    ppermute x1, starting transfers between devices, local(): root_got = lax.ppermute(root_rows[half:], ('yh', 'yl'), pairs)  3.92 us
    ppermute x1, waiting for transfers between devices, local(): root_got = lax.ppermute(root_rows[half:], ('yh', 'yl'), pairs)  2.73 us
  transfers between devices with their start and end apart: 4, of which 3 were waited for; matrix products, arithmetic and copies ran while one was open for 1% of the time, Pallas kernels for 0%

profile of v8, /device:TPU:1, one launch (start us, length us, event | category | flops | bytes accessed | tf_op | source)
XLA Modules:
  0.0 126.1 jit_solution(6403324235591423740)
XLA Ops:
  0.0 0.0 copy-start
  0.0 1.4 %copy-done = bf16[3,1,512,512]{3,2,1,0:T(8,128)(2,1)S(1)} copy-done((bf16[3,1,512,512]{3,2,1,0:T(8,128)(2,1)S(1)}, bf16[3,1,512,512]{3,2,1,0:T(8,128)(2,1)}, u32[]{:S(2)}) %copy-start) | copy-done | bytes 1572888
  1.4 0.0 copy-start.1
  1.4 0.0 copy-start.2
  1.4 1.9 %shard_map.64 = (f32[256,8,128]{2,1,0:T(8,128)S(1)}, f32[256,8,128]{2,1,0:T(8,128)S(1)}) custom-call(s32[1]{0:T(128)} %bitcast.2.refs_0_.core_ref, bf16[3,512,512]{2,1,0:T(8,128)(2,1)S(1)} %bitcast.37), custom_call_target="tpu_custom_call" | custom-call | tf_op jit(solution)/shard_map/pallas_call | solution.py:75
  3.4 8.8 %collective-permute-start = (f32[256,8,128]{2,1,0:T(8,128)S(1)}, f32[256,8,128]{2,1,0:T(8,128)S(1)}, u32[]{:S(2)}, u32[]{:S(2)}) collective-permute-start(f32[256,8,128]{2,1,0:T(8,128)S(1)} %get-tuple-element.23), channel_id=1, source_target_pairs={{0,32},{32,0},{1,33},{33,1},{2,34},{34,2},{3,35},{35,3},{4,36},{36... | collective-permute-start | bytes 3145736 | tf_op jit(solution)/shard_map/ppermute | solution.py:225
  12.2 2.3 %collective-permute-done.got_ref = f32[256,8,128]{2,1,0:T(8,128)S(1)} collective-permute-done((f32[256,8,128]{2,1,0:T(8,128)S(1)}, f32[256,8,128]{2,1,0:T(8,128)S(1)}, u32[]{:S(2)}, u32[]{:S(2)}) %collective-permute-start) | collective-permute-done | bytes 1048608 | tf_op jit(solution)/shard_map/ppermute | solution.py:225
  14.4 0.0 copy-done.1
  14.4 0.0 copy-done.2
  14.4 1.3 %shard_map.65 = f32[2560,128]{1,0:T(8,128)} custom-call(s32[1]{0:T(128)} %bitcast.4.y_ref, f32[256,8,128]{2,1,0:T(8,128)S(1)} %get-tuple-element.22.kept_ref, f32[256,8,128]{2,1,0:T(8,128)S(1)} %collective-permute-done.got_ref, f32[2,32,512]{2,1,0:T(8,128)S(1)} %bitcast.39, f32[2,32,512]{2,1,0:T(8,128)S(1)} %bitcast.40), custom_call_target="tpu_custom_call" | custom-call | tf_op jit(solution)/shard_map/pallas_call | solution.py:110
  15.7 0.0 copy-start.4
  15.7 0.0 copy-start.3
  15.7 17.1 %all-to-all-start = ((f32[256,1,1280]{2,1,0:T(1,128)}), f32[256,1,1280]{2,1,0:T(1,128)S(1)}, u32[]{:S(2)}, u32[]{:S(2)}) async-start(f32[256,1,1280]{2,1,0:T(1,128)} %bitcast.8), calls=%async_computation | async-start | bytes 2621440 | tf_op jit(solution)/shard_map/all_to_all | solution.py:228
  32.9 0.0 copy-done.4
  32.9 0.1 select_reduce_fusion.block_ref
  33.0 0.1 iota_add_fusion
  33.1 0.1 add.53
  33.2 0.0 copy-done.3
  33.2 0.1 fusion.2
  33.3 35.5 %all-to-all-done = f32[256,1,1280]{2,1,0:T(1,128)S(1)} async-done(((f32[256,1,1280]{2,1,0:T(1,128)}), f32[256,1,1280]{2,1,0:T(1,128)S(1)}, u32[]{:S(2)}, u32[]{:S(2)}) %all-to-all-start) | async-done | bytes 1310752 | tf_op jit(solution)/shard_map/all_to_all | solution.py:228
  68.8 0.8 shard_map.66
  69.7 0.0 copy-start.5
  69.7 35.4 %all_to_all.10 = f32[128,16,128]{2,1,0:T(8,128)S(1)} all-to-all(f32[128,16,128]{2,1,0:T(8,128)S(1)} %shard_map.66), channel_id=1, replica_groups=mesh['yh'=2,'yl'=4,'core'=2,'x'=4,'z'=8] {'yl','x','z'}, dimensions={0} | all-to-all | bytes 2097152 | tf_op jit(solution)/shard_map/all_to_all | solution.py:241
  105.0 4.1 %collective-permute-start.1 = (f32[128,16,128]{2,1,0:T(8,128)S(1)}, f32[128,16,128]{2,1,0:T(8,128)S(1)}, u32[]{:S(2)}, u32[]{:S(2)}) collective-permute-start(f32[128,16,128]{2,1,0:T(8,128)S(1)} %all_to_all.10), channel_id=1, source_target_pairs={{0,32},{32,0},{1,33},{33,1},{2,34},{34,2},{3,35},{35,3},{4,36},{36... | collective-permute-start | bytes 3145736 | tf_op jit(solution)/shard_map/ppermute | solution.py:242
  109.2 0.6 dynamic_slice.12
  110.4 0.0 copy-done.5
  110.4 0.6 dynamic_slice.13
  111.7 0.0 collective-permute-done.1
  111.7 1.0 shard_map.67
  112.6 1.8 %fusion.8 = f32[512,512]{1,0:T(8,128)S(1)} fusion(f32[512,512]{1,0:T(8,128)S(1)} %get-tuple-element.24), kind=kOutput, calls=%fused_computation.22 | convolution fusion | flops 1610612736 | bytes 2097152 | tf_op jit(solution)/shard_map/dot_general | solution.py:23
  114.5 1.8 %fusion.9 = f32[512,512]{1,0:T(8,128)S(1)} fusion(f32[512,512]{1,0:T(8,128)S(1)} %fusion.8), kind=kOutput, calls=%fused_computation.23 | convolution fusion | flops 1610612736 | bytes 2097152 | tf_op jit(solution)/shard_map/dot_general | solution.py:23
  116.4 1.9 %subtract_multiply_fusion = (f32[512,512]{1,0:T(8,128)S(1)}, f32[512,512]{1,0:T(8,128)S(1)}) fusion(f32[512,512]{1,0:T(8,128)S(1)} %fusion.9, f32[512,512]{1,0:T(8,128)S(1)} %get-tuple-element.25), kind=kOutput, calls=%fused_computation.2 | convolution fusion | flops 1611661312 | bytes 4194304 | tf_op jit(solution)/shard_map/dot_general | solution.py:23
  118.3 0.5 fusion.3
  118.8 3.9 %collective-permute-start.2 = (f32[32,512]{1,0:T(8,128)S(1)}, f32[32,512]{1,0:T(8,128)S(1)}, u32[]{:S(2)}, u32[]{:S(2)}) collective-permute-start(f32[32,512]{1,0:T(8,128)S(1)} %get-tuple-element.31), channel_id=1, source_target_pairs={{0,448},{64,384},{128,320},{192,256},{256,192},{320,128},{384,64},... | collective-permute-start | bytes 196616 | tf_op jit(solution)/shard_map/ppermute | solution.py:271
  122.7 2.7 %collective-permute-done.2 = f32[32,512]{1,0:T(8,128)S(1)} collective-permute-done((f32[32,512]{1,0:T(8,128)S(1)}, f32[32,512]{1,0:T(8,128)S(1)}, u32[]{:S(2)}, u32[]{:S(2)}) %collective-permute-start.2) | collective-permute-done | bytes 65568 | tf_op jit(solution)/shard_map/ppermute | solution.py:271
  125.4 0.7 maximum_select_fusion
  (5 shorter events, 0.1 us)
Async XLA Ops:
  0.0 1.4 %copy-start = (bf16[3,1,512,512]{3,2,1,0:T(8,128)(2,1)S(1)}, bf16[3,1,512,512]{3,2,1,0:T(8,128)(2,1)}, u32[]{:S(2)}) copy-start(bf16[3,1,512,512]{3,2,1,0:T(8,128)(2,1)} %param.8) | copy-start | bytes 4718596
  1.4 13.0 %copy-start.1 = (f32[1,2,32,512]{3,2,1,0:T(8,128)S(1)}, f32[1,2,32,512]{3,2,1,0:T(8,128)}, u32[]{:S(2)}) copy-start(f32[1,2,32,512]{3,2,1,0:T(8,128)} %param.9) | copy-start | bytes 393220
  1.4 13.0 %copy-start.2 = (f32[1,2,32,512]{3,2,1,0:T(8,128)S(1)}, f32[1,2,32,512]{3,2,1,0:T(8,128)}, u32[]{:S(2)}) copy-start(f32[1,2,32,512]{3,2,1,0:T(8,128)} %param.10) | copy-start | bytes 393220
  3.4 11.1 %collective-permute-start = (f32[256,8,128]{2,1,0:T(8,128)S(1)}, f32[256,8,128]{2,1,0:T(8,128)S(1)}, u32[]{:S(2)}, u32[]{:S(2)}) collective-permute-start(f32[256,8,128]{2,1,0:T(8,128)S(1)} %get-tuple-element.23), channel_id=1, source_target_pairs={{0,32},{32,0},{1,33},{33,1},{2,34},{34,2},{3,35},{35,3},{4,36},{36... | collective-permute-start | bytes 3145736 | tf_op jit(solution)/shard_map/ppermute | solution.py:225
  15.7 17.1 %copy-start.4 = (s32[32]{0:T(128)S(1)}, s32[32]{0:T(128)}, u32[]{:S(2)}) copy-start(s32[32]{0:T(128)} %param.13) | copy-start | bytes 388
  15.7 17.5 %copy-start.3 = (s32[32,2]{0,1:T(2,128)S(1)}, s32[32,2]{0,1:T(2,128)}, u32[]{:S(2)}) copy-start(s32[32,2]{0,1:T(2,128)} %param.11) | copy-start | bytes 772
  15.7 53.1 %all-to-all-start = ((f32[256,1,1280]{2,1,0:T(1,128)}), f32[256,1,1280]{2,1,0:T(1,128)S(1)}, u32[]{:S(2)}, u32[]{:S(2)}) async-start(f32[256,1,1280]{2,1,0:T(1,128)} %bitcast.8), calls=%async_computation | async-start | bytes 2621440 | tf_op jit(solution)/shard_map/all_to_all | solution.py:228
  69.7 40.8 %copy-start.5 = (s32[64]{0:T(128)S(1)}, s32[64]{0:T(128)}, u32[]{:S(2)}) copy-start(s32[64]{0:T(128)} %param.12) | copy-start | bytes 772
  105.0 6.6 %collective-permute-start.1 = (f32[128,16,128]{2,1,0:T(8,128)S(1)}, f32[128,16,128]{2,1,0:T(8,128)S(1)}, u32[]{:S(2)}, u32[]{:S(2)}) collective-permute-start(f32[128,16,128]{2,1,0:T(8,128)S(1)} %all_to_all.10), channel_id=1, source_target_pairs={{0,32},{32,0},{1,33},{33,1},{2,34},{34,2},{3,35},{35,3},{4,36},{36... | collective-permute-start | bytes 3145736 | tf_op jit(solution)/shard_map/ppermute | solution.py:242
  118.8 6.7 %collective-permute-start.2 = (f32[32,512]{1,0:T(8,128)S(1)}, f32[32,512]{1,0:T(8,128)S(1)}, u32[]{:S(2)}, u32[]{:S(2)}) collective-permute-start(f32[32,512]{1,0:T(8,128)S(1)} %get-tuple-element.31), channel_id=1, source_target_pairs={{0,448},{64,384},{128,320},{192,256},{256,192},{320,128},{384,64},... | collective-permute-start | bytes 196616 | tf_op jit(solution)/shard_map/ppermute | solution.py:271

commit v9 on v8

--- a/solution.py
+++ b/solution.py
@@ -17,10 +17,6 @@
 SMEM = pl.BlockSpec(memory_space=pltpu.SMEM)
 VMEM = pl.BlockSpec(memory_space=pltpu.VMEM)
 PARAMS = pltpu.CompilerParams(vmem_limit_bytes=8 * 1024 * 1024)
-
-
-def dot(first, second, precision=lax.Precision.HIGHEST):
-    return jnp.dot(first, second, precision=precision, preferred_element_type=jnp.float32)
 
 
 def shape_of(*shape):
@@ -158,13 +154,44 @@
     )(kind, blocks, owners, slots, messages)
 
 
-def whole_kernel(core_ref, own_ref, other_ref, scaled_ref, warm_ref):
+def cut(value, parts):
+    pieces = []
+    for number in range(parts):
+        piece = value.astype(jnp.bfloat16)
+        pieces.append(piece)
+        if number < parts - 1:
+            value = value - piece.astype(jnp.float32)
+    return pieces
+
+
+def cut_into(out_ref, parts, value_of):
+    width = out_ref.shape[1]
+    for first in range(0, width, LANES):
+        for number, piece in enumerate(cut(value_of(first), parts)):
+            out_ref[number, pl.ds(first, LANES), :] = piece
+
+
+def product(left, right, parts):
+    total = None
+    for order in reversed(range(parts)):
+        for number in range(order + 1):
+            term = jnp.dot(
+                left[number], right(order - number), preferred_element_type=jnp.float32
+            )
+            total = term if total is None else total + term
+    return total
+
+
+def newton_kernel(
+    core_ref, y_ref, count_ref, own_ref, other_ref, out_ref, scaled_ref, work_ref, left_ref, right_ref
+):
     width = scaled_ref.shape[0]
     columns = tile_columns(width)
     chunks = TILE
     share = width // chunks
     half = share // 2
     groups = half // TILE
+    step = 2 * LANES
 
     def assemble(*halves):
         total = jnp.zeros((TILE, LANES), jnp.float32)
@@ -178,17 +205,28 @@
                         scaled_ref[rows, lanes] = value
                         total = total + value * value
                         first = 2 * TILE * (TILE * group * len(columns) + t) + TILE + chunk
-                        warm_ref[rows, lanes] = in_ref[
+                        work_ref[rows, lanes] = in_ref[
                             pl.ds(first, TILE, stride=2 * TILE * len(columns)), :
                         ]
         total = jnp.sum(jnp.sum(total, axis=0, keepdims=True), axis=1, keepdims=True)
         inverse = 1.0 / jnp.sqrt(total + 1e-06)
-        row = lax.broadcasted_iota(jnp.int32, (share, width), 0)
-        column = lax.broadcasted_iota(jnp.int32, (share, width), 1)
-        for first in range(0, width, share):
-            diagonal = jnp.where(column == row + first, DAMPING, 0.0)
-            rows = pl.ds(first, share)
-            scaled_ref[rows, :] = scaled_ref[rows, :] * inverse + diagonal
+        for first in range(0, width, LANES):
+            rows = pl.ds(first, LANES)
+            scaled_ref[rows, :] = scaled_ref[rows, :] * inverse + diagonal(first, DAMPING)
+
+    def diagonal(first, value):
+        row = lax.broadcasted_iota(jnp.int32, (LANES, width), 0)
+        column = lax.broadcasted_iota(jnp.int32, (LANES, width), 1)
+        return jnp.where(column == row + first, value, 0.0)
+
+    def whole_product(right):
+        for first in range(0, width, step):
+            rows = pl.ds(first, step)
+            left = [left_ref[number, rows, :] for number in range(3)]
+            work_ref[rows, :] = product(left, lambda number: right[number], 3)
+
+    def work(first):
+        return work_ref[pl.ds(first, LANES), :]
 
     @pl.when(core_ref[0] == 0)
     def _():
@@ -198,15 +236,46 @@
     def _():
         assemble(other_ref, own_ref)
 
-
-def whole(core, own, other, width):
+    chosen = []
+    for chunk in (y_ref[0], chunks - 1 - y_ref[0]):
+        first = pl.multiple_of(share * chunk + half * core_ref[0], half)
+        chosen.append(work_ref[pl.ds(first, half), :])
+    chosen = jnp.concatenate(chosen, 0)
+
+    for _ in range(2):
+        cut_into(left_ref, 3, work)
+        whole_product(left_ref)
+    cut_into(left_ref, 3, work)
+    cut_into(right_ref, 3, lambda first: scaled_ref[pl.ds(first, LANES), :])
+    whole_product(right_ref)
+    cut_into(left_ref, 2, lambda first: (diagonal(first, 5.0) - work(first)) * 0.25)
+    estimate = product(cut(chosen, 2), lambda number: left_ref[number], 2)
+    out_ref[...] = estimate
+
+    @pl.when(count_ref[0] >= 2)
+    def _():
+        cut_into(right_ref, 2, work)
+        rows = estimate
+        for matrix in (left_ref, left_ref, left_ref, left_ref, right_ref):
+            rows = product(cut(rows, 2), lambda number: matrix[number], 2)
+        out_ref[...] = (5.0 * estimate - rows) * 0.25
+
+
+def newton(core, y, count, own, other, width):
+    square = (width, width)
     return pl.pallas_call(
-        whole_kernel,
-        out_shape=[shape_of(width, width)] * 2,
-        in_specs=[SMEM, VMEM, VMEM],
-        out_specs=[VMEM] * 2,
-        compiler_params=PARAMS,
-    )(core, own, other)
+        newton_kernel,
+        out_shape=shape_of(width // TILE, width),
+        in_specs=[SMEM] * 3 + [VMEM] * 2,
+        out_specs=VMEM,
+        scratch_shapes=[
+            pltpu.VMEM(square, jnp.float32),
+            pltpu.VMEM(square, jnp.float32),
+            pltpu.VMEM((3,) + square, jnp.bfloat16),
+            pltpu.VMEM((3,) + square, jnp.bfloat16),
+        ],
+        compiler_params=pltpu.CompilerParams(vmem_limit_bytes=14 * 1024 * 1024),
+    )(core, y, count, own, other)
 
 
 def local(grad, prev_stats, warm_roots, owner_items, counts, read_shard):
@@ -233,39 +302,22 @@
     matches = owner_items[None] == items[:, None, None]
     owners = jnp.sum(jnp.where(matches, ids[None, :, None], 0), (1, 2))
     slots = jnp.sum(jnp.where(matches, jnp.arange(2, dtype=jnp.int32), 0), (1, 2))
-    iterations = counts[2 * blocks[worker] + kind]
+    mine = jnp.arange(counts.shape[0], dtype=jnp.int32) == 2 * blocks[worker] + kind
+    iterations = jnp.sum(jnp.where(mine, counts, 0)).reshape(1)
 
     tiles = deliver(
         kind.reshape(1), blocks, owners, slots, arrived.reshape(messages.shape)
     )
     own = lax.all_to_all(tiles, LINE, 0, 0, tiled=True)
     other = lax.ppermute(own, "core", SWAP)
-    scaled, warm_start = whole(
-        core.reshape(1), own.reshape(-1, LANES), other.reshape(-1, LANES), width
-    )
-
-    squared = dot(warm_start, warm_start)
-    fourth = dot(squared, squared)
-    identity = jnp.eye(width, dtype=jnp.float32)
-    coupled = dot(fourth, scaled)
-    factor = (5.0 * identity - coupled) * 0.25
-    high = lax.Precision.HIGH
-    across = y_count - 1 - y
-    warm_rows = warm_start.reshape(y_count, 2, half, width)
-    warm_rows = [
-        lax.dynamic_slice(warm_rows, (chunk, core, 0, 0), (1, 1, half, width))
-        for chunk in (y, across)
-    ]
-    warm_rows = jnp.concatenate(warm_rows, 0).reshape(2 * half, width)
-    estimate = dot(warm_rows, factor, high)
-
-    def second_step():
-        rows = estimate
-        for matrix in (factor, factor, factor, factor, coupled):
-            rows = dot(rows, matrix, high)
-        return (5.0 * estimate - rows) * 0.25
-
-    root_rows = lax.cond(iterations >= 2, second_step, lambda: estimate)
+    root_rows = newton(
+        core.reshape(1),
+        y.reshape(1),
+        iterations,
+        own.reshape(-1, LANES),
+        other.reshape(-1, LANES),
+        width,
+    )
     pairs = [(i, y_count - 1 - i) for i in range(y_count)]
     root_kept = root_rows[:half]
     root_got = lax.ppermute(root_rows[half:], ("yh", "yl"), pairs)

time: 128 us -> 128 us (level)
  Pallas kernels: 5.02 us -> 11.4 us
  matrix products: 6.02 us -> 0 us
  starting transfers between devices: 34 us -> 32 us
  waiting for transfers between devices: 40.5 us -> 42.3 us
    pallas_call x1, Pallas kernels: 0.96 us -> 7.36 us  [newton(): pl.pallas_call(newton_kernel, out_shape=shape_of(width // TILE, width), i...]
    dot_general x4 -> x0, matrix products: 6.02 us -> none  [dot(): jnp.dot(first, second, precision=precision, preferred_element_type=jnp.fl...]
    ppermute x1, starting transfers between devices: 3.92 us -> 1.92 us  [local(): root_got = lax.ppermute(root_rows[half:], ('yh', 'yl'), pairs)]
    ppermute x1, waiting for transfers between devices: 2.73 us -> 4.29 us  [local(): root_got = lax.ppermute(root_rows[half:], ('yh', 'yl'), pairs)]
  transfers between devices with their start and end apart: 4 -> 4, of which waited for: 3 -> 4; matrix products, arithmetic and copies ran while one was open for 1% -> 1% of each run, Pallas kernels for 0% -> 0%
where the time goes in v9:
time: 128 us; the launch traced here: 126 us
  waiting for transfers between devices  42.3 us (33%)
  blocking collectives  35.4 us (28%)
  starting transfers between devices  32 us (25%)
  Pallas kernels  11.4 us (9%)
  local copies, waits for them, and re-layouts  2.2 us (2%)
  other arithmetic  1.65 us (1%)
    all_to_all x1, waiting for transfers between devices, local(): lax.all_to_all(messages.reshape(peers, 1, -1), PLANE, 0, 0, tiled=True)  35.5 us
    all_to_all x1, blocking collectives, local(): own = lax.all_to_all(tiles, LINE, 0, 0, tiled=True)  35.4 us
    all_to_all x1, starting transfers between devices, local(): lax.all_to_all(messages.reshape(peers, 1, -1), PLANE, 0, 0, tiled=True)  17.1 us
    ppermute x1, starting transfers between devices, local(): got = lax.ppermute(sent, 'core', SWAP)  8.79 us
    pallas_call x1, Pallas kernels, newton(): pl.pallas_call(newton_kernel, out_shape=shape_of(width // TILE, width), i...  7.36 us
    ppermute x1, waiting for transfers between devices, local(): root_got = lax.ppermute(root_rows[half:], ('yh', 'yl'), pairs)  4.29 us
    ppermute x1, starting transfers between devices, local(): other = lax.ppermute(own, 'core', SWAP)  4.12 us
  transfers between devices with their start and end apart: 4, of which 4 were waited for; matrix products, arithmetic and copies ran while one was open for 1% of the time, Pallas kernels for 0%

profile of v9, /device:TPU:1, one launch (start us, length us, event | category | flops | bytes accessed | tf_op | source)
XLA Modules:
  0.0 125.7 jit_solution(4158957121053460683)
XLA Ops:
  0.0 0.0 copy-start
  0.0 1.4 %copy-done = bf16[3,1,512,512]{3,2,1,0:T(8,128)(2,1)S(1)} copy-done((bf16[3,1,512,512]{3,2,1,0:T(8,128)(2,1)S(1)}, bf16[3,1,512,512]{3,2,1,0:T(8,128)(2,1)}, u32[]{:S(2)}) %copy-start) | copy-done | bytes 1572888
  1.4 0.0 copy-start.1
  1.4 0.0 copy-start.2
  1.4 1.9 %shard_map.64 = (f32[256,8,128]{2,1,0:T(8,128)S(1)}, f32[256,8,128]{2,1,0:T(8,128)S(1)}) custom-call(s32[1]{0:T(128)} %bitcast.refs_0_.core_ref, bf16[3,512,512]{2,1,0:T(8,128)(2,1)S(1)} %bitcast.17), custom_call_target="tpu_custom_call" | custom-call | tf_op jit(solution)/shard_map/pallas_call | solution.py:71
  3.4 8.8 %collective-permute-start = (f32[256,8,128]{2,1,0:T(8,128)S(1)}, f32[256,8,128]{2,1,0:T(8,128)S(1)}, u32[]{:S(2)}, u32[]{:S(2)}) collective-permute-start(f32[256,8,128]{2,1,0:T(8,128)S(1)} %get-tuple-element.8), channel_id=1, source_target_pairs={{0,32},{32,0},{1,33},{33,1},{2,34},{34,2},{3,35},{35,3},{4,36},{36... | collective-permute-start | bytes 3145736 | tf_op jit(solution)/shard_map/ppermute | solution.py:294
  12.2 2.3 %collective-permute-done.got_ref = f32[256,8,128]{2,1,0:T(8,128)S(1)} collective-permute-done((f32[256,8,128]{2,1,0:T(8,128)S(1)}, f32[256,8,128]{2,1,0:T(8,128)S(1)}, u32[]{:S(2)}, u32[]{:S(2)}) %collective-permute-start) | collective-permute-done | bytes 1048608 | tf_op jit(solution)/shard_map/ppermute | solution.py:294
  14.4 0.0 copy-done.1
  14.4 0.0 copy-done.2
  14.4 1.2 shard_map.65
  15.7 0.0 copy-start.4
  15.7 0.0 copy-start.3
  15.7 17.1 %all-to-all-start = ((f32[256,1,1280]{2,1,0:T(1,128)}), f32[256,1,1280]{2,1,0:T(1,128)S(1)}, u32[]{:S(2)}, u32[]{:S(2)}) async-start(f32[256,1,1280]{2,1,0:T(1,128)} %bitcast.8), calls=%async_computation | async-start | bytes 2621440 | tf_op jit(solution)/shard_map/all_to_all | solution.py:297
  32.8 0.0 copy-done.4
  32.8 0.1 select_reduce_fusion.block_ref
  32.9 0.1 iota_add_fusion
  33.0 0.1 add.39
  33.1 0.0 copy-done.3
  33.1 0.1 fusion.1
  33.2 35.5 %all-to-all-done = f32[256,1,1280]{2,1,0:T(1,128)S(1)} async-done(((f32[256,1,1280]{2,1,0:T(1,128)}), f32[256,1,1280]{2,1,0:T(1,128)S(1)}, u32[]{:S(2)}, u32[]{:S(2)}) %all-to-all-start) | async-done | bytes 1310752 | tf_op jit(solution)/shard_map/all_to_all | solution.py:297
  68.8 0.8 shard_map.66
  69.6 0.0 copy-start.5
  69.6 35.4 %all_to_all.10 = f32[128,16,128]{2,1,0:T(8,128)S(1)} all-to-all(f32[128,16,128]{2,1,0:T(8,128)S(1)} %shard_map.66), channel_id=1, replica_groups=mesh['yh'=2,'yl'=4,'core'=2,'x'=4,'z'=8] {'yl','x','z'}, dimensions={0} | all-to-all | bytes 2097152 | tf_op jit(solution)/shard_map/all_to_all | solution.py:311
  105.0 4.1 %collective-permute-start.1 = (f32[128,16,128]{2,1,0:T(8,128)S(1)}, f32[128,16,128]{2,1,0:T(8,128)S(1)}, u32[]{:S(2)}, u32[]{:S(2)}) collective-permute-start(f32[128,16,128]{2,1,0:T(8,128)S(1)} %all_to_all.10), channel_id=1, source_target_pairs={{0,32},{32,0},{1,33},{33,1},{2,34},{34,2},{3,35},{35,3},{4,36},{36... | collective-permute-start | bytes 3145736 | tf_op jit(solution)/shard_map/ppermute | solution.py:312
  109.1 0.7 dynamic_slice.3
  110.4 0.0 copy-done.5
  110.4 0.7 fusion.2
  111.1 0.3 collective-permute-done.1
  111.4 7.4 %shard_map.67 = f32[64,512]{1,0:T(8,128)S(1)} custom-call(s32[1]{0:T(128)} %bitcast.refs_0_.core_ref, s32[1]{0:T(128)} %bitcast.1.y_ref, s32[1]{0:T(128)} %bitcast.3.count_ref, f32[2048,128]{1,0:T(8,128)S(1)} %bitcast.16, f32[2048,128]{1,0:T(8,128)S(1)} %bitcast.18), custom_call_target="tpu_custom_call" | custom-call | tf_op jit(solution)/shard_map/pallas_call | solution.py:266
  118.8 1.9 %collective-permute-start.2 = (f32[32,512]{1,0:T(8,128)S(1)}, f32[32,512]{1,0:T(8,128)S(1)}, u32[]{:S(2)}, u32[]{:S(2)}) collective-permute-start(f32[32,512]{1,0:T(8,128)S(1)} %get-tuple-element.12), channel_id=1, source_target_pairs={{0,448},{64,384},{128,320},{192,256},{256,192},{320,128},{384,64},... | collective-permute-start | bytes 196616 | tf_op jit(solution)/shard_map/ppermute | solution.py:323
  120.7 4.3 %collective-permute-done.2 = f32[32,512]{1,0:T(8,128)S(1)} collective-permute-done((f32[32,512]{1,0:T(8,128)S(1)}, f32[32,512]{1,0:T(8,128)S(1)}, u32[]{:S(2)}, u32[]{:S(2)}) %collective-permute-start.2) | collective-permute-done | bytes 65568 | tf_op jit(solution)/shard_map/ppermute | solution.py:323
  125.0 0.7 maximum_select_fusion
  (2 shorter events, 0.0 us)
Async XLA Ops:
  0.0 1.4 %copy-start = (bf16[3,1,512,512]{3,2,1,0:T(8,128)(2,1)S(1)}, bf16[3,1,512,512]{3,2,1,0:T(8,128)(2,1)}, u32[]{:S(2)}) copy-start(bf16[3,1,512,512]{3,2,1,0:T(8,128)(2,1)} %param.6) | copy-start | bytes 4718596
  1.4 13.0 %copy-start.1 = (f32[1,2,32,512]{3,2,1,0:T(8,128)S(1)}, f32[1,2,32,512]{3,2,1,0:T(8,128)}, u32[]{:S(2)}) copy-start(f32[1,2,32,512]{3,2,1,0:T(8,128)} %param.7) | copy-start | bytes 393220
  1.4 13.0 %copy-start.2 = (f32[1,2,32,512]{3,2,1,0:T(8,128)S(1)}, f32[1,2,32,512]{3,2,1,0:T(8,128)}, u32[]{:S(2)}) copy-start(f32[1,2,32,512]{3,2,1,0:T(8,128)} %param.8) | copy-start | bytes 393220
  3.4 11.1 %collective-permute-start = (f32[256,8,128]{2,1,0:T(8,128)S(1)}, f32[256,8,128]{2,1,0:T(8,128)S(1)}, u32[]{:S(2)}, u32[]{:S(2)}) collective-permute-start(f32[256,8,128]{2,1,0:T(8,128)S(1)} %get-tuple-element.8), channel_id=1, source_target_pairs={{0,32},{32,0},{1,33},{33,1},{2,34},{34,2},{3,35},{35,3},{4,36},{36... | collective-permute-start | bytes 3145736 | tf_op jit(solution)/shard_map/ppermute | solution.py:294
  15.7 17.1 %copy-start.4 = (s32[32]{0:T(128)S(1)}, s32[32]{0:T(128)}, u32[]{:S(2)}) copy-start(s32[32]{0:T(128)} %param.11) | copy-start | bytes 388
  15.7 17.5 %copy-start.3 = (s32[32,2]{0,1:T(2,128)S(1)}, s32[32,2]{0,1:T(2,128)}, u32[]{:S(2)}) copy-start(s32[32,2]{0,1:T(2,128)} %param.9) | copy-start | bytes 772
  15.7 53.1 %all-to-all-start = ((f32[256,1,1280]{2,1,0:T(1,128)}), f32[256,1,1280]{2,1,0:T(1,128)S(1)}, u32[]{:S(2)}, u32[]{:S(2)}) async-start(f32[256,1,1280]{2,1,0:T(1,128)} %bitcast.8), calls=%async_computation | async-start | bytes 2621440 | tf_op jit(solution)/shard_map/all_to_all | solution.py:297
  69.6 40.8 %copy-start.5 = (s32[64]{0:T(128)S(1)}, s32[64]{0:T(128)}, u32[]{:S(2)}) copy-start(s32[64]{0:T(128)} %param.10) | copy-start | bytes 772
  105.0 6.4 %collective-permute-start.1 = (f32[128,16,128]{2,1,0:T(8,128)S(1)}, f32[128,16,128]{2,1,0:T(8,128)S(1)}, u32[]{:S(2)}, u32[]{:S(2)}) collective-permute-start(f32[128,16,128]{2,1,0:T(8,128)S(1)} %all_to_all.10), channel_id=1, source_target_pairs={{0,32},{32,0},{1,33},{33,1},{2,34},{34,2},{3,35},{35,3},{4,36},{36... | collective-permute-start | bytes 3145736 | tf_op jit(solution)/shard_map/ppermute | solution.py:312
  118.8 6.2 %collective-permute-start.2 = (f32[32,512]{1,0:T(8,128)S(1)}, f32[32,512]{1,0:T(8,128)S(1)}, u32[]{:S(2)}, u32[]{:S(2)}) collective-permute-start(f32[32,512]{1,0:T(8,128)S(1)} %get-tuple-element.12), channel_id=1, source_target_pairs={{0,448},{64,384},{128,320},{192,256},{256,192},{320,128},{384,64},... | collective-permute-start | bytes 196616 | tf_op jit(solution)/shard_map/ppermute | solution.py:323

commit v10 on v9

--- a/solution.py
+++ b/solution.py
@@ -164,11 +164,10 @@
     return pieces
 
 
-def cut_into(out_ref, parts, value_of):
-    width = out_ref.shape[1]
-    for first in range(0, width, LANES):
-        for number, piece in enumerate(cut(value_of(first), parts)):
-            out_ref[number, pl.ds(first, LANES), :] = piece
+def cut_into(out_ref, parts, first, value):
+    rows = pl.ds(first, value.shape[0])
+    for number, piece in enumerate(cut(value, parts)):
+        out_ref[number, rows, :] = piece
 
 
 def product(left, right, parts):
@@ -183,9 +182,10 @@
 
 
 def newton_kernel(
-    core_ref, y_ref, count_ref, own_ref, other_ref, out_ref, scaled_ref, work_ref, left_ref, right_ref
+    core_ref, y_ref, count_ref, own_ref, other_ref, out_ref,
+    stat_ref, work_ref, total_ref, first_ref, second_ref, third_ref
 ):
-    width = scaled_ref.shape[0]
+    width = stat_ref.shape[0]
     columns = tile_columns(width)
     chunks = TILE
     share = width // chunks
@@ -202,31 +202,24 @@
                     for t, lanes in enumerate(columns):
                         number = (chunk * groups + group) * len(columns) + t
                         value = in_ref[pl.ds(2 * TILE * number, TILE), :]
-                        scaled_ref[rows, lanes] = value
+                        stat_ref[rows, lanes] = value
                         total = total + value * value
                         first = 2 * TILE * (TILE * group * len(columns) + t) + TILE + chunk
                         work_ref[rows, lanes] = in_ref[
                             pl.ds(first, TILE, stride=2 * TILE * len(columns)), :
                         ]
-        total = jnp.sum(jnp.sum(total, axis=0, keepdims=True), axis=1, keepdims=True)
-        inverse = 1.0 / jnp.sqrt(total + 1e-06)
-        for first in range(0, width, LANES):
-            rows = pl.ds(first, LANES)
-            scaled_ref[rows, :] = scaled_ref[rows, :] * inverse + diagonal(first, DAMPING)
-
-    def diagonal(first, value):
-        row = lax.broadcasted_iota(jnp.int32, (LANES, width), 0)
-        column = lax.broadcasted_iota(jnp.int32, (LANES, width), 1)
+        total_ref[...] = total
+
+    def diagonal(first, rows, value):
+        row = lax.broadcasted_iota(jnp.int32, (rows, width), 0)
+        column = lax.broadcasted_iota(jnp.int32, (rows, width), 1)
         return jnp.where(column == row + first, value, 0.0)
 
-    def whole_product(right):
+    def each_block(left_ref, right_ref, take):
         for first in range(0, width, step):
             rows = pl.ds(first, step)
             left = [left_ref[number, rows, :] for number in range(3)]
-            work_ref[rows, :] = product(left, lambda number: right[number], 3)
-
-    def work(first):
-        return work_ref[pl.ds(first, LANES), :]
+            take(first, product(left, lambda number: right_ref[number], 3))
 
     @pl.when(core_ref[0] == 0)
     def _():
@@ -242,21 +235,31 @@
         chosen.append(work_ref[pl.ds(first, half), :])
     chosen = jnp.concatenate(chosen, 0)
 
-    for _ in range(2):
-        cut_into(left_ref, 3, work)
-        whole_product(left_ref)
-    cut_into(left_ref, 3, work)
-    cut_into(right_ref, 3, lambda first: scaled_ref[pl.ds(first, LANES), :])
-    whole_product(right_ref)
-    cut_into(left_ref, 2, lambda first: (diagonal(first, 5.0) - work(first)) * 0.25)
-    estimate = product(cut(chosen, 2), lambda number: left_ref[number], 2)
+    for first in range(0, width, LANES):
+        cut_into(first_ref, 3, first, work_ref[pl.ds(first, LANES), :])
+    each_block(first_ref, first_ref, lambda first, value: cut_into(second_ref, 3, first, value))
+
+    total = jnp.sum(jnp.sum(total_ref[...], axis=0, keepdims=True), axis=1, keepdims=True)
+    inverse = 1.0 / jnp.sqrt(total + 1e-06)
+    for first in range(0, width, LANES):
+        value = stat_ref[pl.ds(first, LANES), :] * inverse + diagonal(first, LANES, DAMPING)
+        cut_into(third_ref, 3, first, value)
+    each_block(second_ref, second_ref, lambda first, value: cut_into(first_ref, 3, first, value))
+
+    def take_coupled(first, value):
+        work_ref[pl.ds(first, step), :] = value
+        cut_into(second_ref, 2, first, (diagonal(first, step, 5.0) - value) * 0.25)
+
+    each_block(first_ref, third_ref, take_coupled)
+    estimate = product(cut(chosen, 2), lambda number: second_ref[number], 2)
     out_ref[...] = estimate
 
     @pl.when(count_ref[0] >= 2)
     def _():
-        cut_into(right_ref, 2, work)
+        for first in range(0, width, LANES):
+            cut_into(first_ref, 2, first, work_ref[pl.ds(first, LANES), :])
         rows = estimate
-        for matrix in (left_ref, left_ref, left_ref, left_ref, right_ref):
+        for matrix in (second_ref, second_ref, second_ref, second_ref, first_ref):
             rows = product(cut(rows, 2), lambda number: matrix[number], 2)
         out_ref[...] = (5.0 * estimate - rows) * 0.25
 
@@ -271,6 +274,8 @@
         scratch_shapes=[
             pltpu.VMEM(square, jnp.float32),
             pltpu.VMEM(square, jnp.float32),
+            pltpu.VMEM((TILE, LANES), jnp.float32),
+            pltpu.VMEM((3,) + square, jnp.bfloat16),
             pltpu.VMEM((3,) + square, jnp.bfloat16),
             pltpu.VMEM((3,) + square, jnp.bfloat16),
         ],

time: 128 us -> 128 us (level)
  no operation moved by 1% of the time
where the time goes in v10:
time: 128 us; the launch traced here: 125 us
  waiting for transfers between devices  42.3 us (33%)
  blocking collectives  35.4 us (28%)
  starting transfers between devices  32 us (25%)
  Pallas kernels  11.2 us (9%)
  local copies, waits for them, and re-layouts  2.2 us (2%)
  other arithmetic  1.65 us (1%)
    all_to_all x1, waiting for transfers between devices, local(): lax.all_to_all(messages.reshape(peers, 1, -1), PLANE, 0, 0, tiled=True)  35.5 us
    all_to_all x1, blocking collectives, local(): own = lax.all_to_all(tiles, LINE, 0, 0, tiled=True)  35.4 us
    all_to_all x1, starting transfers between devices, local(): lax.all_to_all(messages.reshape(peers, 1, -1), PLANE, 0, 0, tiled=True)  17.1 us
    ppermute x1, starting transfers between devices, local(): got = lax.ppermute(sent, 'core', SWAP)  8.79 us
    pallas_call x1, Pallas kernels, newton(): pl.pallas_call(newton_kernel, out_shape=shape_of(width // TILE, width), i...  7.18 us
    ppermute x1, waiting for transfers between devices, local(): root_got = lax.ppermute(root_rows[half:], ('yh', 'yl'), pairs)  4.29 us
    ppermute x1, starting transfers between devices, local(): other = lax.ppermute(own, 'core', SWAP)  4.12 us
  transfers between devices with their start and end apart: 4, of which 4 were waited for; matrix products, arithmetic and copies ran while one was open for 1% of the time, Pallas kernels for 0%

profile of v10, /device:TPU:1, one launch (start us, length us, event | category | flops | bytes accessed | tf_op | source)
XLA Modules:
  0.0 125.5 jit_solution(2621594824358104973)
XLA Ops:
  0.0 0.0 copy-start
  0.0 1.4 %copy-done = bf16[3,1,512,512]{3,2,1,0:T(8,128)(2,1)S(1)} copy-done((bf16[3,1,512,512]{3,2,1,0:T(8,128)(2,1)S(1)}, bf16[3,1,512,512]{3,2,1,0:T(8,128)(2,1)}, u32[]{:S(2)}) %copy-start) | copy-done | bytes 1572888
  1.4 0.0 copy-start.1
  1.4 0.0 copy-start.2
  1.4 1.9 %shard_map.64 = (f32[256,8,128]{2,1,0:T(8,128)S(1)}, f32[256,8,128]{2,1,0:T(8,128)S(1)}) custom-call(s32[1]{0:T(128)} %bitcast.refs_0_.core_ref, bf16[3,512,512]{2,1,0:T(8,128)(2,1)S(1)} %bitcast.17), custom_call_target="tpu_custom_call" | custom-call | tf_op jit(solution)/shard_map/pallas_call | solution.py:71
  3.4 8.8 %collective-permute-start = (f32[256,8,128]{2,1,0:T(8,128)S(1)}, f32[256,8,128]{2,1,0:T(8,128)S(1)}, u32[]{:S(2)}, u32[]{:S(2)}) collective-permute-start(f32[256,8,128]{2,1,0:T(8,128)S(1)} %get-tuple-element.8), channel_id=1, source_target_pairs={{0,32},{32,0},{1,33},{33,1},{2,34},{34,2},{3,35},{35,3},{4,36},{36... | collective-permute-start | bytes 3145736 | tf_op jit(solution)/shard_map/ppermute | solution.py:299
  12.2 2.3 %collective-permute-done.got_ref = f32[256,8,128]{2,1,0:T(8,128)S(1)} collective-permute-done((f32[256,8,128]{2,1,0:T(8,128)S(1)}, f32[256,8,128]{2,1,0:T(8,128)S(1)}, u32[]{:S(2)}, u32[]{:S(2)}) %collective-permute-start) | collective-permute-done | bytes 1048608 | tf_op jit(solution)/shard_map/ppermute | solution.py:299
  14.4 0.0 copy-done.1
  14.4 0.0 copy-done.2
  14.4 1.2 shard_map.65
  15.7 0.0 copy-start.4
  15.7 0.0 copy-start.3
  15.7 17.1 %all-to-all-start = ((f32[256,1,1280]{2,1,0:T(1,128)}), f32[256,1,1280]{2,1,0:T(1,128)S(1)}, u32[]{:S(2)}, u32[]{:S(2)}) async-start(f32[256,1,1280]{2,1,0:T(1,128)} %bitcast.8), calls=%async_computation | async-start | bytes 2621440 | tf_op jit(solution)/shard_map/all_to_all | solution.py:302
  32.8 0.0 copy-done.4
  32.8 0.1 select_reduce_fusion.block_ref
  32.9 0.1 iota_add_fusion
  33.0 0.1 add.39
  33.1 0.0 copy-done.3
  33.1 0.1 fusion.1
  33.2 35.5 %all-to-all-done = f32[256,1,1280]{2,1,0:T(1,128)S(1)} async-done(((f32[256,1,1280]{2,1,0:T(1,128)}), f32[256,1,1280]{2,1,0:T(1,128)S(1)}, u32[]{:S(2)}, u32[]{:S(2)}) %all-to-all-start) | async-done | bytes 1310752 | tf_op jit(solution)/shard_map/all_to_all | solution.py:302
  68.8 0.8 shard_map.66
  69.6 0.0 copy-start.5
  69.6 35.4 %all_to_all.10 = f32[128,16,128]{2,1,0:T(8,128)S(1)} all-to-all(f32[128,16,128]{2,1,0:T(8,128)S(1)} %shard_map.66), channel_id=1, replica_groups=mesh['yh'=2,'yl'=4,'core'=2,'x'=4,'z'=8] {'yl','x','z'}, dimensions={0} | all-to-all | bytes 2097152 | tf_op jit(solution)/shard_map/all_to_all | solution.py:316
  105.0 4.1 %collective-permute-start.1 = (f32[128,16,128]{2,1,0:T(8,128)S(1)}, f32[128,16,128]{2,1,0:T(8,128)S(1)}, u32[]{:S(2)}, u32[]{:S(2)}) collective-permute-start(f32[128,16,128]{2,1,0:T(8,128)S(1)} %all_to_all.10), channel_id=1, source_target_pairs={{0,32},{32,0},{1,33},{33,1},{2,34},{34,2},{3,35},{35,3},{4,36},{36... | collective-permute-start | bytes 3145736 | tf_op jit(solution)/shard_map/ppermute | solution.py:317
  109.1 0.7 dynamic_slice.3
  110.4 0.0 copy-done.5
  110.4 0.7 fusion.2
  111.1 0.3 collective-permute-done.1
  111.4 7.2 %shard_map.67 = f32[64,512]{1,0:T(8,128)S(1)} custom-call(s32[1]{0:T(128)} %bitcast.refs_0_.core_ref, s32[1]{0:T(128)} %bitcast.1.y_ref, s32[1]{0:T(128)} %bitcast.3.count_ref, f32[2048,128]{1,0:T(8,128)S(1)} %bitcast.16, f32[2048,128]{1,0:T(8,128)S(1)} %bitcast.18), custom_call_target="tpu_custom_call" | custom-call | tf_op jit(solution)/shard_map/pallas_call | solution.py:269
  118.6 1.9 %collective-permute-start.2 = (f32[32,512]{1,0:T(8,128)S(1)}, f32[32,512]{1,0:T(8,128)S(1)}, u32[]{:S(2)}, u32[]{:S(2)}) collective-permute-start(f32[32,512]{1,0:T(8,128)S(1)} %get-tuple-element.12), channel_id=1, source_target_pairs={{0,448},{64,384},{128,320},{192,256},{256,192},{320,128},{384,64},... | collective-permute-start | bytes 196616 | tf_op jit(solution)/shard_map/ppermute | solution.py:328
  120.5 4.3 %collective-permute-done.2 = f32[32,512]{1,0:T(8,128)S(1)} collective-permute-done((f32[32,512]{1,0:T(8,128)S(1)}, f32[32,512]{1,0:T(8,128)S(1)}, u32[]{:S(2)}, u32[]{:S(2)}) %collective-permute-start.2) | collective-permute-done | bytes 65568 | tf_op jit(solution)/shard_map/ppermute | solution.py:328
  124.8 0.7 maximum_select_fusion
  (2 shorter events, 0.0 us)
Async XLA Ops:
  0.0 1.4 %copy-start = (bf16[3,1,512,512]{3,2,1,0:T(8,128)(2,1)S(1)}, bf16[3,1,512,512]{3,2,1,0:T(8,128)(2,1)}, u32[]{:S(2)}) copy-start(bf16[3,1,512,512]{3,2,1,0:T(8,128)(2,1)} %param.6) | copy-start | bytes 4718596
  1.4 13.0 %copy-start.1 = (f32[1,2,32,512]{3,2,1,0:T(8,128)S(1)}, f32[1,2,32,512]{3,2,1,0:T(8,128)}, u32[]{:S(2)}) copy-start(f32[1,2,32,512]{3,2,1,0:T(8,128)} %param.7) | copy-start | bytes 393220
  1.4 13.0 %copy-start.2 = (f32[1,2,32,512]{3,2,1,0:T(8,128)S(1)}, f32[1,2,32,512]{3,2,1,0:T(8,128)}, u32[]{:S(2)}) copy-start(f32[1,2,32,512]{3,2,1,0:T(8,128)} %param.8) | copy-start | bytes 393220
  3.4 11.1 %collective-permute-start = (f32[256,8,128]{2,1,0:T(8,128)S(1)}, f32[256,8,128]{2,1,0:T(8,128)S(1)}, u32[]{:S(2)}, u32[]{:S(2)}) collective-permute-start(f32[256,8,128]{2,1,0:T(8,128)S(1)} %get-tuple-element.8), channel_id=1, source_target_pairs={{0,32},{32,0},{1,33},{33,1},{2,34},{34,2},{3,35},{35,3},{4,36},{36... | collective-permute-start | bytes 3145736 | tf_op jit(solution)/shard_map/ppermute | solution.py:299
  15.7 17.1 %copy-start.4 = (s32[32]{0:T(128)S(1)}, s32[32]{0:T(128)}, u32[]{:S(2)}) copy-start(s32[32]{0:T(128)} %param.11) | copy-start | bytes 388
  15.7 17.5 %copy-start.3 = (s32[32,2]{0,1:T(2,128)S(1)}, s32[32,2]{0,1:T(2,128)}, u32[]{:S(2)}) copy-start(s32[32,2]{0,1:T(2,128)} %param.9) | copy-start | bytes 772
  15.7 53.1 %all-to-all-start = ((f32[256,1,1280]{2,1,0:T(1,128)}), f32[256,1,1280]{2,1,0:T(1,128)S(1)}, u32[]{:S(2)}, u32[]{:S(2)}) async-start(f32[256,1,1280]{2,1,0:T(1,128)} %bitcast.8), calls=%async_computation | async-start | bytes 2621440 | tf_op jit(solution)/shard_map/all_to_all | solution.py:302
  69.6 40.8 %copy-start.5 = (s32[64]{0:T(128)S(1)}, s32[64]{0:T(128)}, u32[]{:S(2)}) copy-start(s32[64]{0:T(128)} %param.10) | copy-start | bytes 772
  105.0 6.4 %collective-permute-start.1 = (f32[128,16,128]{2,1,0:T(8,128)S(1)}, f32[128,16,128]{2,1,0:T(8,128)S(1)}, u32[]{:S(2)}, u32[]{:S(2)}) collective-permute-start(f32[128,16,128]{2,1,0:T(8,128)S(1)} %all_to_all.10), channel_id=1, source_target_pairs={{0,32},{32,0},{1,33},{33,1},{2,34},{34,2},{3,35},{35,3},{4,36},{36... | collective-permute-start | bytes 3145736 | tf_op jit(solution)/shard_map/ppermute | solution.py:317
  118.6 6.2 %collective-permute-start.2 = (f32[32,512]{1,0:T(8,128)S(1)}, f32[32,512]{1,0:T(8,128)S(1)}, u32[]{:S(2)}, u32[]{:S(2)}) collective-permute-start(f32[32,512]{1,0:T(8,128)S(1)} %get-tuple-element.12), channel_id=1, source_target_pairs={{0,448},{64,384},{128,320},{192,256},{256,192},{320,128},{384,64},... | collective-permute-start | bytes 196616 | tf_op jit(solution)/shard_map/ppermute | solution.py:328

commit v11 on v10

--- a/solution.py
+++ b/solution.py
@@ -164,26 +164,34 @@
     return pieces
 
 
-def cut_into(out_ref, parts, first, value):
-    rows = pl.ds(first, value.shape[0])
+def cut_left(out_ref, parts, first, value):
+    rows, width = value.shape
     for number, piece in enumerate(cut(value, parts)):
-        out_ref[number, rows, :] = piece
-
-
-def product(left, right, parts):
+        out_ref[pl.ds(first, rows), pl.ds(width * number, width)] = piece
+
+
+def cut_right(out_ref, parts, first, value):
+    rows, width = value.shape
+    for number, piece in enumerate(cut(value, parts)):
+        out_ref[pl.ds(width * (parts - 1 - number) + first, rows), :] = piece
+
+
+def product(left_of, right_ref, parts):
+    width = right_ref.shape[1]
     total = None
-    for order in reversed(range(parts)):
-        for number in range(order + 1):
-            term = jnp.dot(
-                left[number], right(order - number), preferred_element_type=jnp.float32
-            )
-            total = term if total is None else total + term
+    for count in reversed(range(1, parts + 1)):
+        term = jnp.dot(
+            left_of(width * count),
+            right_ref[pl.ds(width * (parts - count), width * count), :],
+            preferred_element_type=jnp.float32,
+        )
+        total = term if total is None else total + term
     return total
 
 
 def newton_kernel(
     core_ref, y_ref, count_ref, own_ref, other_ref, out_ref,
-    stat_ref, work_ref, total_ref, first_ref, second_ref, third_ref
+    stat_ref, work_ref, total_ref, left_ref, next_ref, right_ref, square_ref, scaled_ref
 ):
     width = stat_ref.shape[0]
     columns = tile_columns(width)
@@ -218,8 +226,11 @@
     def each_block(left_ref, right_ref, take):
         for first in range(0, width, step):
             rows = pl.ds(first, step)
-            left = [left_ref[number, rows, :] for number in range(3)]
-            take(first, product(left, lambda number: right_ref[number], 3))
+            take(first, product(lambda terms: left_ref[rows, pl.ds(0, terms)], right_ref, 3))
+
+    def row_product(rows, right_ref):
+        pieces = jnp.concatenate(cut(rows, 2), 1)
+        return product(lambda terms: pieces[:, :terms], right_ref, 2)
 
     @pl.when(core_ref[0] == 0)
     def _():
@@ -236,31 +247,40 @@
     chosen = jnp.concatenate(chosen, 0)
 
     for first in range(0, width, LANES):
-        cut_into(first_ref, 3, first, work_ref[pl.ds(first, LANES), :])
-    each_block(first_ref, first_ref, lambda first, value: cut_into(second_ref, 3, first, value))
+        value = work_ref[pl.ds(first, LANES), :]
+        cut_left(left_ref, 3, first, value)
+        cut_right(right_ref, 3, first, value)
+
+    def take_square(first, value):
+        cut_left(next_ref, 3, first, value)
+        cut_right(square_ref, 3, first, value)
+
+    each_block(left_ref, right_ref, take_square)
 
     total = jnp.sum(jnp.sum(total_ref[...], axis=0, keepdims=True), axis=1, keepdims=True)
     inverse = 1.0 / jnp.sqrt(total + 1e-06)
     for first in range(0, width, LANES):
         value = stat_ref[pl.ds(first, LANES), :] * inverse + diagonal(first, LANES, DAMPING)
-        cut_into(third_ref, 3, first, value)
-    each_block(second_ref, second_ref, lambda first, value: cut_into(first_ref, 3, first, value))
+        cut_right(scaled_ref, 3, first, value)
+    each_block(next_ref, square_ref, lambda first, value: cut_left(left_ref, 3, first, value))
 
     def take_coupled(first, value):
         work_ref[pl.ds(first, step), :] = value
-        cut_into(second_ref, 2, first, (diagonal(first, step, 5.0) - value) * 0.25)
-
-    each_block(first_ref, third_ref, take_coupled)
-    estimate = product(cut(chosen, 2), lambda number: second_ref[number], 2)
+        cut_right(right_ref, 2, first, (diagonal(first, step, 5.0) - value) * 0.25)
+
+    each_block(left_ref, scaled_ref, take_coupled)
+    factor_ref = right_ref.at[pl.ds(0, 2 * width)]
+    estimate = row_product(chosen, factor_ref)
     out_ref[...] = estimate
 
     @pl.when(count_ref[0] >= 2)
     def _():
         for first in range(0, width, LANES):
-            cut_into(first_ref, 2, first, work_ref[pl.ds(first, LANES), :])
+            cut_right(square_ref, 2, first, work_ref[pl.ds(first, LANES), :])
+        coupled_ref = square_ref.at[pl.ds(0, 2 * width)]
         rows = estimate
-        for matrix in (second_ref, second_ref, second_ref, second_ref, first_ref):
-            rows = product(cut(rows, 2), lambda number: matrix[number], 2)
+        for matrix in (factor_ref, factor_ref, factor_ref, factor_ref, coupled_ref):
+            rows = row_product(rows, matrix)
         out_ref[...] = (5.0 * estimate - rows) * 0.25
 
 
@@ -275,11 +295,13 @@
             pltpu.VMEM(square, jnp.float32),
             pltpu.VMEM(square, jnp.float32),
             pltpu.VMEM((TILE, LANES), jnp.float32),
-            pltpu.VMEM((3,) + square, jnp.bfloat16),
-            pltpu.VMEM((3,) + square, jnp.bfloat16),
-            pltpu.VMEM((3,) + square, jnp.bfloat16),
+            pltpu.VMEM((width, 3 * width), jnp.bfloat16),
+            pltpu.VMEM((width, 3 * width), jnp.bfloat16),
+            pltpu.VMEM((3 * width, width), jnp.bfloat16),
+            pltpu.VMEM((3 * width, width), jnp.bfloat16),
+            pltpu.VMEM((3 * width, width), jnp.bfloat16),
         ],
-        compiler_params=pltpu.CompilerParams(vmem_limit_bytes=14 * 1024 * 1024),
+        compiler_params=pltpu.CompilerParams(vmem_limit_bytes=16 * 1024 * 1024),
     )(core, y, count, own, other)
 
 

time: 128 us -> 127 us (level)
  no operation moved by 1% of the time
where the time goes in v11:
time: 127 us; the launch traced here: 125 us
  waiting for transfers between devices  42.3 us (33%)
  blocking collectives  35.4 us (28%)
  starting transfers between devices  32 us (25%)
  Pallas kernels  11.2 us (9%)
  local copies, waits for them, and re-layouts  2.2 us (2%)
  other arithmetic  1.65 us (1%)
    all_to_all x1, waiting for transfers between devices, local(): lax.all_to_all(messages.reshape(peers, 1, -1), PLANE, 0, 0, tiled=True)  35.5 us
    all_to_all x1, blocking collectives, local(): own = lax.all_to_all(tiles, LINE, 0, 0, tiled=True)  35.4 us
    all_to_all x1, starting transfers between devices, local(): lax.all_to_all(messages.reshape(peers, 1, -1), PLANE, 0, 0, tiled=True)  17.1 us
    ppermute x1, starting transfers between devices, local(): got = lax.ppermute(sent, 'core', SWAP)  8.79 us
    pallas_call x1, Pallas kernels, newton(): pl.pallas_call(newton_kernel, out_shape=shape_of(width // TILE, width), i...  7.12 us
    ppermute x1, waiting for transfers between devices, local(): root_got = lax.ppermute(root_rows[half:], ('yh', 'yl'), pairs)  4.29 us
    ppermute x1, starting transfers between devices, local(): other = lax.ppermute(own, 'core', SWAP)  4.12 us
  transfers between devices with their start and end apart: 4, of which 4 were waited for; matrix products, arithmetic and copies ran while one was open for 1% of the time, Pallas kernels for 0%

profile of v11, /device:TPU:1, one launch (start us, length us, event | category | flops | bytes accessed | tf_op | source)
XLA Modules:
  0.0 125.4 jit_solution(16566614206837519408)
XLA Ops:
  0.0 0.0 copy-start
  0.0 1.4 %copy-done = bf16[3,1,512,512]{3,2,1,0:T(8,128)(2,1)S(1)} copy-done((bf16[3,1,512,512]{3,2,1,0:T(8,128)(2,1)S(1)}, bf16[3,1,512,512]{3,2,1,0:T(8,128)(2,1)}, u32[]{:S(2)}) %copy-start) | copy-done | bytes 1572888
  1.4 0.0 copy-start.1
  1.4 0.0 copy-start.2
  1.4 1.9 %shard_map.64 = (f32[256,8,128]{2,1,0:T(8,128)S(1)}, f32[256,8,128]{2,1,0:T(8,128)S(1)}) custom-call(s32[1]{0:T(128)} %bitcast.refs_0_.core_ref, bf16[3,512,512]{2,1,0:T(8,128)(2,1)S(1)} %bitcast.17), custom_call_target="tpu_custom_call" | custom-call | tf_op jit(solution)/shard_map/pallas_call | solution.py:71
  3.4 8.8 %collective-permute-start = (f32[256,8,128]{2,1,0:T(8,128)S(1)}, f32[256,8,128]{2,1,0:T(8,128)S(1)}, u32[]{:S(2)}, u32[]{:S(2)}) collective-permute-start(f32[256,8,128]{2,1,0:T(8,128)S(1)} %get-tuple-element.8), channel_id=1, source_target_pairs={{0,32},{32,0},{1,33},{33,1},{2,34},{34,2},{3,35},{35,3},{4,36},{36... | collective-permute-start | bytes 3145736 | tf_op jit(solution)/shard_map/ppermute | solution.py:321
  12.2 2.3 %collective-permute-done.got_ref = f32[256,8,128]{2,1,0:T(8,128)S(1)} collective-permute-done((f32[256,8,128]{2,1,0:T(8,128)S(1)}, f32[256,8,128]{2,1,0:T(8,128)S(1)}, u32[]{:S(2)}, u32[]{:S(2)}) %collective-permute-start) | collective-permute-done | bytes 1048608 | tf_op jit(solution)/shard_map/ppermute | solution.py:321
  14.4 0.0 copy-done.1
  14.4 0.0 copy-done.2
  14.4 1.2 shard_map.65
  15.7 0.0 copy-start.4
  15.7 0.0 copy-start.3
  15.7 17.1 %all-to-all-start = ((f32[256,1,1280]{2,1,0:T(1,128)}), f32[256,1,1280]{2,1,0:T(1,128)S(1)}, u32[]{:S(2)}, u32[]{:S(2)}) async-start(f32[256,1,1280]{2,1,0:T(1,128)} %bitcast.8), calls=%async_computation | async-start | bytes 2621440 | tf_op jit(solution)/shard_map/all_to_all | solution.py:324
  32.8 0.0 copy-done.4
  32.8 0.1 select_reduce_fusion.block_ref
  32.9 0.1 iota_add_fusion
  33.0 0.1 add.39
  33.1 0.0 copy-done.3
  33.1 0.1 fusion.1
  33.2 35.5 %all-to-all-done = f32[256,1,1280]{2,1,0:T(1,128)S(1)} async-done(((f32[256,1,1280]{2,1,0:T(1,128)}), f32[256,1,1280]{2,1,0:T(1,128)S(1)}, u32[]{:S(2)}, u32[]{:S(2)}) %all-to-all-start) | async-done | bytes 1310752 | tf_op jit(solution)/shard_map/all_to_all | solution.py:324
  68.8 0.8 shard_map.66
  69.6 0.0 copy-start.5
  69.6 35.4 %all_to_all.10 = f32[128,16,128]{2,1,0:T(8,128)S(1)} all-to-all(f32[128,16,128]{2,1,0:T(8,128)S(1)} %shard_map.66), channel_id=1, replica_groups=mesh['yh'=2,'yl'=4,'core'=2,'x'=4,'z'=8] {'yl','x','z'}, dimensions={0} | all-to-all | bytes 2097152 | tf_op jit(solution)/shard_map/all_to_all | solution.py:338
  105.0 4.1 %collective-permute-start.1 = (f32[128,16,128]{2,1,0:T(8,128)S(1)}, f32[128,16,128]{2,1,0:T(8,128)S(1)}, u32[]{:S(2)}, u32[]{:S(2)}) collective-permute-start(f32[128,16,128]{2,1,0:T(8,128)S(1)} %all_to_all.10), channel_id=1, source_target_pairs={{0,32},{32,0},{1,33},{33,1},{2,34},{34,2},{3,35},{35,3},{4,36},{36... | collective-permute-start | bytes 3145736 | tf_op jit(solution)/shard_map/ppermute | solution.py:339
  109.1 0.7 dynamic_slice.3
  110.4 0.0 copy-done.5
  110.4 0.7 fusion.2
  111.1 0.3 collective-permute-done.1
  111.4 7.1 %shard_map.67 = f32[64,512]{1,0:T(8,128)S(1)} custom-call(s32[1]{0:T(128)} %bitcast.refs_0_.core_ref, s32[1]{0:T(128)} %bitcast.1.y_ref, s32[1]{0:T(128)} %bitcast.3.count_ref, f32[2048,128]{1,0:T(8,128)S(1)} %bitcast.16, f32[2048,128]{1,0:T(8,128)S(1)} %bitcast.18), custom_call_target="tpu_custom_call" | custom-call | tf_op jit(solution)/shard_map/pallas_call | solution.py:289
  118.5 1.9 %collective-permute-start.2 = (f32[32,512]{1,0:T(8,128)S(1)}, f32[32,512]{1,0:T(8,128)S(1)}, u32[]{:S(2)}, u32[]{:S(2)}) collective-permute-start(f32[32,512]{1,0:T(8,128)S(1)} %get-tuple-element.12), channel_id=1, source_target_pairs={{0,448},{64,384},{128,320},{192,256},{256,192},{320,128},{384,64},... | collective-permute-start | bytes 196616 | tf_op jit(solution)/shard_map/ppermute | solution.py:350
  120.5 4.3 %collective-permute-done.2 = f32[32,512]{1,0:T(8,128)S(1)} collective-permute-done((f32[32,512]{1,0:T(8,128)S(1)}, f32[32,512]{1,0:T(8,128)S(1)}, u32[]{:S(2)}, u32[]{:S(2)}) %collective-permute-start.2) | collective-permute-done | bytes 65568 | tf_op jit(solution)/shard_map/ppermute | solution.py:350
  124.8 0.7 maximum_select_fusion
  (2 shorter events, 0.0 us)
Async XLA Ops:
  0.0 1.4 %copy-start = (bf16[3,1,512,512]{3,2,1,0:T(8,128)(2,1)S(1)}, bf16[3,1,512,512]{3,2,1,0:T(8,128)(2,1)}, u32[]{:S(2)}) copy-start(bf16[3,1,512,512]{3,2,1,0:T(8,128)(2,1)} %param.6) | copy-start | bytes 4718596
  1.4 13.0 %copy-start.1 = (f32[1,2,32,512]{3,2,1,0:T(8,128)S(1)}, f32[1,2,32,512]{3,2,1,0:T(8,128)}, u32[]{:S(2)}) copy-start(f32[1,2,32,512]{3,2,1,0:T(8,128)} %param.7) | copy-start | bytes 393220
  1.4 13.0 %copy-start.2 = (f32[1,2,32,512]{3,2,1,0:T(8,128)S(1)}, f32[1,2,32,512]{3,2,1,0:T(8,128)}, u32[]{:S(2)}) copy-start(f32[1,2,32,512]{3,2,1,0:T(8,128)} %param.8) | copy-start | bytes 393220
  3.4 11.1 %collective-permute-start = (f32[256,8,128]{2,1,0:T(8,128)S(1)}, f32[256,8,128]{2,1,0:T(8,128)S(1)}, u32[]{:S(2)}, u32[]{:S(2)}) collective-permute-start(f32[256,8,128]{2,1,0:T(8,128)S(1)} %get-tuple-element.8), channel_id=1, source_target_pairs={{0,32},{32,0},{1,33},{33,1},{2,34},{34,2},{3,35},{35,3},{4,36},{36... | collective-permute-start | bytes 3145736 | tf_op jit(solution)/shard_map/ppermute | solution.py:321
  15.7 17.1 %copy-start.4 = (s32[32]{0:T(128)S(1)}, s32[32]{0:T(128)}, u32[]{:S(2)}) copy-start(s32[32]{0:T(128)} %param.11) | copy-start | bytes 388
  15.7 17.5 %copy-start.3 = (s32[32,2]{0,1:T(2,128)S(1)}, s32[32,2]{0,1:T(2,128)}, u32[]{:S(2)}) copy-start(s32[32,2]{0,1:T(2,128)} %param.9) | copy-start | bytes 772
  15.7 53.1 %all-to-all-start = ((f32[256,1,1280]{2,1,0:T(1,128)}), f32[256,1,1280]{2,1,0:T(1,128)S(1)}, u32[]{:S(2)}, u32[]{:S(2)}) async-start(f32[256,1,1280]{2,1,0:T(1,128)} %bitcast.8), calls=%async_computation | async-start | bytes 2621440 | tf_op jit(solution)/shard_map/all_to_all | solution.py:324
  69.6 40.8 %copy-start.5 = (s32[64]{0:T(128)S(1)}, s32[64]{0:T(128)}, u32[]{:S(2)}) copy-start(s32[64]{0:T(128)} %param.10) | copy-start | bytes 772
  105.0 6.4 %collective-permute-start.1 = (f32[128,16,128]{2,1,0:T(8,128)S(1)}, f32[128,16,128]{2,1,0:T(8,128)S(1)}, u32[]{:S(2)}, u32[]{:S(2)}) collective-permute-start(f32[128,16,128]{2,1,0:T(8,128)S(1)} %all_to_all.10), channel_id=1, source_target_pairs={{0,32},{32,0},{1,33},{33,1},{2,34},{34,2},{3,35},{35,3},{4,36},{36... | collective-permute-start | bytes 3145736 | tf_op jit(solution)/shard_map/ppermute | solution.py:339
  118.5 6.2 %collective-permute-start.2 = (f32[32,512]{1,0:T(8,128)S(1)}, f32[32,512]{1,0:T(8,128)S(1)}, u32[]{:S(2)}, u32[]{:S(2)}) collective-permute-start(f32[32,512]{1,0:T(8,128)S(1)} %get-tuple-element.12), channel_id=1, source_target_pairs={{0,448},{64,384},{128,320},{192,256},{256,192},{320,128},{384,64},... | collective-permute-start | bytes 196616 | tf_op jit(solution)/shard_map/ppermute | solution.py:350

commit v12 on v11

--- a/solution.py
+++ b/solution.py
@@ -8,8 +8,8 @@
 HISTORY = 0.5
 DAMPING = 0.001
 WORKER = ("x", "z")
-PLANE = ("yh", "yl", "x", "z")
-LINE = ("yl", "x", "z")
+PLANE = ("yh", "yl", "z", "x")
+LINE = ("yl", "z", "x")
 SWAP = [(0, 1), (1, 0)]
 LANES = 128
 TILE = 8
@@ -332,8 +332,19 @@
     mine = jnp.arange(counts.shape[0], dtype=jnp.int32) == 2 * blocks[worker] + kind
     iterations = jnp.sum(jnp.where(mine, counts, 0)).reshape(1)
 
+    x_count, z_count = lax.axis_size("x"), lax.axis_size("z")
+
+    def place_of(number):
+        return number % z_count * x_count + number // z_count
+
+    def in_place(values):
+        return values.reshape(x_count, z_count, -1).transpose(1, 0, 2).reshape(-1)
+
+    block_places = in_place(place_of(blocks))
+    owner_places = in_place(place_of(owners))
+
     tiles = deliver(
-        kind.reshape(1), blocks, owners, slots, arrived.reshape(messages.shape)
+        kind.reshape(1), block_places, owner_places, in_place(slots), arrived.reshape(messages.shape)
     )
     own = lax.all_to_all(tiles, LINE, 0, 0, tiled=True)
     other = lax.ppermute(own, "core", SWAP)

time: 127 us -> 129 us (1.016)
  the two profiles are of different devices: /device:TPU:1 before, /device:TPU:2 now
where the time goes in v12:
time: 129 us
  waiting for transfers between devices  45.4 us (35%)
  blocking collectives  37.9 us (29%)
  starting transfers between devices  27.3 us (21%)
  Pallas kernels  12.9 us (10%)
  local copies, waits for them, and re-layouts  2.87 us (2%)
  other arithmetic  1.68 us (1%)
    all_to_all x1, blocking collectives, local(): own = lax.all_to_all(tiles, LINE, 0, 0, tiled=True)  37.9 us
    all_to_all x1, waiting for transfers between devices, local(): lax.all_to_all(messages.reshape(peers, 1, -1), PLANE, 0, 0, tiled=True)  35.4 us
    all_to_all x1, starting transfers between devices, local(): lax.all_to_all(messages.reshape(peers, 1, -1), PLANE, 0, 0, tiled=True)  21.6 us
    pallas_call x1, Pallas kernels, newton(): pl.pallas_call(newton_kernel, out_shape=shape_of(width // TILE, width), i...  8.92 us
    ppermute x1, waiting for transfers between devices, local(): root_got = lax.ppermute(root_rows[half:], ('yh', 'yl'), pairs)  6.82 us
    ppermute x1, waiting for transfers between devices, local(): got = lax.ppermute(sent, 'core', SWAP)  2.62 us
  transfers between devices with their start and end apart: 4, of which 4 were waited for; matrix products, arithmetic and copies ran while one was open for 2% of the time, Pallas kernels for 0%

profile of v12, /device:TPU:2, one launch (start us, length us, event | category | flops | bytes accessed | tf_op | source)
XLA Modules:
  0.0 128.9 jit_solution(4186410138353205720)
XLA Ops:
  0.0 0.0 copy-start
  0.0 1.4 %copy-done = bf16[3,1,512,512]{3,2,1,0:T(8,128)(2,1)S(1)} copy-done((bf16[3,1,512,512]{3,2,1,0:T(8,128)(2,1)S(1)}, bf16[3,1,512,512]{3,2,1,0:T(8,128)(2,1)}, u32[]{:S(2)}) %copy-start) | copy-done | bytes 1572888
  1.4 0.0 copy-start.1
  1.4 0.0 copy-start.2
  1.4 2.0 %shard_map.64 = (f32[256,8,128]{2,1,0:T(8,128)S(1)}, f32[256,8,128]{2,1,0:T(8,128)S(1)}) custom-call(s32[1]{0:T(128)} %bitcast.refs_0_.core_ref, bf16[3,512,512]{2,1,0:T(8,128)(2,1)S(1)} %bitcast.24), custom_call_target="tpu_custom_call" | custom-call | tf_op jit(solution)/shard_map/pallas_call | solution.py:71
  3.4 1.9 %collective-permute-start = (f32[256,8,128]{2,1,0:T(8,128)S(1)}, f32[256,8,128]{2,1,0:T(8,128)S(1)}, u32[]{:S(2)}, u32[]{:S(2)}) collective-permute-start(f32[256,8,128]{2,1,0:T(8,128)S(1)} %get-tuple-element.8), channel_id=1, source_target_pairs={{0,32},{32,0},{1,33},{33,1},{2,34},{34,2},{3,35},{35,3},{4,36},{36... | collective-permute-start | bytes 3145736 | tf_op jit(solution)/shard_map/ppermute | solution.py:321
  5.3 2.6 %collective-permute-done.got_ref = f32[256,8,128]{2,1,0:T(8,128)S(1)} collective-permute-done((f32[256,8,128]{2,1,0:T(8,128)S(1)}, f32[256,8,128]{2,1,0:T(8,128)S(1)}, u32[]{:S(2)}, u32[]{:S(2)}) %collective-permute-start) | collective-permute-done | bytes 1048608 | tf_op jit(solution)/shard_map/ppermute | solution.py:321
  7.9 0.0 copy-done.1
  7.9 0.0 copy-done.2
  7.9 1.2 shard_map.65
  9.2 0.0 copy-start.4
  9.2 0.0 copy-start.3
  9.2 21.6 %all-to-all-start = ((f32[256,1,1280]{2,1,0:T(1,128)}), f32[256,1,1280]{2,1,0:T(1,128)S(1)}, u32[]{:S(2)}, u32[]{:S(2)}) async-start(f32[256,1,1280]{2,1,0:T(1,128)} %bitcast.11), calls=%async_computation | async-start | bytes 2621440 | tf_op jit(solution)/shard_map/all_to_all | solution.py:324
  30.7 0.0 copy-done.4
  30.7 0.1 select_reduce_fusion
  30.9 0.1 reduce_sum.42
  30.9 0.1 iota_add_fusion
  31.0 0.1 add.85
  31.1 0.0 copy-done.3
  31.1 0.1 fusion.1
  31.2 0.1 reduce_sum.44
  31.4 0.1 reshape.228.owner_ref
  31.5 0.1 reshape.229
  31.6 0.1 reshape.230.slot_ref
  31.7 0.1 copy.20
  31.8 0.1 reshape.227.block_ref
  31.9 35.4 %all-to-all-done = f32[256,1,1280]{2,1,0:T(1,128)S(1)} async-done(((f32[256,1,1280]{2,1,0:T(1,128)}), f32[256,1,1280]{2,1,0:T(1,128)S(1)}, u32[]{:S(2)}, u32[]{:S(2)}) %all-to-all-start) | async-done | bytes 1310752 | tf_op jit(solution)/shard_map/all_to_all | solution.py:324
  67.3 0.8 shard_map.66
  68.1 0.0 copy-start.5
  68.1 37.9 %all_to_all.10 = f32[128,16,128]{2,1,0:T(8,128)S(1)} all-to-all(f32[128,16,128]{2,1,0:T(8,128)S(1)} %shard_map.66), channel_id=1, replica_groups=mesh['yh'=2,'yl'=4,'core'=2,'x'=4,'z'=8] {'yl','z','x'}, dimensions={0} | all-to-all | bytes 2097152 | tf_op jit(solution)/shard_map/all_to_all | solution.py:349
  106.0 1.9 %collective-permute-start.1 = (f32[128,16,128]{2,1,0:T(8,128)S(1)}, f32[128,16,128]{2,1,0:T(8,128)S(1)}, u32[]{:S(2)}, u32[]{:S(2)}) collective-permute-start(f32[128,16,128]{2,1,0:T(8,128)S(1)} %all_to_all.10), channel_id=1, source_target_pairs={{0,32},{32,0},{1,33},{33,1},{2,34},{34,2},{3,35},{35,3},{4,36},{36... | collective-permute-start | bytes 3145736 | tf_op jit(solution)/shard_map/ppermute | solution.py:350
  107.9 0.7 dynamic_slice.3
  109.2 0.0 copy-done.5
  109.2 0.7 fusion.14
  109.9 0.6 collective-permute-done.1
  110.6 8.9 %shard_map.67 = f32[64,512]{1,0:T(8,128)S(1)} custom-call(s32[1]{0:T(128)} %bitcast.refs_0_.core_ref, s32[1]{0:T(128)} %bitcast.1.y_ref, s32[1]{0:T(128)} %bitcast.3.count_ref, f32[2048,128]{1,0:T(8,128)S(1)} %bitcast.23, f32[2048,128]{1,0:T(8,128)S(1)} %bitcast.25), custom_call_target="tpu_custom_call" | custom-call | tf_op jit(solution)/shard_map/pallas_call | solution.py:289
  119.5 1.9 %collective-permute-start.2 = (f32[32,512]{1,0:T(8,128)S(1)}, f32[32,512]{1,0:T(8,128)S(1)}, u32[]{:S(2)}, u32[]{:S(2)}) collective-permute-start(f32[32,512]{1,0:T(8,128)S(1)} %get-tuple-element.12), channel_id=1, source_target_pairs={{0,448},{64,384},{128,320},{192,256},{256,192},{320,128},{384,64},... | collective-permute-start | bytes 196616 | tf_op jit(solution)/shard_map/ppermute | solution.py:361
  121.4 6.8 %collective-permute-done.2 = f32[32,512]{1,0:T(8,128)S(1)} collective-permute-done((f32[32,512]{1,0:T(8,128)S(1)}, f32[32,512]{1,0:T(8,128)S(1)}, u32[]{:S(2)}, u32[]{:S(2)}) %collective-permute-start.2) | collective-permute-done | bytes 65568 | tf_op jit(solution)/shard_map/ppermute | solution.py:361
  128.3 0.7 maximum_select_fusion
  (6 shorter events, 0.1 us)
Async XLA Ops:
  0.0 1.4 %copy-start = (bf16[3,1,512,512]{3,2,1,0:T(8,128)(2,1)S(1)}, bf16[3,1,512,512]{3,2,1,0:T(8,128)(2,1)}, u32[]{:S(2)}) copy-start(bf16[3,1,512,512]{3,2,1,0:T(8,128)(2,1)} %param.6) | copy-start | bytes 4718596
  1.4 6.5 %copy-start.1 = (f32[1,2,32,512]{3,2,1,0:T(8,128)S(1)}, f32[1,2,32,512]{3,2,1,0:T(8,128)}, u32[]{:S(2)}) copy-start(f32[1,2,32,512]{3,2,1,0:T(8,128)} %param.7) | copy-start | bytes 393220
  1.4 6.5 %copy-start.2 = (f32[1,2,32,512]{3,2,1,0:T(8,128)S(1)}, f32[1,2,32,512]{3,2,1,0:T(8,128)}, u32[]{:S(2)}) copy-start(f32[1,2,32,512]{3,2,1,0:T(8,128)} %param.8) | copy-start | bytes 393220
  3.4 4.6 %collective-permute-start = (f32[256,8,128]{2,1,0:T(8,128)S(1)}, f32[256,8,128]{2,1,0:T(8,128)S(1)}, u32[]{:S(2)}, u32[]{:S(2)}) collective-permute-start(f32[256,8,128]{2,1,0:T(8,128)S(1)} %get-tuple-element.8), channel_id=1, source_target_pairs={{0,32},{32,0},{1,33},{33,1},{2,34},{34,2},{3,35},{35,3},{4,36},{36... | collective-permute-start | bytes 3145736 | tf_op jit(solution)/shard_map/ppermute | solution.py:321
  9.2 21.6 %copy-start.4 = (s32[32]{0:T(128)S(1)}, s32[32]{0:T(128)}, u32[]{:S(2)}) copy-start(s32[32]{0:T(128)} %param.11) | copy-start | bytes 388
  9.2 22.0 %copy-start.3 = (s32[32,2]{0,1:T(2,128)S(1)}, s32[32,2]{0,1:T(2,128)}, u32[]{:S(2)}) copy-start(s32[32,2]{0,1:T(2,128)} %param.9) | copy-start | bytes 772
  9.2 58.1 %all-to-all-start = ((f32[256,1,1280]{2,1,0:T(1,128)}), f32[256,1,1280]{2,1,0:T(1,128)S(1)}, u32[]{:S(2)}, u32[]{:S(2)}) async-start(f32[256,1,1280]{2,1,0:T(1,128)} %bitcast.11), calls=%async_computation | async-start | bytes 2621440 | tf_op jit(solution)/shard_map/all_to_all | solution.py:324
  68.1 41.1 %copy-start.5 = (s32[64]{0:T(128)S(1)}, s32[64]{0:T(128)}, u32[]{:S(2)}) copy-start(s32[64]{0:T(128)} %param.10) | copy-start | bytes 772
  106.0 4.5 %collective-permute-start.1 = (f32[128,16,128]{2,1,0:T(8,128)S(1)}, f32[128,16,128]{2,1,0:T(8,128)S(1)}, u32[]{:S(2)}, u32[]{:S(2)}) collective-permute-start(f32[128,16,128]{2,1,0:T(8,128)S(1)} %all_to_all.10), channel_id=1, source_target_pairs={{0,32},{32,0},{1,33},{33,1},{2,34},{34,2},{3,35},{35,3},{4,36},{36... | collective-permute-start | bytes 3145736 | tf_op jit(solution)/shard_map/ppermute | solution.py:350
  119.5 8.8 %collective-permute-start.2 = (f32[32,512]{1,0:T(8,128)S(1)}, f32[32,512]{1,0:T(8,128)S(1)}, u32[]{:S(2)}, u32[]{:S(2)}) collective-permute-start(f32[32,512]{1,0:T(8,128)S(1)} %get-tuple-element.12), channel_id=1, source_target_pairs={{0,448},{64,384},{128,320},{192,256},{256,192},{320,128},{384,64},... | collective-permute-start | bytes 196616 | tf_op jit(solution)/shard_map/ppermute | solution.py:361

commit v13 on v11

--- a/solution.py
+++ b/solution.py
@@ -8,12 +8,14 @@
 HISTORY = 0.5
 DAMPING = 0.001
 WORKER = ("x", "z")
-PLANE = ("yh", "yl", "x", "z")
-LINE = ("yl", "x", "z")
+PLANE = ("x", "yh", "yl", "z")
+LINE = ("x", "yl", "z")
 SWAP = [(0, 1), (1, 0)]
 LANES = 128
 TILE = 8
 EXTRA = 2
+DEPTH = 8
+LINES = 4
 SMEM = pl.BlockSpec(memory_space=pltpu.SMEM)
 VMEM = pl.BlockSpec(memory_space=pltpu.VMEM)
 PARAMS = pltpu.CompilerParams(vmem_limit_bytes=8 * 1024 * 1024)
@@ -78,12 +80,19 @@
     )(core, gradients)
 
 
+def message_place(number, chunks):
+    columns = 4
+    chunk, piece = divmod(number, columns * DEPTH)
+    return (piece % columns * chunks + chunk) * DEPTH + piece // columns
+
+
 def message_kernel(y_ref, kept_ref, got_ref, prev_ref, warm_ref, out_ref):
     _, rows, width = warm_ref.shape
     columns = tile_columns(width)
     size = TILE + EXTRA
     for number in range(kept_ref.shape[0]):
-        out_ref[pl.ds(size * number, TILE), :] = kept_ref[number] + got_ref[number]
+        first = size * message_place(number, TILE)
+        out_ref[pl.ds(first, TILE), :] = kept_ref[number] + got_ref[number]
     count = kept_ref.shape[0] // 2
     shares = rows // TILE * len(columns)
     for kind in range(2):
@@ -91,14 +100,15 @@
             group, t = divmod(part, len(columns))
             number = count * kind + y_ref[0] * shares + part
             value = HISTORY * prev_ref[kind, pl.ds(TILE * group, TILE), columns[t]]
-            out_ref[pl.ds(size * number, TILE), :] = kept_ref[number] + got_ref[number] + value
+            line = DEPTH * (2 * LINES * t + LINES * kind) + LINES * y_ref[0] + group
+            out_ref[pl.ds(size * line, TILE), :] = kept_ref[number] + got_ref[number] + value
     for kind in range(2):
         for slot in range(EXTRA):
             for t, lanes in enumerate(columns):
                 for first in range(0, rows, TILE):
-                    number = (kind * rows + first) * len(columns) + t
+                    line = DEPTH * (2 * LINES * t + LINES * kind + first // TILE)
                     out_ref[
-                        pl.ds(size * number + TILE + slot, TILE, stride=size * len(columns)), :
+                        pl.ds(size * line + TILE + slot, TILE, stride=size), :
                     ] = warm_ref[slot, pl.ds(first, TILE), lanes]
 
 
@@ -112,27 +122,27 @@
     )(y, kept, got, prev, warm)
 
 
-def deliver_kernel(kind_ref, block_ref, owner_ref, slot_ref, in_ref, out_ref, dense_ref, sum_ref, warm_ref):
+def deliver_kernel(kind_ref, block_ref, owner_ref, slot_ref, in_ref, out_ref, sum_ref, warm_ref):
     kind = kind_ref[0]
     workers = block_ref.shape[0]
     size = TILE + EXTRA
-    stride = workers * size
-    chunks = in_ref.shape[0] // stride
-    for first in range(0, stride, TILE):
-        total = in_ref[pl.ds(first, TILE), :]
+    chunks = in_ref.shape[0] // (workers * size)
+    stride = DEPTH * size
+    for worker in range(workers):
+        base = size * (worker // DEPTH * chunks * DEPTH + worker % DEPTH)
+        total = in_ref[pl.ds(base, TILE), :]
         for chunk in range(1, chunks):
-            total = total + in_ref[pl.ds(first + stride * chunk, TILE), :]
-        dense_ref[pl.ds(first, TILE), :] = total
-    for worker in range(workers):
-        sum_ref[worker] = dense_ref[pl.ds(size * worker, TILE), :]
+            total = total + in_ref[pl.ds(base + stride * chunk, TILE), :]
+        sum_ref[worker] = total
         for slot in range(EXTRA):
-            first = size * worker + TILE + slot
+            first = base + TILE + slot
             warm_ref[EXTRA * worker + slot] = in_ref[pl.ds(first, chunks, stride=stride), :]
     for reader in range(workers):
         place = 2 * reader + kind
         sums = sum_ref[block_ref[reader]]
         warm = warm_ref[EXTRA * owner_ref[place] + slot_ref[place]]
-        for number in range(reader, out_ref.shape[0], workers):
+        for line in range(LINES):
+            number = (reader // DEPTH * LINES + line) * DEPTH + reader % DEPTH
             out_ref[number, pl.ds(0, TILE), :] = sums
             out_ref[number, pl.ds(TILE, TILE), :] = warm
 
@@ -146,7 +156,6 @@
         in_specs=[SMEM] * 4 + [VMEM],
         out_specs=VMEM,
         scratch_shapes=[
-            pltpu.VMEM((workers * (TILE + EXTRA), LANES), jnp.float32),
             pltpu.VMEM((workers, TILE, LANES), jnp.float32),
             pltpu.VMEM((workers * EXTRA, TILE, LANES), jnp.float32),
         ],
@@ -209,12 +218,12 @@
                     rows = pl.ds(share * chunk + half * part + TILE * group, TILE)
                     for t, lanes in enumerate(columns):
                         number = (chunk * groups + group) * len(columns) + t
-                        value = in_ref[pl.ds(2 * TILE * number, TILE), :]
+                        value = in_ref[pl.ds(2 * TILE * message_place(number, LINES), TILE), :]
                         stat_ref[rows, lanes] = value
                         total = total + value * value
-                        first = 2 * TILE * (TILE * group * len(columns) + t) + TILE + chunk
+                        first = 2 * TILE * DEPTH * (LINES * t + group) + TILE + chunk
                         work_ref[rows, lanes] = in_ref[
-                            pl.ds(first, TILE, stride=2 * TILE * len(columns)), :
+                            pl.ds(first, TILE, stride=2 * TILE), :
                         ]
         total_ref[...] = total
 

time: 127 us -> 127 us (level)
  waiting for transfers between devices: 42.3 us -> 39.4 us
  starting transfers between devices: 32 us -> 34.7 us
    ppermute x1, starting transfers between devices: 1.92 us -> 4.8 us  [local(): root_got = lax.ppermute(root_rows[half:], ('yh', 'yl'), pairs)]
    ppermute x1, waiting for transfers between devices: 4.29 us -> 2.08 us  [local(): root_got = lax.ppermute(root_rows[half:], ('yh', 'yl'), pairs)]
where the time goes in v13:
time: 127 us; the launch traced here: 126 us
  waiting for transfers between devices  39.4 us (31%)
  blocking collectives  36.2 us (29%)
  starting transfers between devices  34.7 us (27%)
  Pallas kernels  10.8 us (9%)
  local copies, waits for them, and re-layouts  2.2 us (2%)
  other arithmetic  1.65 us (1%)
    all_to_all x1, blocking collectives, local(): own = lax.all_to_all(tiles, LINE, 0, 0, tiled=True)  36.2 us
    all_to_all x1, waiting for transfers between devices, local(): lax.all_to_all(messages.reshape(peers, 1, -1), PLANE, 0, 0, tiled=True)  34.8 us
    all_to_all x1, starting transfers between devices, local(): lax.all_to_all(messages.reshape(peers, 1, -1), PLANE, 0, 0, tiled=True)  17.1 us
    ppermute x1, starting transfers between devices, local(): got = lax.ppermute(sent, 'core', SWAP)  8.79 us
    pallas_call x1, Pallas kernels, newton(): pl.pallas_call(newton_kernel, out_shape=shape_of(width // TILE, width), i...  6.91 us
    ppermute x1, starting transfers between devices, local(): root_got = lax.ppermute(root_rows[half:], ('yh', 'yl'), pairs)  4.8 us
    ppermute x1, starting transfers between devices, local(): other = lax.ppermute(own, 'core', SWAP)  3.98 us
  transfers between devices with their start and end apart: 4, of which 4 were waited for; matrix products, arithmetic and copies ran while one was open for 1% of the time, Pallas kernels for 0%

profile of v13, /device:TPU:1, one launch (start us, length us, event | category | flops | bytes accessed | tf_op | source)
XLA Modules:
  0.0 125.7 jit_solution(10384189611648280853)
XLA Ops:
  0.0 0.0 copy-start
  0.0 1.4 %copy-done = bf16[3,1,512,512]{3,2,1,0:T(8,128)(2,1)S(1)} copy-done((bf16[3,1,512,512]{3,2,1,0:T(8,128)(2,1)S(1)}, bf16[3,1,512,512]{3,2,1,0:T(8,128)(2,1)}, u32[]{:S(2)}) %copy-start) | copy-done | bytes 1572888
  1.4 0.0 copy-start.1
  1.4 0.0 copy-start.2
  1.4 1.9 %shard_map.64 = (f32[256,8,128]{2,1,0:T(8,128)S(1)}, f32[256,8,128]{2,1,0:T(8,128)S(1)}) custom-call(s32[1]{0:T(128)} %bitcast.refs_0_.core_ref, bf16[3,512,512]{2,1,0:T(8,128)(2,1)S(1)} %bitcast.17), custom_call_target="tpu_custom_call" | custom-call | tf_op jit(solution)/shard_map/pallas_call | solution.py:73
  3.4 8.8 %collective-permute-start = (f32[256,8,128]{2,1,0:T(8,128)S(1)}, f32[256,8,128]{2,1,0:T(8,128)S(1)}, u32[]{:S(2)}, u32[]{:S(2)}) collective-permute-start(f32[256,8,128]{2,1,0:T(8,128)S(1)} %get-tuple-element.8), channel_id=1, source_target_pairs={{0,32},{32,0},{1,33},{33,1},{2,34},{34,2},{3,35},{35,3},{4,36},{36... | collective-permute-start | bytes 3145736 | tf_op jit(solution)/shard_map/ppermute | solution.py:330
  12.2 2.3 %collective-permute-done.got_ref = f32[256,8,128]{2,1,0:T(8,128)S(1)} collective-permute-done((f32[256,8,128]{2,1,0:T(8,128)S(1)}, f32[256,8,128]{2,1,0:T(8,128)S(1)}, u32[]{:S(2)}, u32[]{:S(2)}) %collective-permute-start) | collective-permute-done | bytes 1048608 | tf_op jit(solution)/shard_map/ppermute | solution.py:330
  14.4 0.0 copy-done.1
  14.4 0.0 copy-done.2
  14.4 1.2 shard_map.65
  15.6 0.0 copy-start.4
  15.6 0.0 copy-start.3
  15.7 17.1 %all-to-all-start = ((f32[256,1,1280]{2,1,0:T(1,128)}), f32[256,1,1280]{2,1,0:T(1,128)S(1)}, u32[]{:S(2)}, u32[]{:S(2)}) async-start(f32[256,1,1280]{2,1,0:T(1,128)} %bitcast.8), calls=%async_computation | async-start | bytes 2621440 | tf_op jit(solution)/shard_map/all_to_all | solution.py:333
  32.8 0.0 copy-done.4
  32.8 0.1 select_reduce_fusion.block_ref
  32.9 0.1 iota_add_fusion
  33.0 0.1 add.39
  33.1 0.0 copy-done.3
  33.1 0.1 fusion.1
  33.2 34.8 %all-to-all-done = f32[256,1,1280]{2,1,0:T(1,128)S(1)} async-done(((f32[256,1,1280]{2,1,0:T(1,128)}), f32[256,1,1280]{2,1,0:T(1,128)S(1)}, u32[]{:S(2)}, u32[]{:S(2)}) %all-to-all-start) | async-done | bytes 1310752 | tf_op jit(solution)/shard_map/all_to_all | solution.py:333
  68.0 0.7 shard_map.66
  68.8 0.0 copy-start.5
  68.8 36.2 %all_to_all.10 = f32[128,16,128]{2,1,0:T(8,128)S(1)} all-to-all(f32[128,16,128]{2,1,0:T(8,128)S(1)} %shard_map.66), channel_id=1, replica_groups=mesh['yh'=2,'yl'=4,'core'=2,'x'=4,'z'=8] {'x','yl','z'}, dimensions={0} | all-to-all | bytes 2097152 | tf_op jit(solution)/shard_map/all_to_all | solution.py:347
  105.0 4.0 %collective-permute-start.1 = (f32[128,16,128]{2,1,0:T(8,128)S(1)}, f32[128,16,128]{2,1,0:T(8,128)S(1)}, u32[]{:S(2)}, u32[]{:S(2)}) collective-permute-start(f32[128,16,128]{2,1,0:T(8,128)S(1)} %all_to_all.10), channel_id=1, source_target_pairs={{0,32},{32,0},{1,33},{33,1},{2,34},{34,2},{3,35},{35,3},{4,36},{36... | collective-permute-start | bytes 3145736 | tf_op jit(solution)/shard_map/ppermute | solution.py:348
  109.0 0.7 dynamic_slice.3
  110.3 0.0 copy-done.5
  110.3 0.7 fusion.2
  111.0 0.3 collective-permute-done.1
  111.2 6.9 %shard_map.67 = f32[64,512]{1,0:T(8,128)S(1)} custom-call(s32[1]{0:T(128)} %bitcast.refs_0_.core_ref, s32[1]{0:T(128)} %bitcast.1.y_ref, s32[1]{0:T(128)} %bitcast.3.count_ref, f32[2048,128]{1,0:T(8,128)S(1)} %bitcast.16, f32[2048,128]{1,0:T(8,128)S(1)} %bitcast.18), custom_call_target="tpu_custom_call" | custom-call | tf_op jit(solution)/shard_map/pallas_call | solution.py:298
  118.2 4.8 %collective-permute-start.2 = (f32[32,512]{1,0:T(8,128)S(1)}, f32[32,512]{1,0:T(8,128)S(1)}, u32[]{:S(2)}, u32[]{:S(2)}) collective-permute-start(f32[32,512]{1,0:T(8,128)S(1)} %get-tuple-element.12), channel_id=1, source_target_pairs={{0,448},{64,384},{128,320},{192,256},{256,192},{320,128},{384,64},... | collective-permute-start | bytes 196616 | tf_op jit(solution)/shard_map/ppermute | solution.py:359
  123.0 2.1 %collective-permute-done.2 = f32[32,512]{1,0:T(8,128)S(1)} collective-permute-done((f32[32,512]{1,0:T(8,128)S(1)}, f32[32,512]{1,0:T(8,128)S(1)}, u32[]{:S(2)}, u32[]{:S(2)}) %collective-permute-start.2) | collective-permute-done | bytes 65568 | tf_op jit(solution)/shard_map/ppermute | solution.py:359
  125.0 0.7 maximum_select_fusion
  (2 shorter events, 0.0 us)
Async XLA Ops:
  0.0 1.4 %copy-start = (bf16[3,1,512,512]{3,2,1,0:T(8,128)(2,1)S(1)}, bf16[3,1,512,512]{3,2,1,0:T(8,128)(2,1)}, u32[]{:S(2)}) copy-start(bf16[3,1,512,512]{3,2,1,0:T(8,128)(2,1)} %param.6) | copy-start | bytes 4718596
  1.4 13.0 %copy-start.1 = (f32[1,2,32,512]{3,2,1,0:T(8,128)S(1)}, f32[1,2,32,512]{3,2,1,0:T(8,128)}, u32[]{:S(2)}) copy-start(f32[1,2,32,512]{3,2,1,0:T(8,128)} %param.7) | copy-start | bytes 393220
  1.4 13.0 %copy-start.2 = (f32[1,2,32,512]{3,2,1,0:T(8,128)S(1)}, f32[1,2,32,512]{3,2,1,0:T(8,128)}, u32[]{:S(2)}) copy-start(f32[1,2,32,512]{3,2,1,0:T(8,128)} %param.8) | copy-start | bytes 393220
  3.4 11.1 %collective-permute-start = (f32[256,8,128]{2,1,0:T(8,128)S(1)}, f32[256,8,128]{2,1,0:T(8,128)S(1)}, u32[]{:S(2)}, u32[]{:S(2)}) collective-permute-start(f32[256,8,128]{2,1,0:T(8,128)S(1)} %get-tuple-element.8), channel_id=1, source_target_pairs={{0,32},{32,0},{1,33},{33,1},{2,34},{34,2},{3,35},{35,3},{4,36},{36... | collective-permute-start | bytes 3145736 | tf_op jit(solution)/shard_map/ppermute | solution.py:330
  15.6 17.1 %copy-start.4 = (s32[32]{0:T(128)S(1)}, s32[32]{0:T(128)}, u32[]{:S(2)}) copy-start(s32[32]{0:T(128)} %param.11) | copy-start | bytes 388
  15.6 17.5 %copy-start.3 = (s32[32,2]{0,1:T(2,128)S(1)}, s32[32,2]{0,1:T(2,128)}, u32[]{:S(2)}) copy-start(s32[32,2]{0,1:T(2,128)} %param.9) | copy-start | bytes 772
  15.7 52.4 %all-to-all-start = ((f32[256,1,1280]{2,1,0:T(1,128)}), f32[256,1,1280]{2,1,0:T(1,128)S(1)}, u32[]{:S(2)}, u32[]{:S(2)}) async-start(f32[256,1,1280]{2,1,0:T(1,128)} %bitcast.8), calls=%async_computation | async-start | bytes 2621440 | tf_op jit(solution)/shard_map/all_to_all | solution.py:333
  68.8 41.5 %copy-start.5 = (s32[64]{0:T(128)S(1)}, s32[64]{0:T(128)}, u32[]{:S(2)}) copy-start(s32[64]{0:T(128)} %param.10) | copy-start | bytes 772
  105.0 6.3 %collective-permute-start.1 = (f32[128,16,128]{2,1,0:T(8,128)S(1)}, f32[128,16,128]{2,1,0:T(8,128)S(1)}, u32[]{:S(2)}, u32[]{:S(2)}) collective-permute-start(f32[128,16,128]{2,1,0:T(8,128)S(1)} %all_to_all.10), channel_id=1, source_target_pairs={{0,32},{32,0},{1,33},{33,1},{2,34},{34,2},{3,35},{35,3},{4,36},{36... | collective-permute-start | bytes 3145736 | tf_op jit(solution)/shard_map/ppermute | solution.py:348
  118.2 6.9 %collective-permute-start.2 = (f32[32,512]{1,0:T(8,128)S(1)}, f32[32,512]{1,0:T(8,128)S(1)}, u32[]{:S(2)}, u32[]{:S(2)}) collective-permute-start(f32[32,512]{1,0:T(8,128)S(1)} %get-tuple-element.12), channel_id=1, source_target_pairs={{0,448},{64,384},{128,320},{192,256},{256,192},{320,128},{384,64},... | collective-permute-start | bytes 196616 | tf_op jit(solution)/shard_map/ppermute | solution.py:359

commit v14 on v13

--- a/solution.py
+++ b/solution.py
@@ -36,7 +36,7 @@
     columns = tile_columns(width)
     chunks = width // (2 * half)
     count = chunks * groups * len(columns)
-    step = 2 * LANES
+    step = 4 * LANES
     for kind in range(2):
         for first in range(0, width, step):
             part = pl.ds(first, step)
@@ -208,7 +208,7 @@
     share = width // chunks
     half = share // 2
     groups = half // TILE
-    step = 2 * LANES
+    step = 4 * LANES
 
     def assemble(*halves):
         total = jnp.zeros((TILE, LANES), jnp.float32)

time: 127 us -> 128 us (level)
  starting transfers between devices: 34.7 us -> 31.8 us
  waiting for transfers between devices: 39.4 us -> 41.6 us
  Pallas kernels: 10.8 us -> 12.5 us
    ppermute x1, starting transfers between devices: 4.8 us -> 1.92 us  [local(): root_got = lax.ppermute(root_rows[half:], ('yh', 'yl'), pairs)]
    ppermute x1, waiting for transfers between devices: 2.08 us -> 4.29 us  [local(): root_got = lax.ppermute(root_rows[half:], ('yh', 'yl'), pairs)]
    pallas_call x1, Pallas kernels: 6.91 us -> 8.63 us  [newton(): pl.pallas_call(newton_kernel, out_shape=shape_of(width // TILE, width), i...]
where the time goes in v14:
time: 128 us; the launch traced here: 127 us
  waiting for transfers between devices  41.6 us (32%)
  blocking collectives  36.2 us (28%)
  starting transfers between devices  31.8 us (25%)
  Pallas kernels  12.5 us (10%)
  local copies, waits for them, and re-layouts  2.2 us (2%)
  other arithmetic  1.65 us (1%)
    all_to_all x1, blocking collectives, local(): own = lax.all_to_all(tiles, LINE, 0, 0, tiled=True)  36.2 us
    all_to_all x1, waiting for transfers between devices, local(): lax.all_to_all(messages.reshape(peers, 1, -1), PLANE, 0, 0, tiled=True)  34.8 us
    all_to_all x1, starting transfers between devices, local(): lax.all_to_all(messages.reshape(peers, 1, -1), PLANE, 0, 0, tiled=True)  17.1 us
    ppermute x1, starting transfers between devices, local(): got = lax.ppermute(sent, 'core', SWAP)  8.8 us
    pallas_call x1, Pallas kernels, newton(): pl.pallas_call(newton_kernel, out_shape=shape_of(width // TILE, width), i...  8.63 us
    ppermute x1, waiting for transfers between devices, local(): root_got = lax.ppermute(root_rows[half:], ('yh', 'yl'), pairs)  4.29 us
    ppermute x1, starting transfers between devices, local(): other = lax.ppermute(own, 'core', SWAP)  3.98 us
  transfers between devices with their start and end apart: 4, of which 4 were waited for; matrix products, arithmetic and copies ran while one was open for 1% of the time, Pallas kernels for 0%

profile of v14, /device:TPU:1, one launch (start us, length us, event | category | flops | bytes accessed | tf_op | source)
XLA Modules:
  0.0 126.8 jit_solution(4773211760638519008)
XLA Ops:
  0.0 0.0 copy-start
  0.0 1.4 %copy-done = bf16[3,1,512,512]{3,2,1,0:T(8,128)(2,1)S(1)} copy-done((bf16[3,1,512,512]{3,2,1,0:T(8,128)(2,1)S(1)}, bf16[3,1,512,512]{3,2,1,0:T(8,128)(2,1)}, u32[]{:S(2)}) %copy-start) | copy-done | bytes 1572888
  1.4 0.0 copy-start.1
  1.4 0.0 copy-start.2
  1.4 1.9 %shard_map.64 = (f32[256,8,128]{2,1,0:T(8,128)S(1)}, f32[256,8,128]{2,1,0:T(8,128)S(1)}) custom-call(s32[1]{0:T(128)} %bitcast.refs_0_.core_ref, bf16[3,512,512]{2,1,0:T(8,128)(2,1)S(1)} %bitcast.17), custom_call_target="tpu_custom_call" | custom-call | tf_op jit(solution)/shard_map/pallas_call | solution.py:73
  3.4 8.8 %collective-permute-start = (f32[256,8,128]{2,1,0:T(8,128)S(1)}, f32[256,8,128]{2,1,0:T(8,128)S(1)}, u32[]{:S(2)}, u32[]{:S(2)}) collective-permute-start(f32[256,8,128]{2,1,0:T(8,128)S(1)} %get-tuple-element.8), channel_id=1, source_target_pairs={{0,32},{32,0},{1,33},{33,1},{2,34},{34,2},{3,35},{35,3},{4,36},{36... | collective-permute-start | bytes 3145736 | tf_op jit(solution)/shard_map/ppermute | solution.py:330
  12.2 2.3 %collective-permute-done.got_ref = f32[256,8,128]{2,1,0:T(8,128)S(1)} collective-permute-done((f32[256,8,128]{2,1,0:T(8,128)S(1)}, f32[256,8,128]{2,1,0:T(8,128)S(1)}, u32[]{:S(2)}, u32[]{:S(2)}) %collective-permute-start) | collective-permute-done | bytes 1048608 | tf_op jit(solution)/shard_map/ppermute | solution.py:330
  14.4 0.0 copy-done.1
  14.4 0.0 copy-done.2
  14.4 1.2 shard_map.65
  15.6 0.0 copy-start.4
  15.7 0.0 copy-start.3
  15.7 17.1 %all-to-all-start = ((f32[256,1,1280]{2,1,0:T(1,128)}), f32[256,1,1280]{2,1,0:T(1,128)S(1)}, u32[]{:S(2)}, u32[]{:S(2)}) async-start(f32[256,1,1280]{2,1,0:T(1,128)} %bitcast.8), calls=%async_computation | async-start | bytes 2621440 | tf_op jit(solution)/shard_map/all_to_all | solution.py:333
  32.8 0.0 copy-done.4
  32.8 0.1 select_reduce_fusion.block_ref
  32.9 0.1 iota_add_fusion
  33.0 0.1 add.39
  33.1 0.0 copy-done.3
  33.1 0.1 fusion.1
  33.2 34.8 %all-to-all-done = f32[256,1,1280]{2,1,0:T(1,128)S(1)} async-done(((f32[256,1,1280]{2,1,0:T(1,128)}), f32[256,1,1280]{2,1,0:T(1,128)S(1)}, u32[]{:S(2)}, u32[]{:S(2)}) %all-to-all-start) | async-done | bytes 1310752 | tf_op jit(solution)/shard_map/all_to_all | solution.py:333
  68.0 0.7 shard_map.66
  68.8 0.0 copy-start.5
  68.8 36.2 %all_to_all.10 = f32[128,16,128]{2,1,0:T(8,128)S(1)} all-to-all(f32[128,16,128]{2,1,0:T(8,128)S(1)} %shard_map.66), channel_id=1, replica_groups=mesh['yh'=2,'yl'=4,'core'=2,'x'=4,'z'=8] {'x','yl','z'}, dimensions={0} | all-to-all | bytes 2097152 | tf_op jit(solution)/shard_map/all_to_all | solution.py:347
  105.0 4.0 %collective-permute-start.1 = (f32[128,16,128]{2,1,0:T(8,128)S(1)}, f32[128,16,128]{2,1,0:T(8,128)S(1)}, u32[]{:S(2)}, u32[]{:S(2)}) collective-permute-start(f32[128,16,128]{2,1,0:T(8,128)S(1)} %all_to_all.10), channel_id=1, source_target_pairs={{0,32},{32,0},{1,33},{33,1},{2,34},{34,2},{3,35},{35,3},{4,36},{36... | collective-permute-start | bytes 3145736 | tf_op jit(solution)/shard_map/ppermute | solution.py:348
  109.0 0.7 dynamic_slice.3
  110.3 0.0 copy-done.5
  110.3 0.7 fusion.2
  111.0 0.3 collective-permute-done.1
  111.2 8.6 %shard_map.67 = f32[64,512]{1,0:T(8,128)S(1)} custom-call(s32[1]{0:T(128)} %bitcast.refs_0_.core_ref, s32[1]{0:T(128)} %bitcast.1.y_ref, s32[1]{0:T(128)} %bitcast.3.count_ref, f32[2048,128]{1,0:T(8,128)S(1)} %bitcast.16, f32[2048,128]{1,0:T(8,128)S(1)} %bitcast.18), custom_call_target="tpu_custom_call" | custom-call | tf_op jit(solution)/shard_map/pallas_call | solution.py:298
  119.9 1.9 %collective-permute-start.2 = (f32[32,512]{1,0:T(8,128)S(1)}, f32[32,512]{1,0:T(8,128)S(1)}, u32[]{:S(2)}, u32[]{:S(2)}) collective-permute-start(f32[32,512]{1,0:T(8,128)S(1)} %get-tuple-element.12), channel_id=1, source_target_pairs={{0,448},{64,384},{128,320},{192,256},{256,192},{320,128},{384,64},... | collective-permute-start | bytes 196616 | tf_op jit(solution)/shard_map/ppermute | solution.py:359
  121.8 4.3 %collective-permute-done.2 = f32[32,512]{1,0:T(8,128)S(1)} collective-permute-done((f32[32,512]{1,0:T(8,128)S(1)}, f32[32,512]{1,0:T(8,128)S(1)}, u32[]{:S(2)}, u32[]{:S(2)}) %collective-permute-start.2) | collective-permute-done | bytes 65568 | tf_op jit(solution)/shard_map/ppermute | solution.py:359
  126.1 0.7 maximum_select_fusion
  (2 shorter events, 0.0 us)
Async XLA Ops:
  0.0 1.4 %copy-start = (bf16[3,1,512,512]{3,2,1,0:T(8,128)(2,1)S(1)}, bf16[3,1,512,512]{3,2,1,0:T(8,128)(2,1)}, u32[]{:S(2)}) copy-start(bf16[3,1,512,512]{3,2,1,0:T(8,128)(2,1)} %param.6) | copy-start | bytes 4718596
  1.4 13.0 %copy-start.1 = (f32[1,2,32,512]{3,2,1,0:T(8,128)S(1)}, f32[1,2,32,512]{3,2,1,0:T(8,128)}, u32[]{:S(2)}) copy-start(f32[1,2,32,512]{3,2,1,0:T(8,128)} %param.7) | copy-start | bytes 393220
  1.4 13.0 %copy-start.2 = (f32[1,2,32,512]{3,2,1,0:T(8,128)S(1)}, f32[1,2,32,512]{3,2,1,0:T(8,128)}, u32[]{:S(2)}) copy-start(f32[1,2,32,512]{3,2,1,0:T(8,128)} %param.8) | copy-start | bytes 393220
  3.4 11.1 %collective-permute-start = (f32[256,8,128]{2,1,0:T(8,128)S(1)}, f32[256,8,128]{2,1,0:T(8,128)S(1)}, u32[]{:S(2)}, u32[]{:S(2)}) collective-permute-start(f32[256,8,128]{2,1,0:T(8,128)S(1)} %get-tuple-element.8), channel_id=1, source_target_pairs={{0,32},{32,0},{1,33},{33,1},{2,34},{34,2},{3,35},{35,3},{4,36},{36... | collective-permute-start | bytes 3145736 | tf_op jit(solution)/shard_map/ppermute | solution.py:330
  15.6 17.1 %copy-start.4 = (s32[32]{0:T(128)S(1)}, s32[32]{0:T(128)}, u32[]{:S(2)}) copy-start(s32[32]{0:T(128)} %param.11) | copy-start | bytes 388
  15.7 17.5 %copy-start.3 = (s32[32,2]{0,1:T(2,128)S(1)}, s32[32,2]{0,1:T(2,128)}, u32[]{:S(2)}) copy-start(s32[32,2]{0,1:T(2,128)} %param.9) | copy-start | bytes 772
  15.7 52.4 %all-to-all-start = ((f32[256,1,1280]{2,1,0:T(1,128)}), f32[256,1,1280]{2,1,0:T(1,128)S(1)}, u32[]{:S(2)}, u32[]{:S(2)}) async-start(f32[256,1,1280]{2,1,0:T(1,128)} %bitcast.8), calls=%async_computation | async-start | bytes 2621440 | tf_op jit(solution)/shard_map/all_to_all | solution.py:333
  68.8 41.5 %copy-start.5 = (s32[64]{0:T(128)S(1)}, s32[64]{0:T(128)}, u32[]{:S(2)}) copy-start(s32[64]{0:T(128)} %param.10) | copy-start | bytes 772
  105.0 6.3 %collective-permute-start.1 = (f32[128,16,128]{2,1,0:T(8,128)S(1)}, f32[128,16,128]{2,1,0:T(8,128)S(1)}, u32[]{:S(2)}, u32[]{:S(2)}) collective-permute-start(f32[128,16,128]{2,1,0:T(8,128)S(1)} %all_to_all.10), channel_id=1, source_target_pairs={{0,32},{32,0},{1,33},{33,1},{2,34},{34,2},{3,35},{35,3},{4,36},{36... | collective-permute-start | bytes 3145736 | tf_op jit(solution)/shard_map/ppermute | solution.py:348
  119.9 6.2 %collective-permute-start.2 = (f32[32,512]{1,0:T(8,128)S(1)}, f32[32,512]{1,0:T(8,128)S(1)}, u32[]{:S(2)}, u32[]{:S(2)}) collective-permute-start(f32[32,512]{1,0:T(8,128)S(1)} %get-tuple-element.12), channel_id=1, source_target_pairs={{0,448},{64,384},{128,320},{192,256},{256,192},{320,128},{384,64},... | collective-permute-start | bytes 196616 | tf_op jit(solution)/shard_map/ppermute | solution.py:359
